TPU v7x, 32 devices: a whole 2x2x4 slice. The times are simulated.
32 devices in a mesh: rows: 8 (over z, x), proto: 4 (over y, core).
Axes of the slice: x: 2, y: 2, z: 4, core: 2. Of those that a mesh axis runs over, the one named last changes fastest.
Arguments:
- teacher_features: bfloat16 [256, 256], P('rows'), may hold values from -6 to 6
- student_features: bfloat16 [1280, 256], P('rows'), may hold values from -8 to 8
- prototypes: bfloat16 [256, 131072], P(None, 'proto'), may hold values from -1 to 1
- pairing: int32 [1280], P('rows'), may hold values from 0 to 255
Outputs:
- proto_grad: float32 [256, 131072], P('rows', 'proto')
- student_grad: float32 [1280, 256], P('rows', 'proto')
- loss: float32 [1280], P('rows')
All inputs are finite; a program needn't handle non-finite values.
Results may differ from a plain program's by a relative error of at most 0.0023.
Values may be sent and summed in bfloat16 or wider, within the bound.
No kernel may reach another device: no remote copies, remote signals or barrier semaphores. Data moves between devices by JAX's collectives and lax.ppermute only.
A program may use at most 192 MiB of HBM per device.

v0:
```python
import jax
import jax.numpy as jnp
from jax import lax
from jax.sharding import PartitionSpec as P

ITERS = 3


teacher_temp = 0.07
student_temp = 0.1
eps = 1e-06


def body(teacher_features, student_features, prototypes, pairing):
    teach_rows = teacher_features.shape[0] * lax.axis_size("rows")
    local_k = prototypes.shape[1]
    total_k = local_k * lax.axis_size("proto")
    vf = prototypes.astype(jnp.float32)
    vnorm = jnp.sqrt(jnp.sum(vf * vf, axis=0) + eps)
    unit = vf / vnorm[None, :]
    unit_b = unit.astype(jnp.bfloat16)
    tf = teacher_features.astype(jnp.float32)
    teach_unit = (tf / jnp.sqrt(jnp.sum(tf * tf, axis=1, keepdims=True) + eps)).astype(jnp.bfloat16)
    teach_all = lax.all_gather(teach_unit, "rows", axis=0, tiled=True)
    energy = jnp.exp(jnp.dot(teach_unit, unit_b, preferred_element_type=jnp.float32) / teacher_temp)
    row_scale = jnp.ones((teacher_features.shape[0],), jnp.float32)
    col_scale = jnp.ones((local_k,), jnp.float32)
    for step in range(ITERS):
        col_sum = col_scale * lax.psum(jnp.sum(energy * row_scale[:, None], axis=0), "rows")
        col_scale = col_scale / (col_sum * total_k)
        row_sum = row_scale * lax.psum(jnp.sum(energy * col_scale[None, :], axis=1), "proto")
        row_scale = row_scale / (row_sum * teach_rows)
    scales_all = lax.all_gather(row_scale, "rows", axis=0, tiled=True)
    chosen = jnp.take(teach_all, pairing, axis=0)
    picked_scale = jnp.take(scales_all, pairing, axis=0)
    energy_sel = jnp.exp(jnp.dot(chosen, unit_b, preferred_element_type=jnp.float32) / teacher_temp)
    target = (energy_sel * col_scale[None, :] * picked_scale[:, None] * teach_rows).astype(
        jnp.bfloat16
    )
    sf = student_features.astype(jnp.float32)
    snorm = jnp.sqrt(jnp.sum(sf * sf, axis=1, keepdims=True) + eps)
    stud_unit = sf / snorm
    stud_unit_b = stud_unit.astype(jnp.bfloat16)
    target_f = target.astype(jnp.float32)
    logits = jnp.dot(stud_unit_b, unit_b, preferred_element_type=jnp.float32) / student_temp
    expo = jnp.exp(logits)
    denom, cross, mass = lax.psum(
        (jnp.sum(expo, axis=1), jnp.sum(target_f * logits, axis=1), jnp.sum(target_f, axis=1)),
        "proto",
    )
    loss = jnp.log(denom) * mass - cross
    grad_scale = total_k / 64.0
    dlogit = (
        grad_scale / student_temp * (mass[:, None] * (expo / denom[:, None]) - target_f)
    ).astype(jnp.bfloat16)
    head = lax.dot_general(
        stud_unit_b, dlogit, (((0,), (0,)), ((), ())), preferred_element_type=jnp.float32
    )
    proj = jnp.sum(unit * head, axis=0)
    term = (head - unit * proj[None, :]) / vnorm[None, :]
    proto_grad = lax.psum_scatter(term, "rows", scatter_dimension=0, tiled=True)
    back = lax.dot_general(
        dlogit, unit_b, (((1,), (1,)), ((), ())), preferred_element_type=jnp.float32
    )
    full = lax.psum(back, "proto")
    along = jnp.sum(stud_unit * full, axis=1, keepdims=True)
    grad_all = (full - stud_unit * along) / snorm
    width = full.shape[1] // lax.axis_size("proto")
    student_grad = lax.dynamic_slice_in_dim(grad_all, lax.axis_index("proto") * width, width, 1)
    return (proto_grad, student_grad, loss)


def solution(mesh):
    return jax.shard_map(
        body,
        mesh=mesh,
        in_specs=(P("rows", None), P("rows", None), P(None, "proto"), P("rows")),
        out_specs=(P("rows", "proto"), P("rows", "proto"), P("rows")),
        check_vma=False,
    )
```

profile of v0, /device:TPU:0, one launch (start us, length us, event | category | flops | bytes accessed | tf_op | source)
XLA Modules:
  0.0 964.1 jit_solution(9637924233998533530)
XLA Ops:
  7.2 0.0 all-reduce.7.cloned.1.call-start
  7.2 7.1 fusion.7
  14.3 0.0 copy-start.3
  14.4 0.0 copy-start.2
  14.4 9.9 %fusion.8 = bf16[256,32768]{1,0:T(8,128)(2,1)S(1)} fusion(f32[32768]{0:T(1024)S(1)} %add_sqrt_fusion, bf16[256,32768]{1,0:T(8,128)(2,1)} %param.6), kind=kLoop, calls=%fused_computation.20 | loop fusion | flops 25165824 | bytes 33685504 | tf_op jit(solution)/shard_map/convert_element_type | solution.py:21
  24.3 0.0 copy-done.3
  24.3 0.0 copy-start
  24.3 0.1 fusion.17
  24.4 0.1 fusion.18
  24.5 5.5 copy-done
  30.0 5.8 fusion.20
  35.8 0.0 all-reduce.7.cloned.1.call-update
  35.8 0.0 all-reduce.9.cloned.1.call-start
  35.9 0.0 copy-done.2
  35.9 0.1 fusion.9
  36.0 0.0 copy-start.4
  36.0 0.0 copy-start.5
  36.0 15.7 %convolution_multiply_fusion = f32[160,32768]{1,0:T(8,128)} fusion(bf16[256,32768]{1,0:T(8,128)(2,1)} %copy-done, bf16[160,256]{1,0:T(8,128)(2,1)S(1)} %copy-done.2, f32[160]{0:T(256)S(1)} %add_sqrt_fusion.1), kind=kOutput, calls=%fused_computation.4 | convolution fusion | flops 2689720320 | bytes 37831296 | tf_op jit(solution)/shard_map/dot_general | solution.py:45
  51.7 56.6 %all-reduce.7.cloned.1.call-done = f32[32768]{0:T(1024)} async-done(((f32[32768]{0:T(1024)}), f32[32768]{0:T(1024)}) %all-reduce.7.cloned.1.call-update) | async-done | bytes 131088 | tf_op jit(solution)/shard_map/psum | solution.py:29
  108.4 0.9 multiply_divide_fusion.1
  109.3 2.6 multiply_reduce_fusion.6
  112.0 5.7 psum.71
  117.6 3.4 multiply_reduce_fusion.5
  121.0 0.0 all-reduce.9.cloned.1.call-update
  121.0 0.0 all-reduce.11.cloned.1.call-start
  121.1 0.0 copy-done.4
  121.1 69.3 %all-reduce.9.cloned.1.call-done = f32[32768]{0:T(1024)} async-done(((f32[32768]{0:T(1024)}), f32[32768]{0:T(1024)}) %all-reduce.9.cloned.1.call-update) | async-done | bytes 131088 | tf_op jit(solution)/shard_map/psum | solution.py:29
  190.4 1.0 broadcast_divide_fusion
  191.4 2.6 multiply_reduce_fusion.4
  194.0 5.7 psum.73
  199.7 3.4 multiply_reduce_fusion.3
  203.1 0.0 all-reduce.11.cloned.1.call-update
  203.1 0.0 all-reduce.13.cloned.1.call-start
  203.2 30.5 %all_gather.6 = bf16[256,256]{1,0:T(8,128)(2,1)S(1)} all-gather(bf16[32,256]{1,0:T(8,128)(2,1)S(1)} %fusion.18), channel_id=1, replica_groups=mesh['rows'=8,'proto'=4] {'rows'}, dimensions={0}, use_global_device_ids=true | all-gather | bytes 147456 | tf_op jit(solution)/shard_map/all_gather | solution.py:24
  233.7 0.0 copy-done.5
  233.7 0.6 dynamic-slice
  235.0 0.9 gather_fusion
  235.9 36.7 %all-reduce.11.cloned.1.call-done = f32[32768]{0:T(1024)} async-done(((f32[32768]{0:T(1024)}), f32[32768]{0:T(1024)}) %all-reduce.11.cloned.1.call-update) | async-done | bytes 131088 | tf_op jit(solution)/shard_map/psum | solution.py:29
  272.6 1.1 multiply_divide_fusion
  273.7 2.6 multiply_reduce_fusion.2
  276.3 5.7 psum.75
  282.0 0.1 divide_dynamic-update-slice_fusion
  282.1 19.9 %all-reduce = f32[256]{0:T(256)S(1)} all-reduce(f32[256]{0:T(256)S(1)} %divide_dynamic-update-slice_fusion), channel_id=1, replica_groups=mesh['rows'=8,'proto'=4] {'rows'}, use_global_device_ids=true, to_apply=%add | all-reduce | flops 256 | bytes 2048
  302.0 1.6 gather_fusion.1
  303.6 20.9 %multiply_reduce_fusion.1 = (f32[160]{0:T(256)S(1)}, f32[160]{0:T(256)S(1)}, f32[160]{0:T(256)S(1)}, f32[160,32768]{1,0:T(8,128)}) fusion(f32[160,32768]{1,0:T(8,128)} %convolution_multiply_fusion, f32[160]{0:T(256)S(1)} %get-tuple-element.15, f32[32768]{0:T(1024)S(1)} %multiply_divide_fusion, bf16[256,32768]{1,0:T(8,128)(2,1)} %copy-done, ...), kind=kOutput, calls=%fused_computation.17 | convolution fusion | flops 2736823552 | bytes 58935968 | tf_op jit(solution)/shard_map/dot_general | solution.py:36
  324.5 5.6 all-reduce.1
  330.1 14.2 %multiply_convert_fusion = bf16[160,32768]{1,0:T(8,128)(2,1)S(1)} fusion(f32[160,32768]{1,0:T(8,128)} %get-tuple-element.23, f32[160,32768]{1,0:T(8,128)} %convolution_multiply_fusion, f32[160]{0:T(256)S(1)} %get-tuple-element.12, f32[160]{0:T(256)S(1)} %get-tuple-element.13), kind=kLoop, calls=%fused_computation.18 | loop fusion | flops 26214400 | bytes 52430080 | tf_op jit(solution)/shard_map/convert_element_type | solution.py:55
  344.3 0.0 copy-start.1
  344.4 3.9 copy-done.1
  348.2 9.9 %fusion.21 = f32[160,256]{1,0:T(8,128)} fusion(bf16[160,32768]{1,0:T(8,128)(2,1)S(1)} %multiply_convert_fusion, bf16[256,32768]{1,0:T(8,128)(2,1)} %copy-done), kind=kOutput, calls=%fused_computation.61 | convolution fusion | flops 2684354560 | bytes 27426816 | tf_op jit(solution)/shard_map/dot_general | solution.py:62
  358.2 22.8 %multiply_reduce_fusion = (f32[32768]{0:T(1024)S(1)}, f32[256,32768]{1,0:T(8,128)}) fusion(f32[32768]{0:T(1024)S(1)} %add_sqrt_fusion, bf16[256,32768]{1,0:T(8,128)(2,1)} %param.6, bf16[160,32768]{1,0:T(8,128)(2,1)} %copy-done.1, f32[160]{0:T(256)S(1)} %add_sqrt_fusion.1, bf16[160,256]{1,0:T(8,128)(2,1)S(1)} %copy-done.2), kind=kOutput, calls=%fused_computation.16 | convolution fusion | flops 2717999104 | bytes 61162112 | tf_op jit(solution)/shard_map/dot_general | solution.py:56
  380.9 0.0 all-reduce.13.cloned.1.call-update
  381.0 0.0 reduce-scatter.2.cloned.1.call-start
  381.0 28.0 %subtract_divide_fusion = f32[256,32768]{1,0:T(8,128)} fusion(f32[256,32768]{1,0:T(8,128)} %get-tuple-element.25, f32[32768]{0:T(1024)S(1)} %get-tuple-element.24, f32[32768]{0:T(1024)S(1)} %add_sqrt_fusion, bf16[256,32768]{1,0:T(8,128)(2,1)} %param.6), kind=kLoop, calls=%fused_computation.15 | loop fusion | flops 41943040 | bytes 84148224 | tf_op jit(solution)/shard_map/div | solution.py:60
  409.0 0.0 reduce-scatter.2.cloned.1.call-update
  409.1 0.6 multiply_subtract_fusion
  409.6 0.6 all-reduce.13.cloned.1.call-done
  410.3 1.1 multiply_reduce_fusion.7
  411.4 1.0 fusion.10
  412.4 0.7 copy.8
  413.1 544.4 %reduce-scatter.2.cloned.1.call-done = f32[32,32768]{1,0:T(8,128)} async-done(((f32[256,32768]{1,0:T(8,128)}), f32[32,32768]{1,0:T(8,128)}) %reduce-scatter.2.cloned.1.call-update) | async-done | bytes 4194320 | tf_op jit(solution)/shard_map/reduce_scatter | solution.py:61
  (9 shorter events, 0.1 us)
Async XLA Ops:
  7.2 101.2 %all-reduce.7.cloned.1.call-start = ((), (), s32[]{:S(2)}) async-start(), calls=%async_computation.1 | async-start | bytes 262144 | tf_op jit(solution)/shard_map/psum | solution.py:29
  14.3 10.0 %copy-start.3 = (bf16[32,256]{1,0:T(8,128)(2,1)S(1)}, bf16[32,256]{1,0:T(8,128)(2,1)}, u32[]{:S(2)}) copy-start(bf16[32,256]{1,0:T(8,128)(2,1)} %param.4) | copy-start | bytes 49156
  14.4 21.5 %copy-start.2 = (bf16[160,256]{1,0:T(8,128)(2,1)S(1)}, bf16[160,256]{1,0:T(8,128)(2,1)}, u32[]{:S(2)}) copy-start(bf16[160,256]{1,0:T(8,128)(2,1)} %param.5) | copy-start | bytes 245764
  24.3 5.7 copy-start
  35.8 154.6 %all-reduce.9.cloned.1.call-start = ((), (), s32[]{:S(2)}) async-start(), calls=%async_computation.2 | async-start | bytes 262144 | tf_op jit(solution)/shard_map/psum | solution.py:29
  36.0 85.1 %copy-start.4 = (s32[160]{0:T(256)S(1)}, s32[160]{0:T(256)}, u32[]{:S(2)}) copy-start(s32[160]{0:T(256)} %param.7) | copy-start | bytes 1924
  36.0 197.7 %copy-start.5 = (u32[32]{0:T(128)S(1)}, u32[32]{0:T(128)}, u32[]{:S(2)}) copy-start(u32[32]{0:T(128)} %constant.63) | copy-start | bytes 388
  121.0 151.6 %all-reduce.11.cloned.1.call-start = ((), (), s32[]{:S(2)}) async-start(), calls=%async_computation.3 | async-start | bytes 262144 | tf_op jit(solution)/shard_map/psum | solution.py:29
  203.1 207.1 %all-reduce.13.cloned.1.call-start = ((), (), s32[]{:S(2)}) async-start(), calls=%async_computation.5 | async-start | bytes 327680 | tf_op jit(solution)/shard_map/psum | solution.py:65
  344.3 3.9 copy-start.1
  381.0 576.6 %reduce-scatter.2.cloned.1.call-start = ((), (), s32[]{:S(2)}) async-start(), calls=%async_computation.4 | async-start | bytes 37748736 | tf_op jit(solution)/shard_map/reduce_scatter | solution.py:61
Sparse Core Ops, SparseCore 0:
  35.9 72.4 all-reduce.6
  121.2 69.1 all-reduce.8
  203.3 69.2 all-reduce.10
  381.1 29.1 all-reduce.12
  414.5 543.0 reduce-scatter.1
where the time goes:
time: 965 us; the launch traced here: 964 us
  waiting for transfers between devices  708 us (73%)
  other arithmetic  80.2 us (8%)
  matrix products  75.1 us (8%)
  blocking collectives  73 us (8%)
  between operations  14.6 us (2%)
  local copies, waits for them, and re-layouts  13.2 us (1%)
    reduce_scatter x1, waiting for transfers between devices, body(): proto_grad = lax.psum_scatter(term, 'rows', scatter_dimension=0, tiled=True)  544 us
    psum x3, waiting for transfers between devices, body(): lax.psum(jnp.sum(energy * row_scale[:, None], axis=0), 'rows')  163 us
    all_gather x1, blocking collectives, body(): teach_all = lax.all_gather(teach_unit, 'rows', axis=0, tiled=True)  30.5 us
    div x1, other arithmetic, body(): term = (head - unit * proj[None, :]) / vnorm[None, :]  28 us
    dot_general x1, matrix products, body(): lax.dot_general(stud_unit_b, dlogit, (((0,), (0,)), ((), ())), preferred_...  22.8 us
    dot_general x1, matrix products, body(): jnp.dot(chosen, unit_b, preferred_element_type=jnp.float32) / teacher_temp  20.9 us
    unnamed x1, blocking collectives  19.9 us
  transfers between devices with their start and end apart: 5, of which 5 were waited for; matrix products, arithmetic and copies ran while one was open for 5% of the time, Pallas kernels for 0%

commit v1 on v0

v1 whole, which is shorter than its diff:
```python
import functools

import jax
import jax.numpy as jnp
from jax import lax
from jax.experimental import pallas as pl
from jax.experimental.pallas import tpu as pltpu
from jax.sharding import PartitionSpec as P

teacher_temp = 0.07
student_temp = 0.1
eps = 1e-06
LOG2E = 1.4426950408889634
GROUP = 4
F32 = jnp.float32
BF16 = jnp.bfloat16
NT = (((1,), (1,)), ((), ()))


def params(mib):
    return pltpu.CompilerParams(vmem_limit_bytes=mib * 1024 * 1024)


def whole(shape):
    return pl.BlockSpec(shape, lambda i, *_: (0,) * len(shape))


def cols(rows, width):
    return pl.BlockSpec((rows, width), lambda i, *_: (0, i))


def to_column(row):
    return jnp.broadcast_to(row, (128, row.shape[1])).T


def lane_sums(x):
    total = x[:, :128]
    for at in range(128, x.shape[1], 128):
        total = total + x[:, at : at + 128]
    return total


def to_row(acc):
    return jnp.sum(acc.T, axis=0, keepdims=True)


def unit_kernel(place, v_ref, unit_ref, inv_ref):
    v = v_ref[...].astype(F32)
    inv = lax.rsqrt(jnp.sum(v * v, axis=0, keepdims=True) + eps)
    unit_ref[...] = (v * inv).astype(BF16)
    inv_ref[...] = inv


def unit_call(place, v, kl, width):
    d = v.shape[0]
    steps = kl // width
    return pl.pallas_call(
        unit_kernel,
        out_shape=(jax.ShapeDtypeStruct((d, kl), BF16), jax.ShapeDtypeStruct((1, kl), F32)),
        grid_spec=pltpu.PrefetchScalarGridSpec(
            num_scalar_prefetch=1,
            grid=(steps,),
            in_specs=[pl.BlockSpec((d, width), lambda i, p: (0, p[0] * steps + i))],
            out_specs=(cols(d, width), cols(1, width)),
        ),
        cost_estimate=pl.CostEstimate(flops=4 * d * kl, bytes_accessed=4 * d * kl, transcendentals=kl),
        compiler_params=params(32),
        name="unit",
    )(place, v)


def energy_kernel(total_k, teach_ref, unit_ref, energy_ref, sum_ref, acc):
    i = pl.program_id(0)
    dots = jnp.dot(teach_ref[...], unit_ref[...], preferred_element_type=F32)
    energy = jnp.exp2(dots * (LOG2E / teacher_temp))
    energy_ref[...] = energy
    col = 1.0 / (jnp.sum(energy, axis=0, keepdims=True) * total_k)
    part = lane_sums(energy * col)

    @pl.when(i == 0)
    def _():
        acc[...] = part

    @pl.when(i > 0)
    def _():
        acc[...] += part

    @pl.when(i == pl.num_programs(0) - 1)
    def _():
        sum_ref[...] = to_row(acc[...])


def energy_call(teach, unit_b, total_k, width):
    t, d = teach.shape
    kl = unit_b.shape[1]
    return pl.pallas_call(
        functools.partial(energy_kernel, float(total_k)),
        out_shape=(jax.ShapeDtypeStruct((t, kl), F32), jax.ShapeDtypeStruct((1, t), F32)),
        grid=(kl // width,),
        in_specs=[whole((t, d)), cols(d, width)],
        out_specs=(cols(t, width), whole((1, t))),
        scratch_shapes=[pltpu.VMEM((t, 128), F32)],
        cost_estimate=pl.CostEstimate(
            flops=2 * t * d * kl, bytes_accessed=4 * t * kl + 2 * d * kl, transcendentals=t * kl
        ),
        compiler_params=params(32),
        name="energy",
    )(teach, unit_b)


def iterate_kernel(total_k, last, sum_in, energy_ref, *refs):
    if last:
        unit_ref, sum_ref, scaled_ref, mean_ref, acc, row = refs
    else:
        sum_ref, acc, row = refs
    i = pl.program_id(0)
    t, width = energy_ref.shape

    @pl.when(i == 0)
    def _():
        row[...] = to_column(1.0 / (sum_in[...] * float(t)))

    scale = row[...]
    mass = []
    for at in range(0, width, 128):
        mass.append(jnp.sum(energy_ref[:, at : at + 128] * scale, axis=0, keepdims=True))
    part = None
    for n, at in enumerate(range(0, width, 128)):
        scaled = energy_ref[:, at : at + 128] * (1.0 / (mass[n] * total_k))
        if last:
            scaled_ref[:, at : at + 128] = scaled.astype(BF16)
        part = scaled if part is None else part + scaled

    @pl.when(i == 0)
    def _():
        acc[...] = part

    @pl.when(i > 0)
    def _():
        acc[...] += part

    if last:
        mean = lax.dot_general(unit_ref[...], scaled_ref[...], NT, preferred_element_type=F32)

        @pl.when(i == 0)
        def _():
            mean_ref[...] = mean

        @pl.when(i > 0)
        def _():
            mean_ref[...] += mean

    @pl.when(i == pl.num_programs(0) - 1)
    def _():
        sum_ref[...] = to_row(acc[...])


def iterate_call(sums, energy, unit_b, total_k, width, last):
    t, kl = energy.shape
    d = unit_b.shape[0]
    out_shape = [jax.ShapeDtypeStruct((1, t), F32)]
    out_specs = [whole((1, t))]
    in_specs = [whole((1, t)), cols(t, width)]
    args = [sums, energy]
    if last:
        out_shape += [jax.ShapeDtypeStruct((t, kl), BF16), jax.ShapeDtypeStruct((d, t), F32)]
        out_specs += [cols(t, width), whole((d, t))]
        in_specs += [cols(d, width)]
        args += [unit_b]
    return pl.pallas_call(
        functools.partial(iterate_kernel, float(total_k), last),
        out_shape=out_shape,
        grid=(kl // width,),
        in_specs=in_specs,
        out_specs=out_specs,
        scratch_shapes=[pltpu.VMEM((t, 128), F32), pltpu.VMEM((t, 128), F32)],
        cost_estimate=pl.CostEstimate(flops=4 * t * kl, bytes_accessed=4 * t * kl, transcendentals=kl),
        compiler_params=params(32),
        name="iterate_last" if last else "iterate",
    )(*args)


def student_kernel(block, place, stud_ref, unit_ref, expo_ref, denom_ref, pull_ref, acc):
    i = pl.program_id(0)
    s = stud_ref.shape[0]

    @pl.when(i == 0)
    def _():
        acc[...] = jnp.zeros_like(acc)
        pull_ref[...] = jnp.zeros_like(pull_ref)

    for at in range(0, s, block):
        logits = jnp.dot(stud_ref[at : at + block, :], unit_ref[...], preferred_element_type=F32)
        expo = jnp.exp2(logits * (LOG2E / student_temp))
        expo_ref[at : at + block, :] = expo.astype(BF16)
        acc[at : at + block, :] += lane_sums(expo)
    mine = pull_ref.shape[1]
    start = pl.multiple_of(place[1] * mine, 128)
    pull_ref[...] += lax.dot_general(
        unit_ref[...], expo_ref[pl.ds(start, mine), :], NT, preferred_element_type=F32
    )

    @pl.when(i == pl.num_programs(0) - 1)
    def _():
        denom_ref[...] = to_row(acc[...])


def student_call(place, stud, unit_b, mine, width):
    s, d = stud.shape
    kl = unit_b.shape[1]
    return pl.pallas_call(
        functools.partial(student_kernel, 256),
        out_shape=(
            jax.ShapeDtypeStruct((s, kl), BF16),
            jax.ShapeDtypeStruct((1, s), F32),
            jax.ShapeDtypeStruct((d, mine), F32),
        ),
        grid_spec=pltpu.PrefetchScalarGridSpec(
            num_scalar_prefetch=1,
            grid=(kl // width,),
            in_specs=[whole((s, d)), cols(d, width)],
            out_specs=(cols(s, width), whole((1, s)), whole((d, mine))),
            scratch_shapes=[pltpu.VMEM((s, 128), F32)],
        ),
        cost_estimate=pl.CostEstimate(
            flops=2 * (s + mine) * d * kl, bytes_accessed=2 * (s + d) * kl, transcendentals=s * kl
        ),
        compiler_params=params(48),
        name="student",
    )(place, stud, unit_b)


def pick(column, pairs):
    t, n = column.shape[0], pairs.shape[1]
    which = lax.broadcasted_iota(jnp.int32, (t, 128), 0)
    out = []
    for at in range(0, n, 128):
        hit = which == pairs[:, at : at + 128]
        out.append(jnp.sum(jnp.where(hit, column, 0.0), axis=0, keepdims=True))
    return jnp.concatenate(out, axis=1)


def gather_kernel(stud_ref, pairs_ref, stud_t_ref, weight_ref):
    t = weight_ref.shape[1]
    s = stud_ref.shape[0]
    stud_t = stud_ref[...].astype(F32).T.astype(BF16)
    stud_t_ref[...] = stud_t
    which = lax.broadcasted_iota(jnp.int32, (t, s), 0)
    onehot = (which == pairs_ref[...]).astype(F32).astype(BF16)
    weight_ref[...] = lax.dot_general(stud_t, onehot, NT, preferred_element_type=F32)


def gather_call(stud, pairs, t):
    s, d = stud.shape
    return pl.pallas_call(
        gather_kernel,
        out_shape=(jax.ShapeDtypeStruct((d, s), BF16), jax.ShapeDtypeStruct((d, t), F32)),
        cost_estimate=pl.CostEstimate(flops=2 * s * d * t, bytes_accessed=6 * s * d, transcendentals=0),
        compiler_params=params(48),
        name="by_teacher",
    )(stud, pairs)


def head_kernel(factor, place, sums_ref, denom_ref, pairs_ref, stud_t_ref, weight_ref, expo_ref,
                scaled_ref, v_ref, inv_ref, own_ref, *refs):
    sends, (lhs, lhs_teach, grad) = refs[:-3], refs[-3:]
    t = scaled_ref.shape[0]

    @pl.when(pl.program_id(0) == 0)
    def _():
        sums = sums_ref[...]
        row = 1.0 / (sums * float(t))
        mass = pick(to_column(row * sums * float(t)), pairs_ref[...])
        lhs[...] = (stud_t_ref[...].astype(F32) * (mass / denom_ref[...] * factor)).astype(BF16)
        lhs_teach[...] = (weight_ref[...] * (row * (-factor * t))).astype(BF16)

    head = jnp.dot(lhs[...], expo_ref[...], preferred_element_type=F32)
    head = head + jnp.dot(lhs_teach[...], scaled_ref[...], preferred_element_type=F32)
    inv = inv_ref[...]
    unit = v_ref[...].astype(F32) * inv
    proj = jnp.sum(unit * head, axis=0, keepdims=True)
    grad[...] = (head - unit * proj) * inv
    rows = own_ref.shape[0]
    base = place[1] * (rows * GROUP)

    def part(n):
        start = pl.multiple_of(base + (place[0] ^ n) * rows, rows)
        return grad[pl.ds(start, rows), :]

    own_ref[...] = part(0)
    for n, ref in enumerate(sends):
        ref[...] = part(n + 1).astype(BF16)


def head_call(place, sums, denom, pairs, stud_t, weight, expo, scaled, v, inv, factor, rows, width):
    d, s = stud_t.shape
    t = scaled.shape[0]
    kl = expo.shape[1]
    steps = kl // width
    return pl.pallas_call(
        functools.partial(head_kernel, factor),
        out_shape=[jax.ShapeDtypeStruct((rows, v.shape[1]), F32)]
        + [jax.ShapeDtypeStruct((rows, kl), BF16)] * (GROUP - 1),
        grid_spec=pltpu.PrefetchScalarGridSpec(
            num_scalar_prefetch=1,
            grid=(steps,),
            in_specs=[
                whole((1, t)), whole((1, s)), whole((1, s)), whole((d, s)), whole((d, t)),
                cols(s, width), cols(t, width),
                pl.BlockSpec((d, width), lambda i, p: (0, p[0] * steps + i)),
                cols(1, width),
            ],
            out_specs=[pl.BlockSpec((rows, width), lambda i, p: (0, p[0] * steps + i))]
            + [cols(rows, width)] * (GROUP - 1),
            scratch_shapes=[pltpu.VMEM((d, s), BF16), pltpu.VMEM((d, t), BF16), pltpu.VMEM((d, width), F32)],
        ),
        cost_estimate=pl.CostEstimate(
            flops=2 * (s + t) * d * kl, bytes_accessed=2 * (s + t + d) * kl, transcendentals=0
        ),
        compiler_params=params(48),
        name="head",
    )(place, sums, denom, pairs, stud_t, weight, expo, scaled, v, inv)


def back_kernel(factor, sums_ref, denom_ref, pairs_ref, stud_t_ref, pull_ref, mean_ref, back_ref):
    d, n = pull_ref.shape
    t = mean_ref.shape[1]
    sums = sums_ref[...]
    row = 1.0 / (sums * float(t))
    pairs = pairs_ref[...]
    mass = pick(to_column(row * sums * float(t)), pairs)
    which = lax.broadcasted_iota(jnp.int32, (t, n), 0)
    onehot = (which == pairs).astype(F32)
    target = jnp.dot(
        mean_ref[...] * (row * t), onehot, preferred_element_type=F32, precision=lax.Precision.HIGHEST
    )
    stud_t = stud_t_ref[...].astype(F32)
    back = (pull_ref[...] * (mass / denom_ref[...]) - target) * factor
    back_ref[:d, :] = back
    along = jnp.sum(stud_t * back, axis=0, keepdims=True)
    cross = jnp.sum(stud_t * target, axis=0, keepdims=True) * (1.0 / student_temp)
    at = lax.broadcasted_iota(jnp.int32, (8, n), 0)
    back_ref[d:, :] = jnp.where(at == 0, along, jnp.where(at == 1, cross, 0.0))


def back_call(sums, denom, pairs, stud_t, pull, mean, factor):
    d, n = pull.shape
    return pl.pallas_call(
        functools.partial(back_kernel, factor),
        out_shape=jax.ShapeDtypeStruct((d + 8, n), F32),
        cost_estimate=pl.CostEstimate(flops=12 * d * n * mean.shape[1], bytes_accessed=12 * d * n, transcendentals=0),
        compiler_params=params(48),
        name="back",
    )(sums, denom, pairs, stud_t, pull, mean)


def body(teacher_features, student_features, v, pairing):
    n_rows, n_proto = lax.axis_size("rows"), lax.axis_size("proto")
    r, p = lax.axis_index("rows"), lax.axis_index("proto")
    d, local_k = v.shape
    total_k = local_k * n_proto
    kl = local_k // GROUP
    t_dev, s_dev = teacher_features.shape[0], student_features.shape[0]
    t, s = t_dev * n_rows, s_dev * n_rows
    at, group = r % GROUP, r // GROUP
    place = jnp.stack([at, group]).astype(jnp.int32)
    factor = total_k / 64.0 / student_temp

    def swap_rows(x, n):
        return lax.ppermute(x, "rows", [(j, j ^ n) for j in range(n_rows)])

    def swap_proto(x, n):
        return lax.ppermute(x, "proto", [(j, j ^ n) for j in range(n_proto)])

    def total(x):
        n = 1
        while n < n_proto:
            x = x + swap_proto(x, n)
            n *= 2
        n = 1
        while n < GROUP:
            x = x + swap_rows(x, n)
            n *= 2
        return x

    tf = teacher_features.astype(F32)
    teach = (tf / jnp.sqrt(jnp.sum(tf * tf, axis=1, keepdims=True) + eps)).astype(BF16)
    sf = student_features.astype(F32)
    snorm = jnp.sqrt(jnp.sum(sf * sf, axis=1, keepdims=True) + eps)
    stud_unit = sf / snorm
    stud = stud_unit.astype(BF16)

    lines = 16 * -(-(-(-s_dev // d)) // 8)
    half = lines // 2
    flat = jnp.pad(pairing, (0, half * d - s_dev)).reshape(half, d)
    digits = jnp.concatenate([flat // 64, flat % 64], axis=0).astype(BF16)

    def join(x, n):
        other = swap_rows(x, n)
        low = (r // n) % 2 == 0
        return jnp.concatenate([jnp.where(low, x, other), jnp.where(low, other, x)], axis=0)

    packed = jnp.concatenate([teach, stud, digits], axis=0)[None]
    n = 1
    while n < GROUP:
        packed = join(packed, n)
        n *= 2
    teach_all, rest = packed[:, :t_dev], packed[:, t_dev:]
    while n < n_rows:
        teach_all = join(teach_all, n)
        rest = join(rest, n)
        n *= 2
    teach_all = teach_all.reshape(t, d)
    stud_all = rest[:, :s_dev].reshape(s, d)
    digits = rest[:, s_dev:].astype(jnp.int32)
    digits = digits[:, :half] * 64 + digits[:, half:]
    pairs = digits.reshape(n_rows, half * d)[:, :s_dev].reshape(1, s)

    width = min(1024, kl)
    unit_b, inv = unit_call(place, v, kl, width)
    energy, sums = energy_call(teach_all, unit_b, total_k, width)
    mine = s_dev * GROUP
    expo, denom, pull = student_call(place, stud_all, unit_b, mine, min(512, kl))
    stud_t, weight = gather_call(stud_all, pairs, t)
    (sums,) = iterate_call(total(sums), energy, unit_b, total_k, width, False)
    sums, scaled, mean = iterate_call(total(sums), energy, unit_b, total_k, width, True)
    both = total(jnp.concatenate([sums, denom], axis=1))
    sums, denom = both[:, :t], both[:, t:]

    rows = d // n_rows
    grads = head_call(
        place, sums, denom, pairs, stud_t, weight, expo, scaled, v, inv, factor, rows, min(1024, kl)
    )
    proto_grad = grads[0]
    for n in range(1, GROUP):
        got = swap_rows(grads[n], n).astype(F32)
        proto_grad = lax.dynamic_update_slice(proto_grad, got, (0, (at ^ n) * kl))

    def of_group(x):
        return lax.dynamic_slice_in_dim(x, group * mine, mine, 1)

    back = back_call(sums, of_group(denom), of_group(pairs), of_group(stud_t), pull, mean, factor)
    body_rows, tail = back[:d], back[d:]
    n = n_proto // 2
    while n >= 1:
        height = body_rows.shape[0] // 2
        bit = (p // n) % 2
        keep = lax.dynamic_slice_in_dim(body_rows, bit * height, height, 0)
        send = lax.dynamic_slice_in_dim(body_rows, (1 - bit) * height, height, 0)
        got = swap_proto(jnp.concatenate([send, tail], axis=0), n)
        body_rows, tail = keep + got[:height], tail + got[height:]
        n //= 2
    terms = jnp.concatenate([body_rows, tail], axis=0)

    def block(n):
        return lax.dynamic_slice_in_dim(terms, (at ^ n) * s_dev, s_dev, 1)

    full = block(0)
    for n in range(1, GROUP):
        full = full + swap_rows(block(n), n)
    share = d // n_proto
    along, cross = full[share], full[share + 1]
    stud_part = lax.dynamic_slice_in_dim(stud_unit, p * share, share, 1)
    student_grad = (full[:share].T - stud_part * along[:, None]) / snorm
    own = lax.dynamic_slice_in_dim(denom[0], r * s_dev, s_dev, 0)
    own_pairs = pairing
    row = 1.0 / (sums[0] * t)
    mass = jnp.take(row * sums[0] * t, own_pairs, axis=0)
    loss = jnp.log(own) * mass - cross
    return (proto_grad, student_grad, loss)


def solution(mesh):
    return jax.shard_map(
        body,
        mesh=mesh,
        in_specs=(P("rows", None), P("rows", None), P(None, "proto"), P("rows")),
        out_specs=(P("rows", "proto"), P("rows", "proto"), P("rows")),
        check_vma=False,
    )
```

time: 965 us -> 176 us (0.18)
  waiting for transfers between devices: 708 us -> 37.7 us
  matrix products: 75.1 us -> 0 us
  blocking collectives: 73 us -> 0 us
  other arithmetic: 80.2 us -> 16.1 us
  Pallas kernels: 0 us -> 53.1 us
  starting transfers between devices: 0.21 us -> 33 us
  local copies, waits for them, and re-layouts: 13.2 us -> 34.3 us
  between operations: 14.6 us -> 1.05 us
    reduce_scatter x1 -> x0, waiting for transfers between devices: 544 us -> none  [body(): proto_grad = lax.psum_scatter(term, 'rows', scatter_dimension=0, tiled=True)]
    psum x4 -> x0, waiting for transfers between devices: 163 us -> none  [the longest x3 163 us: body(): lax.psum(jnp.sum(energy * row_scale[:, None], axis=0), 'rows')]
    dot_general x5 -> x0, matrix products: 75.1 us -> none  [the longest x1 22.8 us: body(): lax.dot_general(stud_unit_b, dlogit, (((0,), (0,)), ((), ())), preferred_...]
    pallas_call x0 -> x8, Pallas kernels: none -> 53.1 us  [the longest x1 18.2 us: student_call(): pl.pallas_call(functools.partial(student_kernel, 256), out_shape=(jax.Sha...]
    ppermute x0 -> x24, waiting for transfers between devices: none -> 37.7 us  [the longest x16 30.3 us: swap_rows(): return lax.ppermute(x, 'rows', [(j, j ^ n) for j in range(n_rows)])]
    ppermute x0 -> x24, starting transfers between devices: none -> 33 us  [the longest x16 26.8 us: swap_rows(): return lax.ppermute(x, 'rows', [(j, j ^ n) for j in range(n_rows)])]
    all_gather x1 -> x0, blocking collectives: 30.5 us -> none  [body(): teach_all = lax.all_gather(teach_unit, 'rows', axis=0, tiled=True)]
    div x7 -> x2, other arithmetic: 32.1 us -> 2.25 us  [the longest x1 1.49 us: body(): student_grad = (full[:share].T - stud_part * along[:, None]) / snorm]
  transfers between devices with their start and end apart: 5 -> 24, of which waited for: 5 -> 16; matrix products, arithmetic and copies ran while one was open for 5% -> 8% of each run, Pallas kernels for 0% -> 17%
where the time goes in v1:
time: 176 us; the launch traced here: 175 us
  Pallas kernels  53.1 us (30%)
  waiting for transfers between devices  37.7 us (21%)
  local copies, waits for them, and re-layouts  34.3 us (19%)
  starting transfers between devices  33 us (19%)
  other arithmetic  16.1 us (9%)
    ppermute x16, waiting for transfers between devices, swap_rows(): return lax.ppermute(x, 'rows', [(j, j ^ n) for j in range(n_rows)])  30.3 us
    unnamed x23, local copies, waits for them, and re-layouts  27.4 us
    ppermute x16, starting transfers between devices, swap_rows(): return lax.ppermute(x, 'rows', [(j, j ^ n) for j in range(n_rows)])  26.8 us
    pallas_call x1, Pallas kernels, student_call(): pl.pallas_call(functools.partial(student_kernel, 256), out_shape=(jax.Sha...  18.2 us
    pallas_call x1, Pallas kernels, head_call(): pl.pallas_call(functools.partial(head_kernel, factor), out_shape=[jax.Sha...  16.6 us
    pallas_call x2, Pallas kernels, iterate_call(): pl.pallas_call(functools.partial(iterate_kernel, float(total_k), last), o...  9.44 us
    ppermute x8, waiting for transfers between devices, swap_proto(): return lax.ppermute(x, 'proto', [(j, j ^ n) for j in range(n_proto)])  7.41 us
    dynamic_update_slice x3, other arithmetic, body(): proto_grad = lax.dynamic_update_slice(proto_grad, got, (0, (at ^ n) * kl))  6.24 us
  transfers between devices with their start and end apart: 24, of which 16 were waited for; matrix products, arithmetic and copies ran while one was open for 8% of the time, Pallas kernels for 17%

profile of v1, /device:TPU:0, one launch (start us, length us, event | category | flops | bytes accessed | tf_op | source)
XLA Modules:
  0.0 175.1 jit_solution(12280490086246113633)
XLA Ops:
  0.6 0.8 copy.28
  1.5 0.8 multiply_reduce_fusion
  2.3 0.7 pad.4
  3.3 1.0 copy.29
  4.3 0.8 convert_divide_fusion
  5.3 3.0 %collective-permute-start = (bf16[1,208,256]{1,2,0:T(8,128)(2,1)S(1)}, bf16[1,208,256]{1,2,0:T(8,128)(2,1)S(1)}, u32[]{:S(2)}, u32[]{:S(2)}) collective-permute-start(bf16[1,208,256]{1,2,0:T(8,128)(2,1)S(1)} %maximum_bitcast_fusion), channel_id=1, source_target_pairs={{0,4},{4,0},{8,12},{12,8},{16,20},{20,16},{24,28},{28,24},{1,5},{5... | collective-permute-start | bytes 319496 | tf_op jit(solution)/shard_map/ppermute | solution.py:370
  8.3 3.5 %collective-permute-done = bf16[1,208,256]{1,2,0:T(8,128)(2,1)S(1)} collective-permute-done((bf16[1,208,256]{1,2,0:T(8,128)(2,1)S(1)}, bf16[1,208,256]{1,2,0:T(8,128)(2,1)S(1)}, u32[]{:S(2)}, u32[]{:S(2)}) %collective-permute-start) | collective-permute-done | bytes 106528 | tf_op jit(solution)/shard_map/ppermute | solution.py:370
  12.0 1.9 %collective-permute-start.1 = (bf16[2,208,256]{1,2,0:T(8,128)(2,1)S(1)}, bf16[2,208,256]{1,2,0:T(8,128)(2,1)S(1)}, u32[]{:S(2)}, u32[]{:S(2)}) collective-permute-start(bf16[2,208,256]{1,2,0:T(8,128)(2,1)S(1)} %pad_maximum_fusion.3), channel_id=1, source_target_pairs={{0,8},{4,12},{8,0},{12,4},{16,24},{20,28},{24,16},{28,20},{1,9},{5... | collective-permute-start | bytes 638984 | tf_op jit(solution)/shard_map/ppermute | solution.py:370
  13.9 5.7 %collective-permute-done.1 = bf16[2,208,256]{1,2,0:T(8,128)(2,1)S(1)} collective-permute-done((bf16[2,208,256]{1,2,0:T(8,128)(2,1)S(1)}, bf16[2,208,256]{1,2,0:T(8,128)(2,1)S(1)}, u32[]{:S(2)}, u32[]{:S(2)}) %collective-permute-start.1) | collective-permute-done | bytes 213024 | tf_op jit(solution)/shard_map/ppermute | solution.py:370
  19.6 2.6 %collective-permute-start.2 = (bf16[4,32,256]{1,2,0:T(8,128)(2,1)S(1)}, bf16[4,32,256]{1,2,0:T(8,128)(2,1)S(1)}, u32[]{:S(2)}, u32[]{:S(2)}) collective-permute-start(bf16[4,32,256]{1,2,0:T(8,128)(2,1)S(1)} %fusion.2), channel_id=1, source_target_pairs={{0,16},{4,20},{8,24},{12,28},{16,0},{20,4},{24,8},{28,12},{1,17},{... | collective-permute-start | bytes 196616 | tf_op jit(solution)/shard_map/ppermute | solution.py:370
  22.3 5.8 %copy-done = bf16[256,32768]{1,0:T(8,128)(2,1)S(1)} copy-done((bf16[256,32768]{1,0:T(8,128)(2,1)S(1)}, bf16[256,32768]{1,0:T(8,128)(2,1)}, u32[]{:S(2)}) %copy-start) | copy-done | bytes 16777240
  28.1 2.7 %unit.1 = (bf16[256,8192]{1,0:T(8,128)(2,1)S(1)}, f32[1,8192]{1,0:T(1,128)S(1)}) custom-call(s32[2]{0:T(128)S(1)} %pad_add_fusion.place, bf16[256,32768]{1,0:T(8,128)(2,1)S(1)} %copy-done), custom_call_target="tpu_custom_call" | custom-call | flops 8388608 | bytes 8388608 | tf_op jit(solution)/shard_map/unit/pallas_call | solution.py:57
  30.8 2.0 %copy-done.4 = bf16[256,8192]{1,0:T(8,128)(2,1)} copy-done((bf16[256,8192]{1,0:T(8,128)(2,1)}, bf16[256,8192]{1,0:T(8,128)(2,1)S(1)}, u32[]{:S(2)}) %copy-start.4) | copy-done | bytes 4194328
  33.1 2.2 %copy-done.5 = bf16[256,8192]{1,0:T(8,128)(2,1)S(1)} copy-done((bf16[256,8192]{1,0:T(8,128)(2,1)S(1)}, bf16[256,8192]{1,0:T(8,128)(2,1)}, u32[]{:S(2)}) %copy-start.5) | copy-done | bytes 4194328
  35.3 4.7 %energy.1 = (f32[256,8192]{1,0:T(8,128)S(1)}, f32[1,256]{1,0:T(1,128)S(1)}) custom-call(bf16[256,256]{1,0:T(8,128)(2,1)S(1)} %bitcast.22, bf16[256,8192]{1,0:T(8,128)(2,1)S(1)} %copy-done.5), custom_call_target="tpu_custom_call" | custom-call | flops 1073741824 | bytes 12582912 | tf_op jit(solution)/shard_map/energy/pallas_call | solution.py:96
  40.0 3.3 %copy-done.1 = f32[256,8192]{1,0:T(8,128)} copy-done((f32[256,8192]{1,0:T(8,128)}, f32[256,8192]{1,0:T(8,128)S(1)}, u32[]{:S(2)}) %copy-start.1) | copy-done | bytes 8388632
  44.5 1.5 collective-permute-start.4
  46.0 2.0 %collective-permute-done.4 = f32[1,256]{1,0:T(1,128)S(1)} collective-permute-done((f32[1,256]{1,0:T(1,128)S(1)}, f32[1,256]{1,0:T(1,128)S(1)}, u32[]{:S(2)}, u32[]{:S(2)}) %collective-permute-start.4) | collective-permute-done | bytes 1056 | tf_op jit(solution)/shard_map/ppermute | solution.py:373
  48.0 1.5 collective-permute-start.5
  49.5 2.1 %collective-permute-done.5 = f32[1,256]{1,0:T(1,128)S(1)} collective-permute-done((f32[1,256]{1,0:T(1,128)S(1)}, f32[1,256]{1,0:T(1,128)S(1)}, u32[]{:S(2)}, u32[]{:S(2)}) %collective-permute-start.5) | collective-permute-done | bytes 1056 | tf_op jit(solution)/shard_map/ppermute | solution.py:370
  51.6 2.8 %collective-permute-start.6 = (f32[1,256]{1,0:T(1,128)S(1)}, f32[1,256]{1,0:T(1,128)S(1)}, u32[]{:S(2)}, u32[]{:S(2)}) collective-permute-start(f32[1,256]{1,0:T(1,128)S(1)} %add.179), channel_id=1, source_target_pairs={{0,8},{4,12},{8,0},{12,4},{16,24},{20,28},{24,16},{28,20},{1,9},{5... | collective-permute-start | bytes 3080 | tf_op jit(solution)/shard_map/ppermute | solution.py:370
  54.4 1.5 collective-permute-done.6
  56.0 3.4 %copy-done.2 = f32[256,8192]{1,0:T(8,128)S(1)} copy-done((f32[256,8192]{1,0:T(8,128)S(1)}, f32[256,8192]{1,0:T(8,128)}, u32[]{:S(2)}) %copy-start.2) | copy-done | bytes 8388632
  59.4 2.7 %iterate.1 = f32[1,256]{1,0:T(1,128)S(1)} custom-call(f32[1,256]{1,0:T(1,128)S(1)} %add.180.sum_in, f32[256,8192]{1,0:T(8,128)S(1)} %copy-done.2), custom_call_target="tpu_custom_call" | custom-call | flops 8388608 | bytes 8388608 | tf_op jit(solution)/shard_map/iterate/pallas_call | solution.py:170
  62.2 1.1 collective-permute-done.7
  63.3 1.5 collective-permute-start.8
  64.8 2.0 %collective-permute-done.8 = f32[1,256]{1,0:T(1,128)S(1)} collective-permute-done((f32[1,256]{1,0:T(1,128)S(1)}, f32[1,256]{1,0:T(1,128)S(1)}, u32[]{:S(2)}, u32[]{:S(2)}) %collective-permute-start.8) | collective-permute-done | bytes 1056 | tf_op jit(solution)/shard_map/ppermute | solution.py:373
  66.9 1.5 collective-permute-start.9
  68.3 2.1 %collective-permute-done.9 = f32[1,256]{1,0:T(1,128)S(1)} collective-permute-done((f32[1,256]{1,0:T(1,128)S(1)}, f32[1,256]{1,0:T(1,128)S(1)}, u32[]{:S(2)}, u32[]{:S(2)}) %collective-permute-start.9) | collective-permute-done | bytes 1056 | tf_op jit(solution)/shard_map/ppermute | solution.py:370
  70.4 2.5 %collective-permute-start.10 = (f32[1,256]{1,0:T(1,128)S(1)}, f32[1,256]{1,0:T(1,128)S(1)}, u32[]{:S(2)}, u32[]{:S(2)}) collective-permute-start(f32[1,256]{1,0:T(1,128)S(1)} %add.183), channel_id=1, source_target_pairs={{0,8},{4,12},{8,0},{12,4},{16,24},{20,28},{24,16},{28,20},{1,9},{5... | collective-permute-start | bytes 3080 | tf_op jit(solution)/shard_map/ppermute | solution.py:370
  72.9 1.5 collective-permute-done.10
  74.4 3.4 %copy-done.3 = f32[256,8192]{1,0:T(8,128)S(1)} copy-done((f32[256,8192]{1,0:T(8,128)S(1)}, f32[256,8192]{1,0:T(8,128)}, u32[]{:S(2)}) %copy-start.3) | copy-done | bytes 8388632
  77.8 2.2 %copy-done.6 = bf16[256,8192]{1,0:T(8,128)(2,1)S(1)} copy-done((bf16[256,8192]{1,0:T(8,128)(2,1)S(1)}, bf16[256,8192]{1,0:T(8,128)(2,1)}, u32[]{:S(2)}) %copy-start.6) | copy-done | bytes 4194328
  80.0 6.7 %iterate_last.1 = (f32[1,256]{1,0:T(1,128)S(1)}, bf16[256,8192]{1,0:T(8,128)(2,1)S(1)}, f32[256,256]{1,0:T(8,128)S(1)}) custom-call(f32[1,256]{1,0:T(1,128)S(1)} %add.184.sum_in, f32[256,8192]{1,0:T(8,128)S(1)} %copy-done.3, bf16[256,8192]{1,0:T(8,128)(2,1)S(1)} %copy-done.6), custom_call_target="tpu_custom_call" | custom-call | flops 8388608 | bytes 8388608 | tf_op jit(solution)/shard_map/iterate_last/pallas_call | solution.py:170
  86.7 2.0 %copy-done.8 = bf16[256,8192]{1,0:T(8,128)(2,1)} copy-done((bf16[256,8192]{1,0:T(8,128)(2,1)}, bf16[256,8192]{1,0:T(8,128)(2,1)S(1)}, u32[]{:S(2)}) %copy-start.8) | copy-done | bytes 4194328
  89.1 1.2 slice_maximum_fusion
  90.5 1.5 copy.36
  92.0 2.2 %copy-done.7 = bf16[256,8192]{1,0:T(8,128)(2,1)S(1)} copy-done((bf16[256,8192]{1,0:T(8,128)(2,1)S(1)}, bf16[256,8192]{1,0:T(8,128)(2,1)}, u32[]{:S(2)}) %copy-start.7) | copy-done | bytes 4194328
  94.2 18.2 %student.1 = (bf16[1280,8192]{1,0:T(8,128)(2,1)}, f32[1,1280]{1,0:T(1,128)S(1)}, f32[256,640]{1,0:T(8,128)S(1)}) custom-call(s32[2]{0:T(128)S(1)} %pad_add_fusion.place, bf16[1280,256]{1,0:T(8,128)(2,1)S(1)} %bitcast.20, bf16[256,8192]{1,0:T(8,128)(2,1)S(1)} %copy-done.7), custom_call_target="tpu_custom_call" | custom-call | flops 8053063680 | bytes 25165824 | tf_op jit(solution)/shard_map/student/pallas_call | solution.py:211
  112.4 1.3 slice_add_fusion
  113.8 1.5 copy.38
  115.4 1.5 collective-permute-start.13
  117.4 1.8 %collective-permute-done.13 = f32[1,1536]{1,0:T(1,128)S(1)} collective-permute-done((f32[1,1536]{1,0:T(1,128)S(1)}, f32[1,1536]{1,0:T(1,128)S(1)}, u32[]{:S(2)}, u32[]{:S(2)}) %collective-permute-start.13) | collective-permute-done | bytes 6176 | tf_op jit(solution)/shard_map/ppermute | solution.py:373
  119.1 1.5 collective-permute-start.14
  120.7 2.2 %collective-permute-done.14 = f32[1,1536]{1,0:T(1,128)S(1)} collective-permute-done((f32[1,1536]{1,0:T(1,128)S(1)}, f32[1,1536]{1,0:T(1,128)S(1)}, u32[]{:S(2)}, u32[]{:S(2)}) %collective-permute-start.14) | collective-permute-done | bytes 6176 | tf_op jit(solution)/shard_map/ppermute | solution.py:370
  122.8 2.1 %collective-permute-start.15 = (f32[1,1536]{1,0:T(1,128)S(1)}, f32[1,1536]{1,0:T(1,128)S(1)}, u32[]{:S(2)}, u32[]{:S(2)}) collective-permute-start(f32[1,1536]{1,0:T(1,128)S(1)} %add.187), channel_id=1, source_target_pairs={{0,8},{4,12},{8,0},{12,4},{16,24},{20,28},{24,16},{28,20},{1,9},{5... | collective-permute-start | bytes 18440 | tf_op jit(solution)/shard_map/ppermute | solution.py:370
  124.9 1.6 collective-permute-done.15
  126.6 1.0 back.1
  127.7 1.5 collective-permute-start.19
  129.2 16.6 %head.1 = (f32[32,32768]{1,0:T(8,128)}, bf16[32,8192]{1,0:T(8,128)(2,1)S(1)}, bf16[32,8192]{1,0:T(8,128)(2,1)S(1)}, bf16[32,8192]{1,0:T(8,128)(2,1)S(1)}) custom-call(s32[2]{0:T(128)S(1)} %pad_add_fusion.place, f32[1,256]{1,0:T(1,128)S(1)} %slice.78.sums_ref, f32[1,1280]{1,0:T(1,128)S(1)} %slice.79.denom_ref, s32[1,1280]{1,0:T(1,128)S(1)} %reshape.45.pairs_ref, ...), custom_call_target="tpu_custom_call" | custom-call | flops 6442450944 | bytes 29360128 | tf_op jit(solution)/shard_map/head/pallas_call | solution.py:300
  145.8 1.5 collective-permute-start.16
  147.3 2.0 %collective-permute-start.17 = (bf16[32,8192]{1,0:T(8,128)(2,1)S(1)}, bf16[32,8192]{1,0:T(8,128)(2,1)}, u32[]{:S(2)}, u32[]{:S(2)}) collective-permute-start(bf16[32,8192]{1,0:T(8,128)(2,1)S(1)} %get-tuple-element.31), channel_id=1, source_target_pairs={{0,8},{4,12},{8,0},{12,4},{16,24},{20,28},{24,16},{28,20},{1,9},{5... | collective-permute-start | bytes 1572872 | tf_op jit(solution)/shard_map/ppermute | solution.py:370
  149.3 1.6 gather_fusion
  151.0 1.0 slice_add_fusion.1
  152.1 0.7 slice_add_fusion.4
  152.9 7.0 %collective-permute-done.16 = bf16[32,8192]{1,0:T(8,128)(2,1)} collective-permute-done((bf16[32,8192]{1,0:T(8,128)(2,1)S(1)}, bf16[32,8192]{1,0:T(8,128)(2,1)}, u32[]{:S(2)}, u32[]{:S(2)}) %collective-permute-start.16) | collective-permute-done | bytes 524320 | tf_op jit(solution)/shard_map/ppermute | solution.py:370
  159.8 2.1 %convert_dynamic-update-slice_fusion.2 = f32[32,32768]{1,0:T(8,128)} fusion(f32[32,32768]{1,0:T(8,128)} %get-tuple-element.29, s32[]{:T(128)S(6)} %select_n.175, bf16[32,8192]{1,0:T(8,128)(2,1)} %collective-permute-done.16), kind=kLoop, calls=%fused_computation.6 | loop fusion | flops 262144 | bytes 1572868 | tf_op jit(solution)/shard_map/dynamic_update_slice | solution.py:437
  162.2 2.1 %convert_dynamic-update-slice_fusion.1 = f32[32,32768]{1,0:T(8,128)} fusion(f32[32,32768]{1,0:T(8,128)} %convert_dynamic-update-slice_fusion.2, s32[]{:T(128)S(6)} %select_n.176, bf16[32,8192]{1,0:T(8,128)(2,1)} %collective-permute-done.17), kind=kLoop, calls=%fused_computation.5 | loop fusion | flops 262144 | bytes 1572868 | tf_op jit(solution)/shard_map/dynamic_update_slice | solution.py:437
  164.5 2.7 %collective-permute-start.23 = (f32[72,160]{1,0:T(8,128)S(1)}, f32[72,160]{1,0:T(8,128)S(1)}, u32[]{:S(2)}, u32[]{:S(2)}) collective-permute-start(f32[72,160]{1,0:T(8,128)S(1)} %get-tuple-element.45), channel_id=1, source_target_pairs={{0,12},{4,8},{8,4},{12,0},{16,28},{20,24},{24,20},{28,16},{1,13},{... | collective-permute-start | bytes 138248 | tf_op jit(solution)/shard_map/ppermute | solution.py:370
  167.2 0.9 collective-permute-start.21
  168.1 2.8 %collective-permute-done.18 = bf16[32,8192]{1,0:T(8,128)(2,1)} collective-permute-done((bf16[32,8192]{1,0:T(8,128)(2,1)S(1)}, bf16[32,8192]{1,0:T(8,128)(2,1)}, u32[]{:S(2)}, u32[]{:S(2)}) %collective-permute-start.18) | collective-permute-done | bytes 524320 | tf_op jit(solution)/shard_map/ppermute | solution.py:370
  170.8 2.1 %convert_dynamic-update-slice_fusion = f32[32,32768]{1,0:T(8,128)} fusion(f32[32,32768]{1,0:T(8,128)} %convert_dynamic-update-slice_fusion.1, s32[]{:T(128)S(6)} %select_n.177, bf16[32,8192]{1,0:T(8,128)(2,1)} %collective-permute-done.18), kind=kLoop, calls=%fused_computation.4 | loop fusion | flops 262144 | bytes 1572868 | tf_op jit(solution)/shard_map/dynamic_update_slice | solution.py:437
  173.0 1.5 fusion.15
  174.5 0.6 fusion.17
  (86 shorter events, 4.6 us)
Async XLA Ops:
  5.3 6.5 %collective-permute-start = (bf16[1,208,256]{1,2,0:T(8,128)(2,1)S(1)}, bf16[1,208,256]{1,2,0:T(8,128)(2,1)S(1)}, u32[]{:S(2)}, u32[]{:S(2)}) collective-permute-start(bf16[1,208,256]{1,2,0:T(8,128)(2,1)S(1)} %maximum_bitcast_fusion), channel_id=1, source_target_pairs={{0,4},{4,0},{8,12},{12,8},{16,20},{20,16},{24,28},{28,24},{1,5},{5... | collective-permute-start | bytes 319496 | tf_op jit(solution)/shard_map/ppermute | solution.py:370
  12.0 7.6 %collective-permute-start.1 = (bf16[2,208,256]{1,2,0:T(8,128)(2,1)S(1)}, bf16[2,208,256]{1,2,0:T(8,128)(2,1)S(1)}, u32[]{:S(2)}, u32[]{:S(2)}) collective-permute-start(bf16[2,208,256]{1,2,0:T(8,128)(2,1)S(1)} %pad_maximum_fusion.3), channel_id=1, source_target_pairs={{0,8},{4,12},{8,0},{12,4},{16,24},{20,28},{24,16},{28,20},{1,9},{5... | collective-permute-start | bytes 638984 | tf_op jit(solution)/shard_map/ppermute | solution.py:370
  19.6 13.2 %collective-permute-start.2 = (bf16[4,32,256]{1,2,0:T(8,128)(2,1)S(1)}, bf16[4,32,256]{1,2,0:T(8,128)(2,1)S(1)}, u32[]{:S(2)}, u32[]{:S(2)}) collective-permute-start(bf16[4,32,256]{1,2,0:T(8,128)(2,1)S(1)} %fusion.2), channel_id=1, source_target_pairs={{0,16},{4,20},{8,24},{12,28},{16,0},{20,4},{24,8},{28,12},{1,17},{... | collective-permute-start | bytes 196616 | tf_op jit(solution)/shard_map/ppermute | solution.py:370
  22.3 5.8 %copy-start = (bf16[256,32768]{1,0:T(8,128)(2,1)S(1)}, bf16[256,32768]{1,0:T(8,128)(2,1)}, u32[]{:S(2)}) copy-start(bf16[256,32768]{1,0:T(8,128)(2,1)} %v_ref.3) | copy-start | bytes 50331652
  30.8 2.0 %copy-start.4 = (bf16[256,8192]{1,0:T(8,128)(2,1)}, bf16[256,8192]{1,0:T(8,128)(2,1)S(1)}, u32[]{:S(2)}) copy-start(bf16[256,8192]{1,0:T(8,128)(2,1)S(1)} %get-tuple-element.19.unit_ref.refs_0_) | copy-start | bytes 12582916
  32.8 13.2 %copy-start.9 = (s32[160]{0:T(256)S(1)}, s32[160]{0:T(256)}, u32[]{:S(2)}) copy-start(s32[160]{0:T(256)} %param.7) | copy-start | bytes 1924
  33.1 2.2 %copy-start.5 = (bf16[256,8192]{1,0:T(8,128)(2,1)S(1)}, bf16[256,8192]{1,0:T(8,128)(2,1)}, u32[]{:S(2)}) copy-start(bf16[256,8192]{1,0:T(8,128)(2,1)} %copy-done.4) | copy-start | bytes 12582916
  40.0 3.3 %copy-start.1 = (f32[256,8192]{1,0:T(8,128)}, f32[256,8192]{1,0:T(8,128)S(1)}, u32[]{:S(2)}) copy-start(f32[256,8192]{1,0:T(8,128)S(1)} %get-tuple-element.21.energy_ref) | copy-start | bytes 25165828
  43.3 1.1 collective-permute-start.3
  43.6 45.2 %collective-permute-start.11 = (bf16[4,176,256]{1,2,0:T(8,128)(2,1)S(1)}, bf16[4,176,256]{1,2,0:T(8,128)(2,1)S(1)}, u32[]{:S(2)}, u32[]{:S(2)}) collective-permute-start(bf16[4,176,256]{1,2,0:T(8,128)(2,1)S(1)} %pad_maximum_fusion.1), channel_id=1, source_target_pairs={{0,16},{4,20},{8,24},{12,28},{16,0},{20,4},{24,8},{28,12},{1,17},{... | collective-permute-start | bytes 1081352 | tf_op jit(solution)/shard_map/ppermute | solution.py:370
  44.5 3.6 %collective-permute-start.4 = (f32[1,256]{1,0:T(1,128)S(1)}, f32[1,256]{1,0:T(1,128)S(1)}, u32[]{:S(2)}, u32[]{:S(2)}) collective-permute-start(f32[1,256]{1,0:T(1,128)S(1)} %add.177), channel_id=1, source_target_pairs={{0,2},{1,3},{2,0},{3,1},{4,6},{5,7},{6,4},{7,5},{8,10},{9,11},{10,... | collective-permute-start | bytes 3080 | tf_op jit(solution)/shard_map/ppermute | solution.py:373
  48.0 3.6 %collective-permute-start.5 = (f32[1,256]{1,0:T(1,128)S(1)}, f32[1,256]{1,0:T(1,128)S(1)}, u32[]{:S(2)}, u32[]{:S(2)}) collective-permute-start(f32[1,256]{1,0:T(1,128)S(1)} %add.178), channel_id=1, source_target_pairs={{0,4},{4,0},{8,12},{12,8},{16,20},{20,16},{24,28},{28,24},{1,5},{5... | collective-permute-start | bytes 3080 | tf_op jit(solution)/shard_map/ppermute | solution.py:370
  51.6 4.4 %collective-permute-start.6 = (f32[1,256]{1,0:T(1,128)S(1)}, f32[1,256]{1,0:T(1,128)S(1)}, u32[]{:S(2)}, u32[]{:S(2)}) collective-permute-start(f32[1,256]{1,0:T(1,128)S(1)} %add.179), channel_id=1, source_target_pairs={{0,8},{4,12},{8,0},{12,4},{16,24},{20,28},{24,16},{28,20},{1,9},{5... | collective-permute-start | bytes 3080 | tf_op jit(solution)/shard_map/ppermute | solution.py:370
  56.0 3.4 %copy-start.2 = (f32[256,8192]{1,0:T(8,128)S(1)}, f32[256,8192]{1,0:T(8,128)}, u32[]{:S(2)}) copy-start(f32[256,8192]{1,0:T(8,128)} %copy-done.1) | copy-start | bytes 25165828
  62.1 1.2 collective-permute-start.7
  63.3 3.6 %collective-permute-start.8 = (f32[1,256]{1,0:T(1,128)S(1)}, f32[1,256]{1,0:T(1,128)S(1)}, u32[]{:S(2)}, u32[]{:S(2)}) collective-permute-start(f32[1,256]{1,0:T(1,128)S(1)} %add.181), channel_id=1, source_target_pairs={{0,2},{1,3},{2,0},{3,1},{4,6},{5,7},{6,4},{7,5},{8,10},{9,11},{10,... | collective-permute-start | bytes 3080 | tf_op jit(solution)/shard_map/ppermute | solution.py:373
  66.9 3.6 %collective-permute-start.9 = (f32[1,256]{1,0:T(1,128)S(1)}, f32[1,256]{1,0:T(1,128)S(1)}, u32[]{:S(2)}, u32[]{:S(2)}) collective-permute-start(f32[1,256]{1,0:T(1,128)S(1)} %add.182), channel_id=1, source_target_pairs={{0,4},{4,0},{8,12},{12,8},{16,20},{20,16},{24,28},{28,24},{1,5},{5... | collective-permute-start | bytes 3080 | tf_op jit(solution)/shard_map/ppermute | solution.py:370
  70.4 4.0 %collective-permute-start.10 = (f32[1,256]{1,0:T(1,128)S(1)}, f32[1,256]{1,0:T(1,128)S(1)}, u32[]{:S(2)}, u32[]{:S(2)}) collective-permute-start(f32[1,256]{1,0:T(1,128)S(1)} %add.183), channel_id=1, source_target_pairs={{0,8},{4,12},{8,0},{12,4},{16,24},{20,28},{24,16},{28,20},{1,9},{5... | collective-permute-start | bytes 3080 | tf_op jit(solution)/shard_map/ppermute | solution.py:370
  74.4 3.4 %copy-start.3 = (f32[256,8192]{1,0:T(8,128)S(1)}, f32[256,8192]{1,0:T(8,128)}, u32[]{:S(2)}) copy-start(f32[256,8192]{1,0:T(8,128)} %copy-done.1) | copy-start | bytes 25165828
  77.8 2.2 %copy-start.6 = (bf16[256,8192]{1,0:T(8,128)(2,1)S(1)}, bf16[256,8192]{1,0:T(8,128)(2,1)}, u32[]{:S(2)}) copy-start(bf16[256,8192]{1,0:T(8,128)(2,1)} %copy-done.4) | copy-start | bytes 12582916
  86.7 2.0 %copy-start.8 = (bf16[256,8192]{1,0:T(8,128)(2,1)}, bf16[256,8192]{1,0:T(8,128)(2,1)S(1)}, u32[]{:S(2)}) copy-start(bf16[256,8192]{1,0:T(8,128)(2,1)S(1)} %get-tuple-element.27.scaled_ref) | copy-start | bytes 12582916
  92.0 2.2 %copy-start.7 = (bf16[256,8192]{1,0:T(8,128)(2,1)S(1)}, bf16[256,8192]{1,0:T(8,128)(2,1)}, u32[]{:S(2)}) copy-start(bf16[256,8192]{1,0:T(8,128)(2,1)} %copy-done.4) | copy-start | bytes 12582916
  112.4 3.0 %collective-permute-start.12 = (f32[1,1536]{1,0:T(1,128)S(1)}, f32[1,1536]{1,0:T(1,128)S(1)}, u32[]{:S(2)}, u32[]{:S(2)}) collective-permute-start(f32[1,1536]{1,0:T(1,128)S(1)} %constant_dynamic-update-slice_fusion), channel_id=1, source_target_pairs={{0,1},{1,0},{2,3},{3,2},{4,5},{5,4},{6,7},{7,6},{8,9},{9,8},{10,11... | collective-permute-start | bytes 18440 | tf_op jit(solution)/shard_map/ppermute | solution.py:373
  115.4 3.7 %collective-permute-start.13 = (f32[1,1536]{1,0:T(1,128)S(1)}, f32[1,1536]{1,0:T(1,128)S(1)}, u32[]{:S(2)}, u32[]{:S(2)}) collective-permute-start(f32[1,1536]{1,0:T(1,128)S(1)} %add.185), channel_id=1, source_target_pairs={{0,2},{1,3},{2,0},{3,1},{4,6},{5,7},{6,4},{7,5},{8,10},{9,11},{10,... | collective-permute-start | bytes 18440 | tf_op jit(solution)/shard_map/ppermute | solution.py:373
  119.1 3.7 %collective-permute-start.14 = (f32[1,1536]{1,0:T(1,128)S(1)}, f32[1,1536]{1,0:T(1,128)S(1)}, u32[]{:S(2)}, u32[]{:S(2)}) collective-permute-start(f32[1,1536]{1,0:T(1,128)S(1)} %add.186), channel_id=1, source_target_pairs={{0,4},{4,0},{8,12},{12,8},{16,20},{20,16},{24,28},{28,24},{1,5},{5... | collective-permute-start | bytes 18440 | tf_op jit(solution)/shard_map/ppermute | solution.py:370
  122.8 3.7 %collective-permute-start.15 = (f32[1,1536]{1,0:T(1,128)S(1)}, f32[1,1536]{1,0:T(1,128)S(1)}, u32[]{:S(2)}, u32[]{:S(2)}) collective-permute-start(f32[1,1536]{1,0:T(1,128)S(1)} %add.187), channel_id=1, source_target_pairs={{0,8},{4,12},{8,0},{12,4},{16,24},{20,28},{24,16},{28,20},{1,9},{5... | collective-permute-start | bytes 18440 | tf_op jit(solution)/shard_map/ppermute | solution.py:370
  127.7 23.3 %collective-permute-start.19 = (f32[136,640]{1,0:T(8,128)S(1)}, f32[136,640]{1,0:T(8,128)}, u32[]{:S(2)}, u32[]{:S(2)}) collective-permute-start(f32[136,640]{1,0:T(8,128)S(1)} %pad_maximum_fusion.2), channel_id=1, source_target_pairs={{0,2},{1,3},{2,0},{3,1},{4,6},{5,7},{6,4},{7,5},{8,10},{9,11},{10,... | collective-permute-start | bytes 1044488 | tf_op jit(solution)/shard_map/ppermute | solution.py:373
  145.8 14.1 %collective-permute-start.16 = (bf16[32,8192]{1,0:T(8,128)(2,1)S(1)}, bf16[32,8192]{1,0:T(8,128)(2,1)}, u32[]{:S(2)}, u32[]{:S(2)}) collective-permute-start(bf16[32,8192]{1,0:T(8,128)(2,1)S(1)} %get-tuple-element.30), channel_id=1, source_target_pairs={{0,4},{4,0},{8,12},{12,8},{16,20},{20,16},{24,28},{28,24},{1,5},{5... | collective-permute-start | bytes 1572872 | tf_op jit(solution)/shard_map/ppermute | solution.py:370
  147.3 15.0 %collective-permute-start.17 = (bf16[32,8192]{1,0:T(8,128)(2,1)S(1)}, bf16[32,8192]{1,0:T(8,128)(2,1)}, u32[]{:S(2)}, u32[]{:S(2)}) collective-permute-start(bf16[32,8192]{1,0:T(8,128)(2,1)S(1)} %get-tuple-element.31), channel_id=1, source_target_pairs={{0,8},{4,12},{8,0},{12,4},{16,24},{20,28},{24,16},{28,20},{1,9},{5... | collective-permute-start | bytes 1572872 | tf_op jit(solution)/shard_map/ppermute | solution.py:370
  149.3 21.5 %collective-permute-start.18 = (bf16[32,8192]{1,0:T(8,128)(2,1)S(1)}, bf16[32,8192]{1,0:T(8,128)(2,1)}, u32[]{:S(2)}, u32[]{:S(2)}) collective-permute-start(bf16[32,8192]{1,0:T(8,128)(2,1)S(1)} %get-tuple-element.32), channel_id=1, source_target_pairs={{0,12},{4,8},{8,4},{12,0},{16,28},{20,24},{24,20},{28,16},{1,13},{... | collective-permute-start | bytes 1572872 | tf_op jit(solution)/shard_map/ppermute | solution.py:370
  152.8 11.5 %collective-permute-start.20 = (f32[72,640]{1,0:T(8,128)S(1)}, f32[72,640]{1,0:T(8,128)S(1)}, u32[]{:S(2)}, u32[]{:S(2)}) collective-permute-start(f32[72,640]{1,0:T(8,128)S(1)} %pad_maximum_fusion.4), channel_id=1, source_target_pairs={{0,1},{1,0},{2,3},{3,2},{4,5},{5,4},{6,7},{7,6},{8,9},{9,8},{10,11... | collective-permute-start | bytes 552968 | tf_op jit(solution)/shard_map/ppermute | solution.py:373
  164.5 8.4 %collective-permute-start.23 = (f32[72,160]{1,0:T(8,128)S(1)}, f32[72,160]{1,0:T(8,128)S(1)}, u32[]{:S(2)}, u32[]{:S(2)}) collective-permute-start(f32[72,160]{1,0:T(8,128)S(1)} %get-tuple-element.45), channel_id=1, source_target_pairs={{0,12},{4,8},{8,4},{12,0},{16,28},{20,24},{24,20},{28,16},{1,13},{... | collective-permute-start | bytes 138248 | tf_op jit(solution)/shard_map/ppermute | solution.py:370
  167.2 5.7 %collective-permute-start.22 = (f32[72,160]{1,0:T(8,128)S(1)}, f32[72,160]{1,0:T(8,128)S(1)}, u32[]{:S(2)}, u32[]{:S(2)}) collective-permute-start(f32[72,160]{1,0:T(8,128)S(1)} %get-tuple-element.44), channel_id=1, source_target_pairs={{0,8},{4,12},{8,0},{12,4},{16,24},{20,28},{24,16},{28,20},{1,9},{5... | collective-permute-start | bytes 138248 | tf_op jit(solution)/shard_map/ppermute | solution.py:370
  167.2 5.7 %collective-permute-start.21 = (f32[72,160]{1,0:T(8,128)S(1)}, f32[72,160]{1,0:T(8,128)S(1)}, u32[]{:S(2)}, u32[]{:S(2)}) collective-permute-start(f32[72,160]{1,0:T(8,128)S(1)} %get-tuple-element.43), channel_id=1, source_target_pairs={{0,4},{4,0},{8,12},{12,8},{16,20},{20,16},{24,28},{28,24},{1,5},{5... | collective-permute-start | bytes 138248 | tf_op jit(solution)/shard_map/ppermute | solution.py:370

commit v2 on v0

v2 whole, which is shorter than its diff:
```python
import functools

import jax
import jax.numpy as jnp
from jax import lax
from jax.experimental import pallas as pl
from jax.experimental.pallas import tpu as pltpu
from jax.sharding import PartitionSpec as P

teacher_temp = 0.07
student_temp = 0.1
eps = 1e-06
LOG2E = 1.4426950408889634
GROUP = 4
CHUNKS = 8
LIMIT = 58
F32 = jnp.float32
BF16 = jnp.bfloat16
NT = (((1,), (1,)), ((), ()))


def params(mib):
    return pltpu.CompilerParams(vmem_limit_bytes=mib * 1024 * 1024)


def vmem(count):
    return [pl.BlockSpec(memory_space=pltpu.VMEM)] * count


def anywhere(count):
    return [pl.BlockSpec(memory_space=pl.ANY)] * count


def grid_one(*shapes):
    return [pl.BlockSpec(shape, lambda i, n=len(shape): (0,) * n) for shape in shapes]


SMEM = pl.BlockSpec(memory_space=pltpu.SMEM)
DMA = pltpu.SemaphoreType.DMA
AHEAD = 3


def begin(chunks, fetch):
    for i in range(min(AHEAD, chunks)):
        for copy in fetch(i):
            copy.start()


def stream(chunks, fetch, work):
    @pl.loop(0, chunks)
    def _(i):
        @pl.when(i + AHEAD < chunks)
        def _():
            for copy in fetch(i + AHEAD):
                copy.start()

        for copy in fetch(i):
            copy.wait()
        work(i)


def to_column(row):
    return jnp.broadcast_to(row, (128, row.shape[1])).T


def lane_sums(x):
    total = x[:, :128]
    for at in range(128, x.shape[1], 128):
        total = total + x[:, at : at + 128]
    return total


def to_row(acc):
    return jnp.sum(acc.T, axis=0, keepdims=True)


def pick(column, pairs):
    t, n = column.shape[0], pairs.shape[1]
    out = []
    for at in range(0, n, 128):
        width = min(128, n - at)
        which = lax.broadcasted_iota(jnp.int32, (t, width), 0)
        hit = which == pairs[:, at : at + width]
        out.append(jnp.sum(jnp.where(hit, column[:, :width], 0.0), axis=0, keepdims=True))
    return jnp.concatenate(out, axis=1)


def prepare_kernel(teach_ref, stud_ref, pairs_ref, out_ref, digits):
    t, s = teach_ref.shape[0], stud_ref.shape[0]
    for ref, at, n in ((teach_ref, 0, t), (stud_ref, t, s)):
        x = ref[...].astype(F32)
        norm = jnp.sqrt(jnp.sum(x * x, axis=1, keepdims=True) + eps)
        out_ref[at : at + n, :] = (x / norm).astype(BF16)
    pairs = pairs_ref[...]
    high = lax.shift_right_logical(pairs, 6)
    row = lax.broadcasted_iota(jnp.int32, (16, s), 0)
    digits[...] = jnp.zeros_like(digits)
    digits[:, :s] = jnp.where(row == 0, high, jnp.where(row == 1, pairs - high * 64, 0)).astype(F32)
    out_ref[t + s :, :] = digits[...].astype(BF16)


def prepare_call(teach, stud, pairs):
    t, s, d = teach.shape[0], stud.shape[0], stud.shape[1]
    return pl.pallas_call(
        prepare_kernel,
        out_shape=jax.ShapeDtypeStruct((t + s + 16, d), BF16),
        grid=(1,),
        in_specs=grid_one((t, d), (s, d), (1, s)),
        out_specs=grid_one((t + s + 16, d))[0],
        scratch_shapes=[pltpu.VMEM((16, d), F32)],
        compiler_params=params(LIMIT),
        name="prepare",
    )(teach, stud, pairs)


def unit_kernel(place, v_hbm, unit_hbm, inv_ref, v, unit, sems_in, sems_out):
    chunks, _, width = v.shape

    def fetch(i):
        start = pl.multiple_of((place[0] * chunks + i) * width, width)
        return (pltpu.make_async_copy(v_hbm.at[:, pl.ds(start, width)], v.at[i], sems_in.at[i]),)

    def store(i):
        return pltpu.make_async_copy(unit.at[i], unit_hbm.at[i], sems_out.at[i])

    begin(chunks, fetch)

    def work(i):
        x = v[i].astype(F32)
        inv = lax.rsqrt(jnp.sum(x * x, axis=0, keepdims=True) + eps)
        unit[i] = (x * inv).astype(BF16)
        inv_ref[i] = inv
        store(i).start()

    stream(chunks, fetch, work)
    for i in range(chunks):
        store(i).wait()


def unit_call(place, v, kl):
    d = v.shape[0]
    shape = (CHUNKS, d, kl // CHUNKS)
    return pl.pallas_call(
        unit_kernel,
        out_shape=(
            jax.ShapeDtypeStruct(shape, BF16),
            jax.ShapeDtypeStruct((CHUNKS, 1, kl // CHUNKS), F32),
        ),
        in_specs=[SMEM] + anywhere(1),
        out_specs=tuple(anywhere(1) + vmem(1)),
        scratch_shapes=[pltpu.VMEM(shape, BF16), pltpu.VMEM(shape, BF16), DMA((CHUNKS,)), DMA((CHUNKS,))],
        cost_estimate=pl.CostEstimate(flops=4 * d * kl, bytes_accessed=4 * d * kl, transcendentals=kl),
        compiler_params=params(LIMIT),
        name="unit",
    )(place, v)


def energy_kernel(total_k, teach_ref, unit_hbm, energy_hbm, sum_ref, unit, energy, acc, sems_in, sems_out):
    chunks = unit.shape[0]

    def fetch(i):
        return (pltpu.make_async_copy(unit_hbm.at[i], unit.at[i], sems_in.at[i]),)

    def store(i):
        return pltpu.make_async_copy(energy.at[i], energy_hbm.at[i], sems_out.at[i])

    begin(chunks, fetch)
    acc[...] = jnp.zeros_like(acc)

    def work(i):
        dots = jnp.dot(teach_ref[...], unit[i], preferred_element_type=F32)
        e = jnp.exp2(dots * (LOG2E / teacher_temp))
        energy[i] = e.astype(BF16)
        store(i).start()
        col = 1.0 / (jnp.sum(e, axis=0, keepdims=True) * total_k)
        acc[...] += lane_sums(e * col)

    stream(chunks, fetch, work)
    sum_ref[...] = to_row(acc[...])
    for i in range(chunks):
        store(i).wait()


def energy_call(teach, unit, total_k):
    t, d = teach.shape
    chunks, _, width = unit.shape
    shape = (chunks, t, width)
    return pl.pallas_call(
        functools.partial(energy_kernel, float(total_k)),
        out_shape=(jax.ShapeDtypeStruct(shape, BF16), jax.ShapeDtypeStruct((1, t), F32)),
        in_specs=vmem(1) + anywhere(1),
        out_specs=tuple(anywhere(1) + vmem(1)),
        scratch_shapes=[
            pltpu.VMEM(unit.shape, BF16), pltpu.VMEM(shape, BF16), pltpu.VMEM((t, 128), F32),
            DMA((chunks,)), DMA((chunks,)),
        ],
        cost_estimate=pl.CostEstimate(
            flops=2 * t * d * chunks * width, bytes_accessed=4 * t * chunks * width, transcendentals=0
        ),
        compiler_params=params(LIMIT),
        name="energy",
    )(teach, unit)


def iterate_kernel(total_k, last, sum_in, energy_hbm, *refs):
    if last:
        unit_hbm, denom_ref, sum_ref, mean_ref, scaled_hbm = refs[:5]
        acc, row, energy, sems_in, scaled, unit, sems_out = refs[5:]
        mean_ref[...] = jnp.zeros_like(mean_ref)
    else:
        sum_ref, acc, row, energy, sems_in = refs
    chunks, t, width = energy.shape

    def fetch(i):
        copy = pltpu.make_async_copy(energy_hbm.at[i], energy.at[i], sems_in.at[i, 0])
        if not last:
            return (copy,)
        return (copy, pltpu.make_async_copy(unit_hbm.at[i], unit.at[i], sems_in.at[i, 1]))

    def store(i):
        return pltpu.make_async_copy(scaled.at[i], scaled_hbm.at[i], sems_out.at[i])

    begin(chunks, fetch)
    row[...] = to_column(1.0 / (sum_in[...] * float(t)))
    acc[...] = jnp.zeros_like(acc)

    def work(i):
        scale = row[...]
        col = []
        for at in range(0, width, 128):
            mass = jnp.sum(energy[i, :, at : at + 128].astype(F32) * scale, axis=0, keepdims=True)
            col.append(1.0 / (mass * total_k))
        part = None
        for n, at in enumerate(range(0, width, 128)):
            x = energy[i, :, at : at + 128].astype(F32) * col[n]
            if last:
                scaled[i, :, at : at + 128] = x.astype(BF16)
            part = x if part is None else part + x
        acc[...] += part
        if last:
            store(i).start()
            mean_ref[...] += lax.dot_general(unit[i], scaled[i], NT, preferred_element_type=F32)

    stream(chunks, fetch, work)
    sum_ref[:, :t] = to_row(acc[...])
    if last:
        sum_ref[:, t:] = denom_ref[...]
        for i in range(chunks):
            store(i).wait()


def iterate_call(sums, energy, total_k, more=()):
    chunks, t, width = energy.shape
    last = bool(more)
    out_shape = [jax.ShapeDtypeStruct((1, t), F32)]
    in_specs, out_specs = vmem(1) + anywhere(1), vmem(1)
    scratch = [
        pltpu.VMEM((t, 128), F32), pltpu.VMEM((t, 128), F32), pltpu.VMEM(energy.shape, BF16), DMA((chunks, 2))
    ]
    if last:
        unit, denom = more
        d = unit.shape[1]
        out_shape = [
            jax.ShapeDtypeStruct((1, t + denom.shape[1]), F32),
            jax.ShapeDtypeStruct((d, t), F32),
            jax.ShapeDtypeStruct(energy.shape, BF16),
        ]
        in_specs, out_specs = in_specs + anywhere(1) + vmem(1), vmem(2) + anywhere(1)
        scratch += [pltpu.VMEM(energy.shape, BF16), pltpu.VMEM(unit.shape, BF16), DMA((chunks,))]
    return pl.pallas_call(
        functools.partial(iterate_kernel, float(total_k), last),
        out_shape=out_shape,
        in_specs=in_specs,
        out_specs=out_specs,
        scratch_shapes=scratch,
        cost_estimate=pl.CostEstimate(
            flops=4 * t * chunks * width, bytes_accessed=4 * t * chunks * width, transcendentals=0
        ),
        compiler_params=params(LIMIT),
        name="iterate_last" if last else "iterate",
    )(sums, energy, *more)


def student_kernel(place, rest_ref, pairs_ref, unit_hbm, expo_hbm, denom_ref, pull_ref, stud_t_hbm, weight_hbm,
                   unit, expo, acc, pull, stud, stud_t, weight, sems_in, sems_out, sems):
    chunks, s, width = expo.shape
    s_dev = s // rest_ref.shape[0]
    n = pull.shape[0]
    t = weight.shape[1]
    start = pl.multiple_of(place[1] * n, 128)

    def fetch(i):
        return (pltpu.make_async_copy(unit_hbm.at[i], unit.at[i], sems_in.at[i]),)

    def store(i):
        return pltpu.make_async_copy(expo.at[i], expo_hbm.at[i], sems_out.at[i])

    begin(chunks, fetch)
    acc[...] = jnp.zeros_like(acc)
    pull[...] = jnp.zeros_like(pull)
    for i in range(rest_ref.shape[0]):
        stud[i * s_dev : (i + 1) * s_dev, :] = rest_ref[i, :s_dev, :]
    rows_t = stud[...].astype(F32).T.astype(BF16)
    stud_t[...] = rows_t
    which = lax.broadcasted_iota(jnp.int32, (t, s), 0)
    onehot = (which == pairs_ref[...]).astype(F32).astype(BF16)
    weight[...] = lax.dot_general(rows_t, onehot, NT, preferred_element_type=F32)
    extra = (
        pltpu.make_async_copy(stud_t, stud_t_hbm, sems.at[0]),
        pltpu.make_async_copy(weight, weight_hbm, sems.at[1]),
    )
    for copy in extra:
        copy.start()

    def work(i):
        for at in range(0, s, 256):
            logits = jnp.dot(stud[at : at + 256, :], unit[i], preferred_element_type=F32)
            x = jnp.exp2(logits * (LOG2E / student_temp))
            expo[i, at : at + 256, :] = x.astype(BF16)
            acc[at : at + 256, :] += lane_sums(x)
        store(i).start()
        pull[...] += lax.dot_general(expo[i, pl.ds(start, n), :], unit[i], NT, preferred_element_type=F32)

    stream(chunks, fetch, work)
    denom_ref[...] = to_row(acc[...])
    pull_ref[...] = pull[...].T
    for copy in extra:
        copy.wait()
    for i in range(chunks):
        store(i).wait()


def student_call(place, rest, pairs, unit, t, n):
    chunks, d, width = unit.shape
    s = rest.shape[0] * (rest.shape[1] - 16)
    shape = (chunks, s, width)
    return pl.pallas_call(
        student_kernel,
        out_shape=(
            jax.ShapeDtypeStruct(shape, BF16),
            jax.ShapeDtypeStruct((1, s), F32),
            jax.ShapeDtypeStruct((d, n), F32),
            jax.ShapeDtypeStruct((d, s), BF16),
            jax.ShapeDtypeStruct((d, t), F32),
        ),
        in_specs=[SMEM] + vmem(2) + anywhere(1),
        out_specs=tuple(anywhere(1) + vmem(2) + anywhere(2)),
        scratch_shapes=[
            pltpu.VMEM(unit.shape, BF16), pltpu.VMEM(shape, BF16), pltpu.VMEM((s, 128), F32),
            pltpu.VMEM((n, d), F32), pltpu.VMEM((s, d), BF16), pltpu.VMEM((d, s), BF16), pltpu.VMEM((d, t), F32),
            DMA((chunks,)), DMA((chunks,)), DMA((2,)),
        ],
        cost_estimate=pl.CostEstimate(
            flops=4 * s * d * chunks * width, bytes_accessed=2 * s * chunks * width, transcendentals=0
        ),
        compiler_params=params(LIMIT),
        name="student",
    )(place, rest, pairs, unit)


def head_kernel(factor, place, both_ref, pairs_ref, stud_t_ref, weight_ref, inv_ref, expo_hbm,
                scaled_hbm, v_hbm, own_hbm, *refs):
    sends, refs = refs[: GROUP - 1], refs[GROUP - 1 :]
    lhs, lhs_teach, grad, expo, scaled, v, own, sems_in, sems_out = refs
    chunks, t, width = scaled.shape
    rows = own.shape[1]

    def start_of(i):
        return pl.multiple_of((place[0] * chunks + i) * width, width)

    def fetches(i):
        return (
            pltpu.make_async_copy(expo_hbm.at[i], expo.at[i], sems_in.at[i, 0]),
            pltpu.make_async_copy(scaled_hbm.at[i], scaled.at[i], sems_in.at[i, 1]),
            pltpu.make_async_copy(v_hbm.at[:, pl.ds(start_of(i), width)], v.at[i], sems_in.at[i, 2]),
        )

    def store(i):
        return pltpu.make_async_copy(own.at[i], own_hbm.at[:, pl.ds(start_of(i), width)], sems_out.at[i])

    begin(chunks, fetches)
    sums, denom = both_ref[:, :t], both_ref[:, t:]
    row = 1.0 / (sums * float(t))
    mass = pick(to_column(row * sums * float(t)), pairs_ref[...])
    lhs[...] = (stud_t_ref[...].astype(F32) * (mass / denom * factor)).astype(BF16)
    lhs_teach[...] = (weight_ref[...] * (row * (-factor * t))).astype(BF16)
    base = place[1] * (rows * GROUP)

    def part(n):
        start = pl.multiple_of(base + (place[0] ^ n) * rows, rows)
        return grad[pl.ds(start, rows), :]

    def work(i):
        head = jnp.dot(lhs[...], expo[i], preferred_element_type=F32)
        head = head + jnp.dot(lhs_teach[...], scaled[i], preferred_element_type=F32)
        inv = inv_ref[i]
        unit = v[i].astype(F32) * inv
        proj = jnp.sum(unit * head, axis=0, keepdims=True)
        grad[...] = (head - unit * proj) * inv
        own[i] = part(0)
        store(i).start()
        at = pl.ds(pl.multiple_of(i * width, width), width)
        for n, ref in enumerate(sends):
            ref[:, at] = part(n + 1).astype(BF16)

    stream(chunks, fetches, work)
    for i in range(chunks):
        store(i).wait()


def head_call(place, both, pairs, stud_t, weight, inv, expo, scaled, v, factor, rows):
    d, s = stud_t.shape
    chunks, t, width = scaled.shape
    kl = chunks * width
    return pl.pallas_call(
        functools.partial(head_kernel, factor),
        out_shape=[jax.ShapeDtypeStruct((rows, v.shape[1]), F32)]
        + [jax.ShapeDtypeStruct((rows, kl), BF16)] * (GROUP - 1),
        in_specs=[SMEM] + vmem(5) + anywhere(3),
        out_specs=anywhere(1) + vmem(GROUP - 1),
        scratch_shapes=[
            pltpu.VMEM((d, s), BF16), pltpu.VMEM((d, t), BF16), pltpu.VMEM((d, width), F32),
            pltpu.VMEM(expo.shape, BF16), pltpu.VMEM(scaled.shape, BF16), pltpu.VMEM((chunks, d, width), BF16),
            pltpu.VMEM((chunks, rows, width), F32), DMA((chunks, 3)), DMA((chunks,)),
        ],
        cost_estimate=pl.CostEstimate(
            flops=4 * (s + t) * d * kl, bytes_accessed=2 * (s + t + d) * kl, transcendentals=0
        ),
        compiler_params=params(LIMIT),
        name="head",
    )(place, both, pairs, stud_t, weight, inv, expo, scaled, v)


def back_kernel(factor, place, both_ref, pairs_ref, stud_t_ref, pull_ref, mean_ref, back_ref):
    d, n = pull_ref.shape
    t = mean_ref.shape[1]
    start = pl.multiple_of(place[1] * n, 128)
    mine = pl.ds(start, n)
    sums = both_ref[:, :t]
    denom = both_ref[:, pl.ds(pl.multiple_of(t + place[1] * n, 128), n)]
    row = 1.0 / (sums * float(t))
    pairs = pairs_ref[:, mine]
    mass = pick(to_column(row * sums * float(t)), pairs)
    which = lax.broadcasted_iota(jnp.int32, (t, n), 0)
    onehot = (which == pairs).astype(F32)
    target = jnp.dot(
        mean_ref[...] * (row * t), onehot, preferred_element_type=F32, precision=lax.Precision.HIGHEST
    )
    stud_t = stud_t_ref[:, mine].astype(F32)
    back = (pull_ref[...] * (mass / denom) - target) * factor
    back_ref[:d, :] = back
    along = jnp.sum(stud_t * back, axis=0, keepdims=True)
    cross = jnp.sum(stud_t * target, axis=0, keepdims=True) * (1.0 / student_temp)
    at = lax.broadcasted_iota(jnp.int32, (8, n), 0)
    back_ref[d:, :] = jnp.where(at == 0, along, jnp.where(at == 1, cross, 0.0))


def back_call(place, both, pairs, stud_t, pull, mean, factor):
    d, n = pull.shape
    return pl.pallas_call(
        functools.partial(back_kernel, factor),
        out_shape=jax.ShapeDtypeStruct((d + 8, n), F32),
        in_specs=[SMEM] + vmem(5),
        out_specs=vmem(1)[0],
        cost_estimate=pl.CostEstimate(flops=12 * d * n * mean.shape[1], bytes_accessed=12 * d * n, transcendentals=0),
        compiler_params=params(LIMIT),
        name="back",
    )(place, both, pairs, stud_t, pull, mean)


def finish_kernel(t, place, both_ref, denom_ref, pairs_ref, stud_ref, *refs):
    terms, (grad_ref, loss_ref, unit) = refs[:GROUP], refs[GROUP:]
    total = (terms[0][...] + terms[1][...]) + (terms[2][...] + terms[3][...])
    share = grad_ref.shape[0]
    x = stud_ref[...].astype(F32).T
    norm = jnp.sqrt(jnp.sum(x * x, axis=0, keepdims=True) + eps)
    unit[...] = x / norm
    part = unit[pl.ds(pl.multiple_of(place[2] * share, share), share), :]
    along, cross = total[share : share + 1, :], total[share + 1 : share + 2, :]
    grad_ref[...] = (total[:share, :] - part * along) / norm
    sums = both_ref[:, :t]
    mass = pick(to_column(1.0 / (sums * float(t)) * sums * float(t)), pairs_ref[...])
    loss_ref[...] = jnp.log(denom_ref[...]) * mass - cross


def finish_call(t, place, both, denom, pairs, stud, terms, share):
    s, d = stud.shape
    return pl.pallas_call(
        functools.partial(finish_kernel, t),
        out_shape=(jax.ShapeDtypeStruct((share, s), F32), jax.ShapeDtypeStruct((1, s), F32)),
        in_specs=[SMEM] + vmem(4 + GROUP),
        out_specs=tuple(vmem(2)),
        scratch_shapes=[pltpu.VMEM((d, s), F32)],
        compiler_params=params(8),
        name="finish",
    )(place, both, denom, pairs, stud, *terms)


def body(teacher_features, student_features, v, pairing):
    n_rows, n_proto = lax.axis_size("rows"), lax.axis_size("proto")
    r, p = lax.axis_index("rows"), lax.axis_index("proto")
    d, local_k = v.shape
    total_k = local_k * n_proto
    kl = local_k // GROUP
    t_dev, s_dev = teacher_features.shape[0], student_features.shape[0]
    t, s = t_dev * n_rows, s_dev * n_rows
    at, group = r % GROUP, r // GROUP
    place = jnp.stack([at, group, p]).astype(jnp.int32)
    factor = total_k / 64.0 / student_temp

    def swap_rows(x, n):
        return lax.ppermute(x, "rows", [(j, j ^ n) for j in range(n_rows)])

    def swap_proto(x, n):
        return lax.ppermute(x, "proto", [(j, j ^ n) for j in range(n_proto)])

    def total(x):
        for swap, size in ((swap_proto, n_proto), (swap_rows, GROUP)):
            n = 1
            while n < size:
                x = (x + swap(x, n)) + (swap(x, 2 * n) + swap(x, 3 * n))
                n *= 4
        return x

    def join(x, n, other=None):
        other = swap_rows(x, n) if other is None else other
        low = (r // n) % 2 == 0
        return jnp.concatenate([jnp.where(low, x, other), jnp.where(low, other, x)], axis=0)

    own_pairs = pairing.reshape(1, s_dev)
    unit, inv = unit_call(place, v, kl)
    packed = prepare_call(teacher_features, student_features, own_pairs)[None]
    packed = join(packed, 1)
    other, unit, inv = lax.optimization_barrier((swap_rows(packed, 2), unit, inv))
    packed = join(packed, 2, other)
    teach_all, rest = packed[:, :t_dev], packed[:, t_dev:]
    n = GROUP
    while n < n_rows:
        teach_all = join(teach_all, n)
        rest = join(rest, n)
        n *= 2
    teach_all = teach_all.reshape(t, d)
    digits = rest[:, s_dev : s_dev + 2, :s_dev].astype(F32)
    pairs = (digits[:, 0] * 64.0 + digits[:, 1]).astype(jnp.int32).reshape(1, s)

    energy, sums = energy_call(teach_all, unit, total_k)
    expo, denom, pull, stud_t, weight = student_call(place, rest, pairs, unit, t, s_dev * GROUP)
    (sums,) = iterate_call(total(sums), energy, total_k)
    both, mean, scaled = iterate_call(total(sums), energy, total_k, (unit, denom))
    both = total(both)

    rows = d // n_rows
    grads = head_call(place, both, pairs, stud_t, weight, inv, expo, scaled, v, factor, rows)
    proto_grad = grads[0]
    for n in range(1, GROUP):
        got = swap_rows(grads[n], n).astype(F32)
        proto_grad = lax.dynamic_update_slice(proto_grad, got, (0, (at ^ n) * kl))

    back = back_call(place, both, pairs, stud_t, pull, mean, factor)
    body_rows, tail = back[:d], back[d:]
    n = n_proto // 2
    while n >= 1:
        height = body_rows.shape[0] // 2
        bit = (p // n) % 2
        keep = lax.dynamic_slice_in_dim(body_rows, bit * height, height, 0)
        send = lax.dynamic_slice_in_dim(body_rows, (1 - bit) * height, height, 0)
        got = swap_proto(jnp.concatenate([send, tail], axis=0), n)
        body_rows, tail = keep + got[:height], tail + got[height:]
        n //= 2
    terms = jnp.concatenate([body_rows, tail], axis=0)

    def block(n):
        return lax.dynamic_slice_in_dim(terms, (at ^ n) * s_dev, s_dev, 1)

    parts = [block(0)] + [swap_rows(block(n), n) for n in range(1, GROUP)]
    own = lax.dynamic_slice_in_dim(both, t + r * s_dev, s_dev, 1)
    student_grad, loss = finish_call(t, place, both, own, own_pairs, student_features, parts, d // n_proto)
    return (proto_grad, student_grad.T, loss.reshape(s_dev))


def solution(mesh):
    return jax.shard_map(
        body,
        mesh=mesh,
        in_specs=(P("rows", None), P("rows", None), P(None, "proto"), P("rows")),
        out_specs=(P("rows", "proto"), P("rows", "proto"), P("rows")),
        check_vma=False,
    )
```

time: 965 us -> 158 us (0.16)
  waiting for transfers between devices: 708 us -> 44.1 us
  matrix products: 75.1 us -> 0 us
  blocking collectives: 73 us -> 0 us
  other arithmetic: 80.2 us -> 11.3 us
  Pallas kernels: 0 us -> 62.8 us
  starting transfers between devices: 0.21 us -> 35.3 us
  between operations: 14.6 us -> 0.87 us
  local copies, waits for them, and re-layouts: 13.2 us -> 2.67 us
    reduce_scatter x1 -> x0, waiting for transfers between devices: 544 us -> none  [body(): proto_grad = lax.psum_scatter(term, 'rows', scatter_dimension=0, tiled=True)]
    psum x4 -> x0, waiting for transfers between devices: 163 us -> none  [the longest x3 163 us: body(): lax.psum(jnp.sum(energy * row_scale[:, None], axis=0), 'rows')]
    dot_general x5 -> x0, matrix products: 75.1 us -> none  [the longest x1 22.8 us: body(): lax.dot_general(stud_unit_b, dlogit, (((0,), (0,)), ((), ())), preferred_...]
    pallas_call x0 -> x9, Pallas kernels: none -> 62.8 us  [the longest x1 15.1 us: head_call(): pl.pallas_call(functools.partial(head_kernel, factor), out_shape=[jax.Sha...]
    ppermute x0 -> x30, waiting for transfers between devices: none -> 44.1 us  [the longest x19 38.9 us: swap_rows(): return lax.ppermute(x, 'rows', [(j, j ^ n) for j in range(n_rows)])]
    ppermute x0 -> x30, starting transfers between devices: none -> 35.3 us  [the longest x19 27.6 us: swap_rows(): return lax.ppermute(x, 'rows', [(j, j ^ n) for j in range(n_rows)])]
    div x7 -> x0, other arithmetic: 32.1 us -> none  [the longest x1 28 us: body(): term = (head - unit * proj[None, :]) / vnorm[None, :]]
    all_gather x1 -> x0, blocking collectives: 30.5 us -> none  [body(): teach_all = lax.all_gather(teach_unit, 'rows', axis=0, tiled=True)]
  transfers between devices with their start and end apart: 5 -> 30, of which waited for: 5 -> 18; matrix products, arithmetic and copies ran while one was open for 5% -> 4% of each run, Pallas kernels for 0% -> 13%
where the time goes in v2:
time: 158 us; the launch traced here: 157 us
  Pallas kernels  62.8 us (40%)
  waiting for transfers between devices  44.1 us (28%)
  starting transfers between devices  35.3 us (22%)
  other arithmetic  11.3 us (7%)
  local copies, waits for them, and re-layouts  2.67 us (2%)
    ppermute x19, waiting for transfers between devices, swap_rows(): return lax.ppermute(x, 'rows', [(j, j ^ n) for j in range(n_rows)])  38.9 us
    ppermute x19, starting transfers between devices, swap_rows(): return lax.ppermute(x, 'rows', [(j, j ^ n) for j in range(n_rows)])  27.6 us
    pallas_call x1, Pallas kernels, head_call(): pl.pallas_call(functools.partial(head_kernel, factor), out_shape=[jax.Sha...  15.1 us
    pallas_call x1, Pallas kernels, student_call(): pl.pallas_call(student_kernel, out_shape=(jax.ShapeDtypeStruct(shape, BF1...  15 us
    pallas_call x2, Pallas kernels, iterate_call(): pl.pallas_call(functools.partial(iterate_kernel, float(total_k), last), o...  13.5 us
    ppermute x11, starting transfers between devices, swap_proto(): return lax.ppermute(x, 'proto', [(j, j ^ n) for j in range(n_proto)])  7.67 us
    pallas_call x1, Pallas kernels, energy_call(): pl.pallas_call(functools.partial(energy_kernel, float(total_k)), out_shap...  6.89 us
    pallas_call x1, Pallas kernels, unit_call(): pl.pallas_call(unit_kernel, out_shape=(jax.ShapeDtypeStruct(shape, BF16),...  6.04 us
  transfers between devices with their start and end apart: 30, of which 18 were waited for; matrix products, arithmetic and copies ran while one was open for 4% of the time, Pallas kernels for 13%

profile of v2, /device:TPU:0, one launch (start us, length us, event | category | flops | bytes accessed | tf_op | source)
XLA Modules:
  0.0 157.0 jit_solution(17521748121576586940)
XLA Ops:
  0.6 1.7 %prepare.1 = bf16[208,256]{1,0:T(8,128)(2,1)} custom-call(bf16[32,256]{1,0:T(8,128)(2,1)} %teach_ref.1, bf16[160,256]{1,0:T(8,128)(2,1)} %stud_ref.3, s32[1,160]{1,0:T(1,128)} %bitcast.10), custom_call_target="tpu_custom_call" | custom-call | tf_op jit(solution)/shard_map/prepare/pallas_call | solution.py:104
  2.3 2.9 %collective-permute-start = (bf16[1,208,256]{2,1,0:T(8,128)(2,1)}, bf16[1,208,256]{2,1,0:T(8,128)(2,1)S(1)}, u32[]{:S(2)}, u32[]{:S(2)}) collective-permute-start(bf16[1,208,256]{2,1,0:T(8,128)(2,1)} %bitcast.13), channel_id=1, source_target_pairs={{0,4},{4,0},{8,12},{12,8},{16,20},{20,16},{24,28},{28,24},{1,5},{5... | collective-permute-start | bytes 319496 | tf_op jit(solution)/shard_map/ppermute | solution.py:512
  5.2 3.2 %collective-permute-done = bf16[1,208,256]{2,1,0:T(8,128)(2,1)S(1)} collective-permute-done((bf16[1,208,256]{2,1,0:T(8,128)(2,1)}, bf16[1,208,256]{2,1,0:T(8,128)(2,1)S(1)}, u32[]{:S(2)}, u32[]{:S(2)}) %collective-permute-start) | collective-permute-done | bytes 106528 | tf_op jit(solution)/shard_map/ppermute | solution.py:512
  8.4 0.9 broadcast_select_fusion.5
  9.4 1.9 %collective-permute-start.1 = (bf16[2,208,256]{2,1,0:T(8,128)(2,1)S(1)}, bf16[2,208,256]{2,1,0:T(8,128)(2,1)S(1)}, u32[]{:S(2)}, u32[]{:S(2)}) collective-permute-start(bf16[2,208,256]{2,1,0:T(8,128)(2,1)S(1)} %pad_maximum_fusion.3), channel_id=1, source_target_pairs={{0,8},{4,12},{8,0},{12,4},{16,24},{20,28},{24,16},{28,20},{1,9},{5... | collective-permute-start | bytes 638984 | tf_op jit(solution)/shard_map/ppermute | solution.py:512
  11.2 0.6 pad_add_fusion.place
  11.9 6.0 %unit.1 = (bf16[8,256,1024]{2,1,0:T(8,128)(2,1)}, f32[8,1,1024]{2,1,0:T(1,128)}) custom-call(s32[3]{0:T(128)} %pad_add_fusion.place, bf16[256,32768]{1,0:T(8,128)(2,1)} %v_hbm.3), custom_call_target="tpu_custom_call" | custom-call | flops 8388608 | bytes 8388608 | tf_op jit(solution)/shard_map/unit/pallas_call | solution.py:143
  18.0 2.7 %collective-permute-start.2 = (bf16[4,32,256]{2,1,0:T(8,128)(2,1)S(1)}, bf16[4,32,256]{2,1,0:T(8,128)(2,1)S(1)}, u32[]{:S(2)}, u32[]{:S(2)}) collective-permute-start(bf16[4,32,256]{2,1,0:T(8,128)(2,1)S(1)} %pad_maximum_fusion.6), channel_id=1, source_target_pairs={{0,16},{4,20},{8,24},{12,28},{16,0},{20,4},{24,8},{28,12},{1,17},{... | collective-permute-start | bytes 196616 | tf_op jit(solution)/shard_map/ppermute | solution.py:512
  20.6 2.9 %collective-permute-done.2 = bf16[4,32,256]{2,1,0:T(8,128)(2,1)S(1)} collective-permute-done((bf16[4,32,256]{2,1,0:T(8,128)(2,1)S(1)}, bf16[4,32,256]{2,1,0:T(8,128)(2,1)S(1)}, u32[]{:S(2)}, u32[]{:S(2)}) %collective-permute-start.2) | collective-permute-done | bytes 65568 | tf_op jit(solution)/shard_map/ppermute | solution.py:512
  23.6 0.7 pad_maximum_fusion.5
  24.2 6.9 %energy.1 = (bf16[8,256,1024]{2,1,0:T(8,128)(2,1)}, f32[1,256]{1,0:T(1,128)}) custom-call(bf16[256,256]{1,0:T(8,128)(2,1)} %bitcast.12, bf16[8,256,1024]{2,1,0:T(8,128)(2,1)} %get-tuple-element.27.unit_hbm.refs_0_), custom_call_target="tpu_custom_call" | custom-call | flops 1073741824 | bytes 8388608 | tf_op jit(solution)/shard_map/energy/pallas_call | solution.py:188
  31.2 1.8 %collective-permute-start.4 = (f32[1,256]{1,0:T(1,128)}, f32[1,256]{1,0:T(1,128)S(1)}, u32[]{:S(2)}, u32[]{:S(2)}) collective-permute-start(f32[1,256]{1,0:T(1,128)} %get-tuple-element.28), channel_id=1, source_target_pairs={{0,2},{1,3},{2,0},{3,1},{4,6},{5,7},{6,4},{7,5},{8,10},{9,11},{10,... | collective-permute-start | bytes 3080 | tf_op jit(solution)/shard_map/ppermute | solution.py:515
  33.1 1.9 %collective-permute-done.4 = f32[1,256]{1,0:T(1,128)S(1)} collective-permute-done((f32[1,256]{1,0:T(1,128)}, f32[1,256]{1,0:T(1,128)S(1)}, u32[]{:S(2)}, u32[]{:S(2)}) %collective-permute-start.4) | collective-permute-done | bytes 1056 | tf_op jit(solution)/shard_map/ppermute | solution.py:515
  35.1 1.2 collective-permute-done.5
  36.3 0.7 add_add_fusion.5
  36.9 1.5 collective-permute-start.6
  38.4 2.0 %collective-permute-start.8 = (f32[1,256]{1,0:T(1,128)S(1)}, f32[1,256]{1,0:T(1,128)S(1)}, u32[]{:S(2)}, u32[]{:S(2)}) collective-permute-start(f32[1,256]{1,0:T(1,128)S(1)} %add_add_fusion.5), channel_id=1, source_target_pairs={{0,12},{4,8},{8,4},{12,0},{16,28},{20,24},{24,20},{28,16},{1,13},{... | collective-permute-start | bytes 3080 | tf_op jit(solution)/shard_map/ppermute | solution.py:512
  40.5 1.5 collective-permute-done.7
  42.0 0.9 collective-permute-done.8
  42.9 0.6 add_add_fusion.4.sum_in
  43.5 5.0 %iterate.1 = f32[1,256]{1,0:T(1,128)} custom-call(f32[1,256]{1,0:T(1,128)} %add_add_fusion.4.sum_in, bf16[8,256,1024]{2,1,0:T(8,128)(2,1)} %get-tuple-element.29.energy_hbm), custom_call_target="tpu_custom_call" | custom-call | flops 8388608 | bytes 8388608 | tf_op jit(solution)/shard_map/iterate/pallas_call | solution.py:270
  48.5 0.6 collective-permute-start.10
  49.1 1.6 collective-permute-start.9
  50.7 2.5 %collective-permute-start.15 = (bf16[4,176,256]{2,1,0:T(8,128)(2,1)S(1)}, bf16[4,176,256]{2,1,0:T(8,128)(2,1)S(1)}, u32[]{:S(2)}, u32[]{:S(2)}) collective-permute-start(bf16[4,176,256]{2,1,0:T(8,128)(2,1)S(1)} %pad_maximum_fusion.1), channel_id=1, source_target_pairs={{0,16},{4,20},{8,24},{12,28},{16,0},{20,4},{24,8},{28,12},{1,17},{... | collective-permute-start | bytes 1081352 | tf_op jit(solution)/shard_map/ppermute | solution.py:512
  53.2 0.6 add_add_fusion.3
  53.9 0.5 collective-permute-start.12
  54.4 1.6 %collective-permute-start.13 = (f32[1,256]{1,0:T(1,128)S(1)}, f32[1,256]{1,0:T(1,128)S(1)}, u32[]{:S(2)}, u32[]{:S(2)}) collective-permute-start(f32[1,256]{1,0:T(1,128)S(1)} %add_add_fusion.3), channel_id=1, source_target_pairs={{0,8},{4,12},{8,0},{12,4},{16,24},{20,28},{24,16},{28,20},{1,9},{5... | collective-permute-start | bytes 3080 | tf_op jit(solution)/shard_map/ppermute | solution.py:512
  56.0 1.4 collective-permute-start.14
  57.4 3.7 %collective-permute-done.13 = f32[1,256]{1,0:T(1,128)S(1)} collective-permute-done((f32[1,256]{1,0:T(1,128)S(1)}, f32[1,256]{1,0:T(1,128)S(1)}, u32[]{:S(2)}, u32[]{:S(2)}) %collective-permute-start.13) | collective-permute-done | bytes 1056 | tf_op jit(solution)/shard_map/ppermute | solution.py:512
  61.2 0.6 add_add_fusion.2.sum_in
  61.7 8.0 %collective-permute-done.15 = bf16[4,176,256]{2,1,0:T(8,128)(2,1)S(1)} collective-permute-done((bf16[4,176,256]{2,1,0:T(8,128)(2,1)S(1)}, bf16[4,176,256]{2,1,0:T(8,128)(2,1)S(1)}, u32[]{:S(2)}, u32[]{:S(2)}) %collective-permute-start.15) | collective-permute-done | bytes 360480 | tf_op jit(solution)/shard_map/ppermute | solution.py:512
  69.8 1.0 pad_maximum_fusion.rest_ref
  70.8 0.7 convert_element_type.27.pairs_ref
  71.5 15.0 %student.1 = (bf16[8,1280,1024]{2,1,0:T(8,128)(2,1)}, f32[1,1280]{1,0:T(1,128)}, f32[256,640]{1,0:T(8,128)}, bf16[256,1280]{1,0:T(8,128)(2,1)}, f32[256,256]{1,0:T(8,128)}) custom-call(s32[3]{0:T(128)} %pad_add_fusion.place, bf16[8,176,256]{2,1,0:T(8,128)(2,1)} %pad_maximum_fusion.rest_ref, s32[1,1280]{1,0:T(1,128)} %convert_element_type.27.pairs_ref, ...), custom_call_target="tpu_custom_call" | custom-call | flops 10737418240 | bytes 20971520 | tf_op jit(solution)/shard_map/student/pallas_call | solution.py:337
  86.4 8.5 %iterate_last.1 = (f32[1,1536]{1,0:T(1,128)}, f32[256,256]{1,0:T(8,128)}, bf16[8,256,1024]{2,1,0:T(8,128)(2,1)}) custom-call(f32[1,256]{1,0:T(1,128)} %add_add_fusion.2.sum_in, bf16[8,256,1024]{2,1,0:T(8,128)(2,1)} %get-tuple-element.29.energy_hbm, bf16[8,256,1024]{2,1,0:T(8,128)(2,1)} %get-tuple-element.27.unit_hbm.refs_0_, f32[1,1280]{1,0:T(1,128)} %get-tuple-element.30.refs_1_), custom_call_target="tpu_custom_call" | custom-call | flops 8388608 | bytes 8388608 | tf_op jit(solution)/shard_map/iterate_last/pallas_call | solution.py:270
  95.0 0.6 collective-permute-start.17
  95.7 1.2 collective-permute-start.18
  96.9 2.1 %collective-permute-done.17 = f32[1,1536]{1,0:T(1,128)S(1)} collective-permute-done((f32[1,1536]{1,0:T(1,128)}, f32[1,1536]{1,0:T(1,128)S(1)}, u32[]{:S(2)}, u32[]{:S(2)}) %collective-permute-start.17) | collective-permute-done | bytes 6176 | tf_op jit(solution)/shard_map/ppermute | solution.py:515
  99.0 0.7 add_add_fusion.1
  99.7 0.7 collective-permute-start.19
  100.8 2.4 %collective-permute-start.21 = (f32[1,1536]{1,0:T(1,128)S(1)}, f32[1,1536]{1,0:T(1,128)S(1)}, u32[]{:S(2)}, u32[]{:S(2)}) collective-permute-start(f32[1,1536]{1,0:T(1,128)S(1)} %add_add_fusion.1), channel_id=1, source_target_pairs={{0,12},{4,8},{8,4},{12,0},{16,28},{20,24},{24,20},{28,16},{1,13},{... | collective-permute-start | bytes 18440 | tf_op jit(solution)/shard_map/ppermute | solution.py:512
  103.4 0.6 collective-permute-done.20
  104.0 1.3 collective-permute-done.21
  105.3 0.6 add_add_fusion.both_ref
  106.0 3.2 %back.1 = f32[264,640]{1,0:T(8,128)} custom-call(s32[3]{0:T(128)} %pad_add_fusion.place, f32[1,1536]{1,0:T(1,128)} %add_add_fusion.both_ref, s32[1,1280]{1,0:T(1,128)} %convert_element_type.27.pairs_ref, bf16[256,1280]{1,0:T(8,128)(2,1)} %get-tuple-element.32.stud_t_ref, f32[256,640]{1,0:T(8,128)} %get-tuple-element.41.pull_ref, ...), custom_call_target="tpu_custom_call" | custom-call | flops 503316480 | bytes 1966080 | tf_op jit(solution)/shard_map/back/pallas_call | solution.py:460
  109.2 1.1 slice.48
  110.3 0.7 slice.49
  111.1 1.5 collective-permute-start.25
  112.6 15.1 %head.1 = (f32[32,32768]{1,0:T(8,128)}, bf16[32,8192]{1,0:T(8,128)(2,1)}, bf16[32,8192]{1,0:T(8,128)(2,1)}, bf16[32,8192]{1,0:T(8,128)(2,1)}) custom-call(s32[3]{0:T(128)} %pad_add_fusion.place, f32[1,1536]{1,0:T(1,128)} %add_add_fusion.both_ref, s32[1,1280]{1,0:T(1,128)} %convert_element_type.27.pairs_ref, bf16[256,1280]{1,0:T(8,128)(2,1)} %get-tuple-element.32.stud_t_ref, ...), custom_call_target="tpu_custom_call" | custom-call | flops 12884901888 | bytes 29360128 | tf_op jit(solution)/shard_map/head/pallas_call | solution.py:415
  127.8 1.6 collective-permute-start.22
  129.3 1.5 collective-permute-start.23
  130.8 0.5 collective-permute-start.24
  131.5 0.7 slice_add_fusion.3
  132.3 9.7 %collective-permute-done.22 = bf16[32,8192]{1,0:T(8,128)(2,1)S(1)} collective-permute-done((bf16[32,8192]{1,0:T(8,128)(2,1)}, bf16[32,8192]{1,0:T(8,128)(2,1)S(1)}, u32[]{:S(2)}, u32[]{:S(2)}) %collective-permute-start.22) | collective-permute-done | bytes 524320 | tf_op jit(solution)/shard_map/ppermute | solution.py:512
  142.0 1.0 convert_dynamic-update-slice_fusion.2
  143.0 1.4 collective-permute-done.23
  144.4 1.0 convert_dynamic-update-slice_fusion.1
  145.7 0.6 collective-permute-start.27
  146.3 1.5 collective-permute-start.28
  147.8 1.4 collective-permute-start.29
  149.2 4.9 %collective-permute-done.24 = bf16[32,8192]{1,0:T(8,128)(2,1)S(1)} collective-permute-done((bf16[32,8192]{1,0:T(8,128)(2,1)}, bf16[32,8192]{1,0:T(8,128)(2,1)S(1)}, u32[]{:S(2)}, u32[]{:S(2)}) %collective-permute-start.24) | collective-permute-done | bytes 524320 | tf_op jit(solution)/shard_map/ppermute | solution.py:512
  154.1 1.0 convert_dynamic-update-slice_fusion
  155.1 0.5 collective-permute-done.29.refs_3_
  155.7 1.4 finish.1
  (47 shorter events, 1.7 us)
Async XLA Ops:
  2.3 6.1 %collective-permute-start = (bf16[1,208,256]{2,1,0:T(8,128)(2,1)}, bf16[1,208,256]{2,1,0:T(8,128)(2,1)S(1)}, u32[]{:S(2)}, u32[]{:S(2)}) collective-permute-start(bf16[1,208,256]{2,1,0:T(8,128)(2,1)} %bitcast.13), channel_id=1, source_target_pairs={{0,4},{4,0},{8,12},{12,8},{16,20},{20,16},{24,28},{28,24},{1,5},{5... | collective-permute-start | bytes 319496 | tf_op jit(solution)/shard_map/ppermute | solution.py:512
  9.4 8.6 %collective-permute-start.1 = (bf16[2,208,256]{2,1,0:T(8,128)(2,1)S(1)}, bf16[2,208,256]{2,1,0:T(8,128)(2,1)S(1)}, u32[]{:S(2)}, u32[]{:S(2)}) collective-permute-start(bf16[2,208,256]{2,1,0:T(8,128)(2,1)S(1)} %pad_maximum_fusion.3), channel_id=1, source_target_pairs={{0,8},{4,12},{8,0},{12,4},{16,24},{20,28},{24,16},{28,20},{1,9},{5... | collective-permute-start | bytes 638984 | tf_op jit(solution)/shard_map/ppermute | solution.py:512
  18.0 5.6 %collective-permute-start.2 = (bf16[4,32,256]{2,1,0:T(8,128)(2,1)S(1)}, bf16[4,32,256]{2,1,0:T(8,128)(2,1)S(1)}, u32[]{:S(2)}, u32[]{:S(2)}) collective-permute-start(bf16[4,32,256]{2,1,0:T(8,128)(2,1)S(1)} %pad_maximum_fusion.6), channel_id=1, source_target_pairs={{0,16},{4,20},{8,24},{12,28},{16,0},{20,4},{24,8},{28,12},{1,17},{... | collective-permute-start | bytes 196616 | tf_op jit(solution)/shard_map/ppermute | solution.py:512
  31.1 2.0 %collective-permute-start.3 = (f32[1,256]{1,0:T(1,128)}, f32[1,256]{1,0:T(1,128)S(1)}, u32[]{:S(2)}, u32[]{:S(2)}) collective-permute-start(f32[1,256]{1,0:T(1,128)} %get-tuple-element.28), channel_id=1, source_target_pairs={{0,1},{1,0},{2,3},{3,2},{4,5},{5,4},{6,7},{7,6},{8,9},{9,8},{10,11... | collective-permute-start | bytes 3080 | tf_op jit(solution)/shard_map/ppermute | solution.py:515
  31.2 3.8 %collective-permute-start.4 = (f32[1,256]{1,0:T(1,128)}, f32[1,256]{1,0:T(1,128)S(1)}, u32[]{:S(2)}, u32[]{:S(2)}) collective-permute-start(f32[1,256]{1,0:T(1,128)} %get-tuple-element.28), channel_id=1, source_target_pairs={{0,2},{1,3},{2,0},{3,1},{4,6},{5,7},{6,4},{7,5},{8,10},{9,11},{10,... | collective-permute-start | bytes 3080 | tf_op jit(solution)/shard_map/ppermute | solution.py:515
  33.0 3.2 %collective-permute-start.5 = (f32[1,256]{1,0:T(1,128)}, f32[1,256]{1,0:T(1,128)S(1)}, u32[]{:S(2)}, u32[]{:S(2)}) collective-permute-start(f32[1,256]{1,0:T(1,128)} %get-tuple-element.28), channel_id=1, source_target_pairs={{0,3},{1,2},{2,1},{3,0},{4,7},{5,6},{6,5},{7,4},{8,11},{9,10},{10,... | collective-permute-start | bytes 3080 | tf_op jit(solution)/shard_map/ppermute | solution.py:515
  36.9 3.6 %collective-permute-start.6 = (f32[1,256]{1,0:T(1,128)S(1)}, f32[1,256]{1,0:T(1,128)S(1)}, u32[]{:S(2)}, u32[]{:S(2)}) collective-permute-start(f32[1,256]{1,0:T(1,128)S(1)} %add_add_fusion.5), channel_id=1, source_target_pairs={{0,4},{4,0},{8,12},{12,8},{16,20},{20,16},{24,28},{28,24},{1,5},{5... | collective-permute-start | bytes 3080 | tf_op jit(solution)/shard_map/ppermute | solution.py:512
  38.4 3.6 %collective-permute-start.7 = (f32[1,256]{1,0:T(1,128)S(1)}, f32[1,256]{1,0:T(1,128)S(1)}, u32[]{:S(2)}, u32[]{:S(2)}) collective-permute-start(f32[1,256]{1,0:T(1,128)S(1)} %add_add_fusion.5), channel_id=1, source_target_pairs={{0,8},{4,12},{8,0},{12,4},{16,24},{20,28},{24,16},{28,20},{1,9},{5... | collective-permute-start | bytes 3080 | tf_op jit(solution)/shard_map/ppermute | solution.py:512
  38.4 4.5 %collective-permute-start.8 = (f32[1,256]{1,0:T(1,128)S(1)}, f32[1,256]{1,0:T(1,128)S(1)}, u32[]{:S(2)}, u32[]{:S(2)}) collective-permute-start(f32[1,256]{1,0:T(1,128)S(1)} %add_add_fusion.5), channel_id=1, source_target_pairs={{0,12},{4,8},{8,4},{12,0},{16,28},{20,24},{24,20},{28,16},{1,13},{... | collective-permute-start | bytes 3080 | tf_op jit(solution)/shard_map/ppermute | solution.py:512
  48.5 4.8 %collective-permute-start.10 = (f32[1,256]{1,0:T(1,128)}, f32[1,256]{1,0:T(1,128)S(1)}, u32[]{:S(2)}, u32[]{:S(2)}) collective-permute-start(f32[1,256]{1,0:T(1,128)} %iterate.1), channel_id=1, source_target_pairs={{0,2},{1,3},{2,0},{3,1},{4,6},{5,7},{6,4},{7,5},{8,10},{9,11},{10,... | collective-permute-start | bytes 3080 | tf_op jit(solution)/shard_map/ppermute | solution.py:515
  49.1 4.1 %collective-permute-start.11 = (f32[1,256]{1,0:T(1,128)}, f32[1,256]{1,0:T(1,128)S(1)}, u32[]{:S(2)}, u32[]{:S(2)}) collective-permute-start(f32[1,256]{1,0:T(1,128)} %iterate.1), channel_id=1, source_target_pairs={{0,3},{1,2},{2,1},{3,0},{4,7},{5,6},{6,5},{7,4},{8,11},{9,10},{10,... | collective-permute-start | bytes 3080 | tf_op jit(solution)/shard_map/ppermute | solution.py:515
  49.1 4.1 %collective-permute-start.9 = (f32[1,256]{1,0:T(1,128)}, f32[1,256]{1,0:T(1,128)S(1)}, u32[]{:S(2)}, u32[]{:S(2)}) collective-permute-start(f32[1,256]{1,0:T(1,128)} %iterate.1), channel_id=1, source_target_pairs={{0,1},{1,0},{2,3},{3,2},{4,5},{5,4},{6,7},{7,6},{8,9},{9,8},{10,11... | collective-permute-start | bytes 3080 | tf_op jit(solution)/shard_map/ppermute | solution.py:515
  50.7 19.0 %collective-permute-start.15 = (bf16[4,176,256]{2,1,0:T(8,128)(2,1)S(1)}, bf16[4,176,256]{2,1,0:T(8,128)(2,1)S(1)}, u32[]{:S(2)}, u32[]{:S(2)}) collective-permute-start(bf16[4,176,256]{2,1,0:T(8,128)(2,1)S(1)} %pad_maximum_fusion.1), channel_id=1, source_target_pairs={{0,16},{4,20},{8,24},{12,28},{16,0},{20,4},{24,8},{28,12},{1,17},{... | collective-permute-start | bytes 1081352 | tf_op jit(solution)/shard_map/ppermute | solution.py:512
  53.9 3.6 %collective-permute-start.12 = (f32[1,256]{1,0:T(1,128)S(1)}, f32[1,256]{1,0:T(1,128)S(1)}, u32[]{:S(2)}, u32[]{:S(2)}) collective-permute-start(f32[1,256]{1,0:T(1,128)S(1)} %add_add_fusion.3), channel_id=1, source_target_pairs={{0,4},{4,0},{8,12},{12,8},{16,20},{20,16},{24,28},{28,24},{1,5},{5... | collective-permute-start | bytes 3080 | tf_op jit(solution)/shard_map/ppermute | solution.py:512
  54.4 6.7 %collective-permute-start.13 = (f32[1,256]{1,0:T(1,128)S(1)}, f32[1,256]{1,0:T(1,128)S(1)}, u32[]{:S(2)}, u32[]{:S(2)}) collective-permute-start(f32[1,256]{1,0:T(1,128)S(1)} %add_add_fusion.3), channel_id=1, source_target_pairs={{0,8},{4,12},{8,0},{12,4},{16,24},{20,28},{24,16},{28,20},{1,9},{5... | collective-permute-start | bytes 3080 | tf_op jit(solution)/shard_map/ppermute | solution.py:512
  56.0 5.2 %collective-permute-start.14 = (f32[1,256]{1,0:T(1,128)S(1)}, f32[1,256]{1,0:T(1,128)S(1)}, u32[]{:S(2)}, u32[]{:S(2)}) collective-permute-start(f32[1,256]{1,0:T(1,128)S(1)} %add_add_fusion.3), channel_id=1, source_target_pairs={{0,12},{4,8},{8,4},{12,0},{16,28},{20,24},{24,20},{28,16},{1,13},{... | collective-permute-start | bytes 3080 | tf_op jit(solution)/shard_map/ppermute | solution.py:512
  94.9 1.9 %collective-permute-start.16 = (f32[1,1536]{1,0:T(1,128)}, f32[1,1536]{1,0:T(1,128)S(1)}, u32[]{:S(2)}, u32[]{:S(2)}) collective-permute-start(f32[1,1536]{1,0:T(1,128)} %get-tuple-element.31), channel_id=1, source_target_pairs={{0,1},{1,0},{2,3},{3,2},{4,5},{5,4},{6,7},{7,6},{8,9},{9,8},{10,11... | collective-permute-start | bytes 18440 | tf_op jit(solution)/shard_map/ppermute | solution.py:515
  95.0 4.0 %collective-permute-start.17 = (f32[1,1536]{1,0:T(1,128)}, f32[1,1536]{1,0:T(1,128)S(1)}, u32[]{:S(2)}, u32[]{:S(2)}) collective-permute-start(f32[1,1536]{1,0:T(1,128)} %get-tuple-element.31), channel_id=1, source_target_pairs={{0,2},{1,3},{2,0},{3,1},{4,6},{5,7},{6,4},{7,5},{8,10},{9,11},{10,... | collective-permute-start | bytes 18440 | tf_op jit(solution)/shard_map/ppermute | solution.py:515
  95.7 3.3 %collective-permute-start.18 = (f32[1,1536]{1,0:T(1,128)}, f32[1,1536]{1,0:T(1,128)S(1)}, u32[]{:S(2)}, u32[]{:S(2)}) collective-permute-start(f32[1,1536]{1,0:T(1,128)} %get-tuple-element.31), channel_id=1, source_target_pairs={{0,3},{1,2},{2,1},{3,0},{4,7},{5,6},{6,5},{7,4},{8,11},{9,10},{10,... | collective-permute-start | bytes 18440 | tf_op jit(solution)/shard_map/ppermute | solution.py:515
  99.7 3.7 %collective-permute-start.19 = (f32[1,1536]{1,0:T(1,128)S(1)}, f32[1,1536]{1,0:T(1,128)S(1)}, u32[]{:S(2)}, u32[]{:S(2)}) collective-permute-start(f32[1,1536]{1,0:T(1,128)S(1)} %add_add_fusion.1), channel_id=1, source_target_pairs={{0,4},{4,0},{8,12},{12,8},{16,20},{20,16},{24,28},{28,24},{1,5},{5... | collective-permute-start | bytes 18440 | tf_op jit(solution)/shard_map/ppermute | solution.py:512
  100.4 3.7 %collective-permute-start.20 = (f32[1,1536]{1,0:T(1,128)S(1)}, f32[1,1536]{1,0:T(1,128)S(1)}, u32[]{:S(2)}, u32[]{:S(2)}) collective-permute-start(f32[1,1536]{1,0:T(1,128)S(1)} %add_add_fusion.1), channel_id=1, source_target_pairs={{0,8},{4,12},{8,0},{12,4},{16,24},{20,28},{24,16},{28,20},{1,9},{5... | collective-permute-start | bytes 18440 | tf_op jit(solution)/shard_map/ppermute | solution.py:512
  100.8 4.5 %collective-permute-start.21 = (f32[1,1536]{1,0:T(1,128)S(1)}, f32[1,1536]{1,0:T(1,128)S(1)}, u32[]{:S(2)}, u32[]{:S(2)}) collective-permute-start(f32[1,1536]{1,0:T(1,128)S(1)} %add_add_fusion.1), channel_id=1, source_target_pairs={{0,12},{4,8},{8,4},{12,0},{16,28},{20,24},{24,20},{28,16},{1,13},{... | collective-permute-start | bytes 18440 | tf_op jit(solution)/shard_map/ppermute | solution.py:512
  111.1 20.3 %collective-permute-start.25 = (f32[136,640]{1,0:T(8,128)S(1)}, f32[136,640]{1,0:T(8,128)S(1)}, u32[]{:S(2)}, u32[]{:S(2)}) collective-permute-start(f32[136,640]{1,0:T(8,128)S(1)} %pad_maximum_fusion.2), channel_id=1, source_target_pairs={{0,2},{1,3},{2,0},{3,1},{4,6},{5,7},{6,4},{7,5},{8,10},{9,11},{10,... | collective-permute-start | bytes 1044488 | tf_op jit(solution)/shard_map/ppermute | solution.py:515
  112.6 18.7 %copy-start.1 = (f32[1,1536]{1,0:T(1,128)S(1)}, f32[1,1536]{1,0:T(1,128)}, u32[]{:S(2)}) copy-start(f32[1,1536]{1,0:T(1,128)} %add_add_fusion.both_ref) | copy-start | bytes 18436
  127.7 27.9 %copy-start = (bf16[160,256]{1,0:T(8,128)(2,1)S(1)}, bf16[160,256]{1,0:T(8,128)(2,1)}, u32[]{:S(2)}) copy-start(bf16[160,256]{1,0:T(8,128)(2,1)} %stud_ref.3) | copy-start | bytes 245764
  127.7 27.9 %copy-start.2 = (s32[3]{0:T(128)S(1)}, s32[3]{0:T(128)}, u32[]{:S(2)}) copy-start(s32[3]{0:T(128)} %pad_add_fusion.place) | copy-start | bytes 40
  127.7 27.9 %copy-start.3 = (s32[160]{0:T(256)S(1)}, s32[160]{0:T(256)}, u32[]{:S(2)}) copy-start(s32[160]{0:T(256)} %param.7) | copy-start | bytes 1924
  127.8 14.2 %collective-permute-start.22 = (bf16[32,8192]{1,0:T(8,128)(2,1)}, bf16[32,8192]{1,0:T(8,128)(2,1)S(1)}, u32[]{:S(2)}, u32[]{:S(2)}) collective-permute-start(bf16[32,8192]{1,0:T(8,128)(2,1)} %get-tuple-element.38), channel_id=1, source_target_pairs={{0,4},{4,0},{8,12},{12,8},{16,20},{20,16},{24,28},{28,24},{1,5},{5... | collective-permute-start | bytes 1572872 | tf_op jit(solution)/shard_map/ppermute | solution.py:512
  129.3 15.1 %collective-permute-start.23 = (bf16[32,8192]{1,0:T(8,128)(2,1)}, bf16[32,8192]{1,0:T(8,128)(2,1)S(1)}, u32[]{:S(2)}, u32[]{:S(2)}) collective-permute-start(bf16[32,8192]{1,0:T(8,128)(2,1)} %get-tuple-element.39), channel_id=1, source_target_pairs={{0,8},{4,12},{8,0},{12,4},{16,24},{20,28},{24,16},{28,20},{1,9},{5... | collective-permute-start | bytes 1572872 | tf_op jit(solution)/shard_map/ppermute | solution.py:512
  130.8 23.3 %collective-permute-start.24 = (bf16[32,8192]{1,0:T(8,128)(2,1)}, bf16[32,8192]{1,0:T(8,128)(2,1)S(1)}, u32[]{:S(2)}, u32[]{:S(2)}) collective-permute-start(bf16[32,8192]{1,0:T(8,128)(2,1)} %get-tuple-element.40), channel_id=1, source_target_pairs={{0,12},{4,8},{8,4},{12,0},{16,28},{20,24},{24,20},{28,16},{1,13},{... | collective-permute-start | bytes 1572872 | tf_op jit(solution)/shard_map/ppermute | solution.py:512
  132.2 13.2 %collective-permute-start.26 = (f32[72,640]{1,0:T(8,128)S(1)}, f32[72,640]{1,0:T(8,128)S(1)}, u32[]{:S(2)}, u32[]{:S(2)}) collective-permute-start(f32[72,640]{1,0:T(8,128)S(1)} %pad_maximum_fusion.4), channel_id=1, source_target_pairs={{0,1},{1,0},{2,3},{3,2},{4,5},{5,4},{6,7},{7,6},{8,9},{9,8},{10,11... | collective-permute-start | bytes 552968 | tf_op jit(solution)/shard_map/ppermute | solution.py:515
  145.7 9.5 %collective-permute-start.27 = (f32[72,160]{1,0:T(8,128)S(1)}, f32[72,160]{1,0:T(8,128)S(1)}, u32[]{:S(2)}, u32[]{:S(2)}) collective-permute-start(f32[72,160]{1,0:T(8,128)S(1)} %get-tuple-element.53), channel_id=1, source_target_pairs={{0,4},{4,0},{8,12},{12,8},{16,20},{20,16},{24,28},{28,24},{1,5},{5... | collective-permute-start | bytes 138248 | tf_op jit(solution)/shard_map/ppermute | solution.py:512
  146.3 8.9 %collective-permute-start.28 = (f32[72,160]{1,0:T(8,128)S(1)}, f32[72,160]{1,0:T(8,128)S(1)}, u32[]{:S(2)}, u32[]{:S(2)}) collective-permute-start(f32[72,160]{1,0:T(8,128)S(1)} %get-tuple-element.54), channel_id=1, source_target_pairs={{0,8},{4,12},{8,0},{12,4},{16,24},{20,28},{24,16},{28,20},{1,9},{5... | collective-permute-start | bytes 138248 | tf_op jit(solution)/shard_map/ppermute | solution.py:512
  147.8 7.9 %collective-permute-start.29 = (f32[72,160]{1,0:T(8,128)S(1)}, f32[72,160]{1,0:T(8,128)S(1)}, u32[]{:S(2)}, u32[]{:S(2)}) collective-permute-start(f32[72,160]{1,0:T(8,128)S(1)} %get-tuple-element.51), channel_id=1, source_target_pairs={{0,12},{4,8},{8,4},{12,0},{16,28},{20,24},{24,20},{28,16},{1,13},{... | collective-permute-start | bytes 138248 | tf_op jit(solution)/shard_map/ppermute | solution.py:512

commit v3 on v2

--- a/solution.py
+++ b/solution.py
@@ -13,7 +13,8 @@
 LOG2E = 1.4426950408889634
 GROUP = 4
 CHUNKS = 8
-LIMIT = 58
+LIMIT = 50
+PARTS = 2
 F32 = jnp.float32
 BF16 = jnp.bfloat16
 NT = (((1,), (1,)), ((), ()))
@@ -108,7 +109,7 @@
         in_specs=grid_one((t, d), (s, d), (1, s)),
         out_specs=grid_one((t + s + 16, d))[0],
         scratch_shapes=[pltpu.VMEM((16, d), F32)],
-        compiler_params=params(LIMIT),
+        compiler_params=params(58),
         name="prepare",
     )(teach, stud, pairs)
 
@@ -204,8 +205,8 @@
 
 def iterate_kernel(total_k, last, sum_in, energy_hbm, *refs):
     if last:
-        unit_hbm, denom_ref, sum_ref, mean_ref, scaled_hbm = refs[:5]
-        acc, row, energy, sems_in, scaled, unit, sems_out = refs[5:]
+        unit_hbm, near_ref, far_ref, sum_ref, mean_ref, scaled_hbm = refs[:6]
+        acc, row, energy, sems_in, scaled, unit, sems_out = refs[6:]
         mean_ref[...] = jnp.zeros_like(mean_ref)
     else:
         sum_ref, acc, row, energy, sems_in = refs
@@ -244,7 +245,9 @@
     stream(chunks, fetch, work)
     sum_ref[:, :t] = to_row(acc[...])
     if last:
-        sum_ref[:, t:] = denom_ref[...]
+        n = near_ref.shape[1]
+        sum_ref[:, t : t + n] = near_ref[...]
+        sum_ref[:, t + n :] = far_ref[...]
         for i in range(chunks):
             store(i).wait()
 
@@ -258,14 +261,14 @@
         pltpu.VMEM((t, 128), F32), pltpu.VMEM((t, 128), F32), pltpu.VMEM(energy.shape, BF16), DMA((chunks, 2))
     ]
     if last:
-        unit, denom = more
+        unit, near, far = more
         d = unit.shape[1]
         out_shape = [
-            jax.ShapeDtypeStruct((1, t + denom.shape[1]), F32),
+            jax.ShapeDtypeStruct((1, t + near.shape[1] + far.shape[1]), F32),
             jax.ShapeDtypeStruct((d, t), F32),
             jax.ShapeDtypeStruct(energy.shape, BF16),
         ]
-        in_specs, out_specs = in_specs + anywhere(1) + vmem(1), vmem(2) + anywhere(1)
+        in_specs, out_specs = in_specs + anywhere(1) + vmem(2), vmem(2) + anywhere(1)
         scratch += [pltpu.VMEM(energy.shape, BF16), pltpu.VMEM(unit.shape, BF16), DMA((chunks,))]
     return pl.pallas_call(
         functools.partial(iterate_kernel, float(total_k), last),
@@ -281,13 +284,14 @@
     )(sums, energy, *more)
 
 
-def student_kernel(place, rest_ref, pairs_ref, unit_hbm, expo_hbm, denom_ref, pull_ref, stud_t_hbm, weight_hbm,
-                   unit, expo, acc, pull, stud, stud_t, weight, sems_in, sems_out, sems):
+def student_kernel(block, near, rest_ref, pairs_ref, unit_hbm, expo_hbm, denom_ref, stud_t_ref, weight_ref, *refs):
+    if near:
+        pull_ref, pull, refs = refs[0], refs[-1], refs[1:-1]
+        pull[...] = jnp.zeros_like(pull)
+    unit, expo, acc, stud, sems_in, sems_out = refs
     chunks, s, width = expo.shape
     s_dev = s // rest_ref.shape[0]
-    n = pull.shape[0]
-    t = weight.shape[1]
-    start = pl.multiple_of(place[1] * n, 128)
+    t = weight_ref.shape[1]
 
     def fetch(i):
         return (pltpu.make_async_copy(unit_hbm.at[i], unit.at[i], sems_in.at[i]),)
@@ -297,81 +301,112 @@
 
     begin(chunks, fetch)
     acc[...] = jnp.zeros_like(acc)
-    pull[...] = jnp.zeros_like(pull)
     for i in range(rest_ref.shape[0]):
         stud[i * s_dev : (i + 1) * s_dev, :] = rest_ref[i, :s_dev, :]
     rows_t = stud[...].astype(F32).T.astype(BF16)
-    stud_t[...] = rows_t
+    stud_t_ref[...] = rows_t
     which = lax.broadcasted_iota(jnp.int32, (t, s), 0)
     onehot = (which == pairs_ref[...]).astype(F32).astype(BF16)
-    weight[...] = lax.dot_general(rows_t, onehot, NT, preferred_element_type=F32)
-    extra = (
-        pltpu.make_async_copy(stud_t, stud_t_hbm, sems.at[0]),
-        pltpu.make_async_copy(weight, weight_hbm, sems.at[1]),
-    )
-    for copy in extra:
-        copy.start()
+    weight_ref[...] = lax.dot_general(rows_t, onehot, NT, preferred_element_type=F32)
 
     def work(i):
-        for at in range(0, s, 256):
-            logits = jnp.dot(stud[at : at + 256, :], unit[i], preferred_element_type=F32)
+        for at in range(0, s, block):
+            logits = jnp.dot(stud[at : at + block, :], unit[i], preferred_element_type=F32)
             x = jnp.exp2(logits * (LOG2E / student_temp))
-            expo[i, at : at + 256, :] = x.astype(BF16)
-            acc[at : at + 256, :] += lane_sums(x)
+            expo[i, at : at + block, :] = x.astype(BF16)
+            acc[at : at + block, :] += lane_sums(x)
         store(i).start()
-        pull[...] += lax.dot_general(expo[i, pl.ds(start, n), :], unit[i], NT, preferred_element_type=F32)
+        if near:
+            pull[...] += lax.dot_general(expo[i], unit[i], NT, preferred_element_type=F32)
 
     stream(chunks, fetch, work)
     denom_ref[...] = to_row(acc[...])
-    pull_ref[...] = pull[...].T
-    for copy in extra:
-        copy.wait()
+    if near:
+        pull_ref[...] = pull[...].T
     for i in range(chunks):
         store(i).wait()
 
 
-def student_call(place, rest, pairs, unit, t, n):
+def student_call(rest, pairs, unit, t, near):
     chunks, d, width = unit.shape
     s = rest.shape[0] * (rest.shape[1] - 16)
     shape = (chunks, s, width)
+    out_shape = [
+        jax.ShapeDtypeStruct(shape, BF16),
+        jax.ShapeDtypeStruct((1, s), F32),
+        jax.ShapeDtypeStruct((d, s), BF16),
+        jax.ShapeDtypeStruct((d, t), F32),
+    ]
+    scratch = [
+        pltpu.VMEM(unit.shape, BF16), pltpu.VMEM(shape, BF16), pltpu.VMEM((s, 128), F32),
+        pltpu.VMEM((s, d), BF16), DMA((chunks,)), DMA((chunks,)),
+    ]
+    if near:
+        out_shape += [jax.ShapeDtypeStruct((d, s), F32)]
+        scratch += [pltpu.VMEM((s, d), F32)]
     return pl.pallas_call(
-        student_kernel,
-        out_shape=(
-            jax.ShapeDtypeStruct(shape, BF16),
-            jax.ShapeDtypeStruct((1, s), F32),
-            jax.ShapeDtypeStruct((d, n), F32),
-            jax.ShapeDtypeStruct((d, s), BF16),
-            jax.ShapeDtypeStruct((d, t), F32),
-        ),
-        in_specs=[SMEM] + vmem(2) + anywhere(1),
-        out_specs=tuple(anywhere(1) + vmem(2) + anywhere(2)),
-        scratch_shapes=[
-            pltpu.VMEM(unit.shape, BF16), pltpu.VMEM(shape, BF16), pltpu.VMEM((s, 128), F32),
-            pltpu.VMEM((n, d), F32), pltpu.VMEM((s, d), BF16), pltpu.VMEM((d, s), BF16), pltpu.VMEM((d, t), F32),
-            DMA((chunks,)), DMA((chunks,)), DMA((2,)),
-        ],
+        functools.partial(student_kernel, 2 * (rest.shape[1] - 16), near),
+        out_shape=out_shape,
+        in_specs=vmem(2) + anywhere(1),
+        out_specs=anywhere(1) + vmem(len(out_shape) - 1),
+        scratch_shapes=scratch,
         cost_estimate=pl.CostEstimate(
             flops=4 * s * d * chunks * width, bytes_accessed=2 * s * chunks * width, transcendentals=0
         ),
         compiler_params=params(LIMIT),
-        name="student",
-    )(place, rest, pairs, unit)
-
-
-def head_kernel(factor, place, both_ref, pairs_ref, stud_t_ref, weight_ref, inv_ref, expo_hbm,
-                scaled_hbm, v_hbm, own_hbm, *refs):
-    sends, refs = refs[: GROUP - 1], refs[GROUP - 1 :]
+        name="student_near" if near else "student_far",
+    )(rest, pairs, unit)
+
+
+def back_terms(factor, place, both_ref, pairs_ref, stud_t_ref, pull_ref, mean_ref, keep_ref, send_ref, tail_ref, back):
+    d, n = pull_ref.shape
+    t = mean_ref.shape[1]
+    sums = both_ref[:, :t]
+    denom = both_ref[:, t : t + n]
+    row = 1.0 / (sums * float(t))
+    pairs = pairs_ref[:, :n]
+    mass = pick(to_column(row * sums * float(t)), pairs)
+    which = lax.broadcasted_iota(jnp.int32, (t, n), 0)
+    onehot = (which == pairs).astype(F32)
+    target = jnp.dot(
+        mean_ref[...] * (row * t), onehot, preferred_element_type=F32, precision=lax.Precision.HIGHEST
+    )
+    stud_t = stud_t_ref[...].astype(F32)
+    terms = (pull_ref[...] * (mass / denom) - target) * factor
+    back[...] = terms
+    along = jnp.sum(stud_t * terms, axis=0, keepdims=True)
+    cross = jnp.sum(stud_t * target, axis=0, keepdims=True) * (1.0 / student_temp)
+    at = lax.broadcasted_iota(jnp.int32, (8, n), 0)
+    tail = jnp.where(at == 0, along, jnp.where(at == 1, cross, 0.0))
+    half = d // 2
+    keep_ref[...] = back[pl.ds(pl.multiple_of(place[3] * half, half), half), :]
+    send_ref[:half, :] = back[pl.ds(pl.multiple_of((1 - place[3]) * half, half), half), :]
+    send_ref[half:, :] = tail
+    tail_ref[...] = tail
+
+
+def head_kernel(factor, first, place, both_ref, pairs_ref, near_ref, far_ref, weight_ref, more_weight_ref,
+                inv_ref, near_hbm, far_hbm, scaled_hbm, v_hbm, *refs):
+    if first == 0:
+        pull_ref, mean_ref, own_hbm = refs[:3]
+        sends, terms, refs = refs[3 : GROUP + 2], refs[GROUP + 2 : GROUP + 5], refs[GROUP + 5 :]
+        back, refs = refs[-1], refs[:-1]
+    else:
+        own_hbm, sends, refs = refs[1], refs[2 : GROUP + 1], refs[GROUP + 1 :]
     lhs, lhs_teach, grad, expo, scaled, v, own, sems_in, sems_out = refs
     chunks, t, width = scaled.shape
+    all_chunks = inv_ref.shape[0]
+    n_near, n_far = near_ref.shape[1], far_ref.shape[1]
     rows = own.shape[1]
 
     def start_of(i):
-        return pl.multiple_of((place[0] * chunks + i) * width, width)
+        return pl.multiple_of((place[0] * all_chunks + first + i) * width, width)
 
     def fetches(i):
         return (
-            pltpu.make_async_copy(expo_hbm.at[i], expo.at[i], sems_in.at[i, 0]),
-            pltpu.make_async_copy(scaled_hbm.at[i], scaled.at[i], sems_in.at[i, 1]),
+            pltpu.make_async_copy(near_hbm.at[first + i], expo.at[i, pl.ds(0, n_near), :], sems_in.at[i, 0]),
+            pltpu.make_async_copy(far_hbm.at[first + i], expo.at[i, pl.ds(n_near, n_far), :], sems_in.at[i, 3]),
+            pltpu.make_async_copy(scaled_hbm.at[first + i], scaled.at[i], sems_in.at[i, 1]),
             pltpu.make_async_copy(v_hbm.at[:, pl.ds(start_of(i), width)], v.at[i], sems_in.at[i, 2]),
         )
 
@@ -382,8 +417,12 @@
     sums, denom = both_ref[:, :t], both_ref[:, t:]
     row = 1.0 / (sums * float(t))
     mass = pick(to_column(row * sums * float(t)), pairs_ref[...])
-    lhs[...] = (stud_t_ref[...].astype(F32) * (mass / denom * factor)).astype(BF16)
-    lhs_teach[...] = (weight_ref[...] * (row * (-factor * t))).astype(BF16)
+    scale = mass / denom * factor
+    lhs[:, :n_near] = (near_ref[...].astype(F32) * scale[:, :n_near]).astype(BF16)
+    lhs[:, n_near:] = (far_ref[...].astype(F32) * scale[:, n_near:]).astype(BF16)
+    lhs_teach[...] = ((weight_ref[...] + more_weight_ref[...]) * (row * (-factor * t))).astype(BF16)
+    if first == 0:
+        back_terms(factor, place, both_ref, pairs_ref, near_ref, pull_ref, mean_ref, *terms, back)
     base = place[1] * (rows * GROUP)
 
     def part(n):
@@ -393,7 +432,7 @@
     def work(i):
         head = jnp.dot(lhs[...], expo[i], preferred_element_type=F32)
         head = head + jnp.dot(lhs_teach[...], scaled[i], preferred_element_type=F32)
-        inv = inv_ref[i]
+        inv = inv_ref[first + i]
         unit = v[i].astype(F32) * inv
         proj = jnp.sum(unit * head, axis=0, keepdims=True)
         grad[...] = (head - unit * proj) * inv
@@ -408,64 +447,41 @@
         store(i).wait()
 
 
-def head_call(place, both, pairs, stud_t, weight, inv, expo, scaled, v, factor, rows):
-    d, s = stud_t.shape
-    chunks, t, width = scaled.shape
+def head_call(first, chunks, place, both, pairs, students, inv, scaled, v, factor, rows, more):
+    near, far, near_t, far_t, weight, more_weight = students
+    d, s = near_t.shape[0], pairs.shape[1]
+    _, t, width = scaled.shape
     kl = chunks * width
+    out_shape = [jax.ShapeDtypeStruct((rows, v.shape[1]), F32)] + [jax.ShapeDtypeStruct((rows, kl), BF16)] * (GROUP - 1)
+    out_specs = anywhere(1) + vmem(GROUP - 1)
+    scratch = [
+        pltpu.VMEM((d, s), BF16), pltpu.VMEM((d, t), BF16), pltpu.VMEM((d, width), F32),
+        pltpu.VMEM((chunks, s, width), BF16), pltpu.VMEM((chunks, t, width), BF16),
+        pltpu.VMEM((chunks, d, width), BF16), pltpu.VMEM((chunks, rows, width), F32),
+        DMA((chunks, 4)), DMA((chunks,)),
+    ]
+    if first == 0:
+        n = more[0].shape[1]
+        out_shape += [
+            jax.ShapeDtypeStruct((d // 2, n), F32),
+            jax.ShapeDtypeStruct((d // 2 + 8, n), F32),
+            jax.ShapeDtypeStruct((8, n), F32),
+        ]
+        out_specs += vmem(3)
+        scratch += [pltpu.VMEM((d, n), F32)]
     return pl.pallas_call(
-        functools.partial(head_kernel, factor),
-        out_shape=[jax.ShapeDtypeStruct((rows, v.shape[1]), F32)]
-        + [jax.ShapeDtypeStruct((rows, kl), BF16)] * (GROUP - 1),
-        in_specs=[SMEM] + vmem(5) + anywhere(3),
-        out_specs=anywhere(1) + vmem(GROUP - 1),
-        scratch_shapes=[
-            pltpu.VMEM((d, s), BF16), pltpu.VMEM((d, t), BF16), pltpu.VMEM((d, width), F32),
-            pltpu.VMEM(expo.shape, BF16), pltpu.VMEM(scaled.shape, BF16), pltpu.VMEM((chunks, d, width), BF16),
-            pltpu.VMEM((chunks, rows, width), F32), DMA((chunks, 3)), DMA((chunks,)),
-        ],
+        functools.partial(head_kernel, factor, first),
+        out_shape=out_shape,
+        in_specs=[SMEM] + vmem(7) + anywhere(4) + (vmem(2) if first == 0 else anywhere(1)),
+        out_specs=out_specs,
+        scratch_shapes=scratch,
+        input_output_aliases={} if first == 0 else {12: 0},
         cost_estimate=pl.CostEstimate(
             flops=4 * (s + t) * d * kl, bytes_accessed=2 * (s + t + d) * kl, transcendentals=0
         ),
         compiler_params=params(LIMIT),
         name="head",
-    )(place, both, pairs, stud_t, weight, inv, expo, scaled, v)
-
-
-def back_kernel(factor, place, both_ref, pairs_ref, stud_t_ref, pull_ref, mean_ref, back_ref):
-    d, n = pull_ref.shape
-    t = mean_ref.shape[1]
-    start = pl.multiple_of(place[1] * n, 128)
-    mine = pl.ds(start, n)
-    sums = both_ref[:, :t]
-    denom = both_ref[:, pl.ds(pl.multiple_of(t + place[1] * n, 128), n)]
-    row = 1.0 / (sums * float(t))
-    pairs = pairs_ref[:, mine]
-    mass = pick(to_column(row * sums * float(t)), pairs)
-    which = lax.broadcasted_iota(jnp.int32, (t, n), 0)
-    onehot = (which == pairs).astype(F32)
-    target = jnp.dot(
-        mean_ref[...] * (row * t), onehot, preferred_element_type=F32, precision=lax.Precision.HIGHEST
-    )
-    stud_t = stud_t_ref[:, mine].astype(F32)
-    back = (pull_ref[...] * (mass / denom) - target) * factor
-    back_ref[:d, :] = back
-    along = jnp.sum(stud_t * back, axis=0, keepdims=True)
-    cross = jnp.sum(stud_t * target, axis=0, keepdims=True) * (1.0 / student_temp)
-    at = lax.broadcasted_iota(jnp.int32, (8, n), 0)
-    back_ref[d:, :] = jnp.where(at == 0, along, jnp.where(at == 1, cross, 0.0))
-
-
-def back_call(place, both, pairs, stud_t, pull, mean, factor):
-    d, n = pull.shape
-    return pl.pallas_call(
-        functools.partial(back_kernel, factor),
-        out_shape=jax.ShapeDtypeStruct((d + 8, n), F32),
-        in_specs=[SMEM] + vmem(5),
-        out_specs=vmem(1)[0],
-        cost_estimate=pl.CostEstimate(flops=12 * d * n * mean.shape[1], bytes_accessed=12 * d * n, transcendentals=0),
-        compiler_params=params(LIMIT),
-        name="back",
-    )(place, both, pairs, stud_t, pull, mean)
+    )(place, both, pairs, near_t, far_t, weight, more_weight, inv, near, far, scaled, v, *more)
 
 
 def finish_kernel(t, place, both_ref, denom_ref, pairs_ref, stud_ref, *refs):
@@ -505,7 +521,8 @@
     t_dev, s_dev = teacher_features.shape[0], student_features.shape[0]
     t, s = t_dev * n_rows, s_dev * n_rows
     at, group = r % GROUP, r // GROUP
-    place = jnp.stack([at, group, p]).astype(jnp.int32)
+    top = (p * 2) // n_proto
+    place = jnp.stack([at, group, p, top]).astype(jnp.int32)
     factor = total_k / 64.0 / student_temp
 
     def swap_rows(x, n):
@@ -533,39 +550,70 @@
     packed = join(packed, 1)
     other, unit, inv = lax.optimization_barrier((swap_rows(packed, 2), unit, inv))
     packed = join(packed, 2, other)
-    teach_all, rest = packed[:, :t_dev], packed[:, t_dev:]
+    teach_all, near = packed[:, :t_dev], packed[:, t_dev:]
     n = GROUP
     while n < n_rows:
         teach_all = join(teach_all, n)
-        rest = join(rest, n)
         n *= 2
     teach_all = teach_all.reshape(t, d)
-    digits = rest[:, s_dev : s_dev + 2, :s_dev].astype(F32)
-    pairs = (digits[:, 0] * 64.0 + digits[:, 1]).astype(jnp.int32).reshape(1, s)
+
+    def pairs_of(rest):
+        digits = rest[:, s_dev : s_dev + 2, :s_dev].astype(F32)
+        return (digits[:, 0] * 64.0 + digits[:, 1]).astype(jnp.int32).reshape(1, -1)
 
     energy, sums = energy_call(teach_all, unit, total_k)
-    expo, denom, pull, stud_t, weight = student_call(place, rest, pairs, unit, t, s_dev * GROUP)
-    (sums,) = iterate_call(total(sums), energy, total_k)
-    both, mean, scaled = iterate_call(total(sums), energy, total_k, (unit, denom))
+    far = swap_rows(near, GROUP)
+    n = 2 * GROUP
+    while n < n_rows:
+        far = jnp.concatenate([far, swap_rows(jnp.concatenate([near, far], axis=0), n)], axis=0)
+        n *= 2
+    near_pairs = pairs_of(near)
+    expo_near, denom_near, near_t, weight, pull = student_call(near, near_pairs, unit, t, True)
+    sums = total(sums)
+    far, denom_near, sums = lax.optimization_barrier((far, denom_near, sums))
+    far_pairs = pairs_of(far)
+    expo_far, denom_far, far_t, more_weight = student_call(far, far_pairs, unit, t, False)
+    pairs = jnp.concatenate([near_pairs, far_pairs], axis=1)
+    (sums,) = iterate_call(sums, energy, total_k)
+    both, mean, scaled = iterate_call(total(sums), energy, total_k, (unit, denom_near, denom_far))
     both = total(both)
+    students = (expo_near, expo_far, near_t, far_t, weight, more_weight)
 
     rows = d // n_rows
-    grads = head_call(place, both, pairs, stud_t, weight, inv, expo, scaled, v, factor, rows)
-    proto_grad = grads[0]
-    for n in range(1, GROUP):
-        got = swap_rows(grads[n], n).astype(F32)
-        proto_grad = lax.dynamic_update_slice(proto_grad, got, (0, (at ^ n) * kl))
-
-    back = back_call(place, both, pairs, stud_t, pull, mean, factor)
-    body_rows, tail = back[:d], back[d:]
+    chunks = CHUNKS // PARTS
+    more = (pull, mean)
+    pieces = []
+    for first in range(0, CHUNKS, chunks):
+        out = head_call(
+            first, chunks, place, both, pairs, students, inv, scaled, v, factor, rows, more
+        )
+        if first == 0:
+            body_rows, send, tail = out[GROUP:]
+        more = (out[0],)
+        arrived = []
+        for n in range(1, GROUP):
+            share = out[n]
+            if pieces:
+                share, pieces[-1][n - 1] = lax.optimization_barrier((share, pieces[-1][n - 1]))
+            arrived.append(swap_rows(share, n))
+        pieces.append(arrived)
+    proto_grad = out[0]
+    for part, arrived in enumerate(pieces):
+        for n, got in enumerate(arrived, 1):
+            start = (at ^ n) * kl + part * (kl // PARTS)
+            proto_grad = lax.dynamic_update_slice(proto_grad, got.astype(F32), (0, start))
+
     n = n_proto // 2
     while n >= 1:
-        height = body_rows.shape[0] // 2
-        bit = (p // n) % 2
-        keep = lax.dynamic_slice_in_dim(body_rows, bit * height, height, 0)
-        send = lax.dynamic_slice_in_dim(body_rows, (1 - bit) * height, height, 0)
-        got = swap_proto(jnp.concatenate([send, tail], axis=0), n)
-        body_rows, tail = keep + got[:height], tail + got[height:]
+        if n < n_proto // 2:
+            height = body_rows.shape[0] // 2
+            bit = (p // n) % 2
+            send = lax.dynamic_slice_in_dim(body_rows, (1 - bit) * height, height, 0)
+            body_rows = lax.dynamic_slice_in_dim(body_rows, bit * height, height, 0)
+            send = jnp.concatenate([send, tail], axis=0)
+        got = swap_proto(send, n)
+        height = body_rows.shape[0]
+        body_rows, tail = body_rows + got[:height], tail + got[height:]
         n //= 2
     terms = jnp.concatenate([body_rows, tail], axis=0)
 
@@ -573,7 +621,7 @@
         return lax.dynamic_slice_in_dim(terms, (at ^ n) * s_dev, s_dev, 1)
 
     parts = [block(0)] + [swap_rows(block(n), n) for n in range(1, GROUP)]
-    own = lax.dynamic_slice_in_dim(both, t + r * s_dev, s_dev, 1)
+    own = lax.dynamic_slice_in_dim(both, t + at * s_dev, s_dev, 1)
     student_grad, loss = finish_call(t, place, both, own, own_pairs, student_features, parts, d // n_proto)
     return (proto_grad, student_grad.T, loss.reshape(s_dev))
 

time: 158 us -> 129 us (0.82)
  waiting for transfers between devices: 44.1 us -> 25.5 us
  Pallas kernels: 62.8 us -> 57.4 us
  other arithmetic: 11.3 us -> 6.49 us
  starting transfers between devices: 35.3 us -> 37.9 us
  local copies, waits for them, and re-layouts: 2.67 us -> 0.3 us
    ppermute x19 -> x22, waiting for transfers between devices: 38.9 us -> 20.5 us  [swap_rows(): return lax.ppermute(x, 'rows', [(j, j ^ n) for j in range(n_rows)])]
    add x6, other arithmetic: 3.77 us -> 0.05 us  [total(): x = x + swap(x, n) + (swap(x, 2 * n) + swap(x, 3 * n))]
    ppermute x19 -> x22, starting transfers between devices: 27.6 us -> 30.6 us  [swap_rows(): return lax.ppermute(x, 'rows', [(j, j ^ n) for j in range(n_rows)])]
    pallas_call x2, Pallas kernels: 13.5 us -> 10.8 us  [iterate_call(): pl.pallas_call(functools.partial(iterate_kernel, float(total_k), last), o...]
    slice x2 -> x0, local copies, waits for them, and re-layouts: 1.86 us -> none  [body(): body_rows, tail = (back[:d], back[d:])]
    dynamic_update_slice x3 -> x6, other arithmetic: 3.12 us -> 4.97 us  [body(): lax.dynamic_update_slice(proto_grad, got.astype(F32), (0, start))]
    pallas_call x3 -> x4, Pallas kernels: 33.3 us -> 32.7 us  [the longest x2 16.9 us: head_call(): pl.pallas_call(functools.partial(head_kernel, factor, first), out_shape=o...]
  transfers between devices with their start and end apart: 30 -> 33, of which waited for: 18 -> 17; matrix products, arithmetic and copies ran while one was open for 4% -> 4% of each run, Pallas kernels for 13% -> 23%
where the time goes in v3:
time: 129 us
  Pallas kernels  57.4 us (44%)
  starting transfers between devices  37.9 us (29%)
  waiting for transfers between devices  25.5 us (20%)
  other arithmetic  6.49 us (5%)
    ppermute x22, starting transfers between devices, swap_rows(): return lax.ppermute(x, 'rows', [(j, j ^ n) for j in range(n_rows)])  30.6 us
    ppermute x22, waiting for transfers between devices, swap_rows(): return lax.ppermute(x, 'rows', [(j, j ^ n) for j in range(n_rows)])  20.5 us
    pallas_call x2, Pallas kernels, head_call(): pl.pallas_call(functools.partial(head_kernel, factor, first), out_shape=o...  16.9 us
    pallas_call x2, Pallas kernels, student_call(): pl.pallas_call(functools.partial(student_kernel, 2 * (rest.shape[1] - 16)...  15.8 us
    pallas_call x2, Pallas kernels, iterate_call(): pl.pallas_call(functools.partial(iterate_kernel, float(total_k), last), o...  10.8 us
    ppermute x11, starting transfers between devices, swap_proto(): return lax.ppermute(x, 'proto', [(j, j ^ n) for j in range(n_proto)])  7.32 us
    pallas_call x1, Pallas kernels, energy_call(): pl.pallas_call(functools.partial(energy_kernel, float(total_k)), out_shap...  5.47 us
    pallas_call x1, Pallas kernels, unit_call(): pl.pallas_call(unit_kernel, out_shape=(jax.ShapeDtypeStruct(shape, BF16),...  5.31 us
  transfers between devices with their start and end apart: 33, of which 17 were waited for; matrix products, arithmetic and copies ran while one was open for 4% of the time, Pallas kernels for 23%

profile of v3, /device:TPU:0, one launch (start us, length us, event | category | flops | bytes accessed | tf_op | source)
XLA Modules:
  0.0 128.5 jit_solution(14907626783757339461)
XLA Ops:
  0.6 1.7 %prepare.1 = bf16[208,256]{1,0:T(8,128)(2,1)} custom-call(bf16[32,256]{1,0:T(8,128)(2,1)} %teach_ref.1, bf16[160,256]{1,0:T(8,128)(2,1)} %stud_ref.3, s32[1,160]{1,0:T(1,128)} %bitcast.12), custom_call_target="tpu_custom_call" | custom-call | tf_op jit(solution)/shard_map/prepare/pallas_call | solution.py:105
  2.3 2.9 %collective-permute-start = (bf16[1,208,256]{2,1,0:T(8,128)(2,1)}, bf16[1,208,256]{2,1,0:T(8,128)(2,1)S(1)}, u32[]{:S(2)}, u32[]{:S(2)}) collective-permute-start(bf16[1,208,256]{2,1,0:T(8,128)(2,1)} %bitcast.14), channel_id=1, source_target_pairs={{0,4},{4,0},{8,12},{12,8},{16,20},{20,16},{24,28},{28,24},{1,5},{5... | collective-permute-start | bytes 319496 | tf_op jit(solution)/shard_map/ppermute | solution.py:529
  5.2 3.2 %collective-permute-done = bf16[1,208,256]{2,1,0:T(8,128)(2,1)S(1)} collective-permute-done((bf16[1,208,256]{2,1,0:T(8,128)(2,1)}, bf16[1,208,256]{2,1,0:T(8,128)(2,1)S(1)}, u32[]{:S(2)}, u32[]{:S(2)}) %collective-permute-start) | collective-permute-done | bytes 106528 | tf_op jit(solution)/shard_map/ppermute | solution.py:529
  8.4 0.9 broadcast_select_fusion.3
  9.4 1.9 %collective-permute-start.1 = (bf16[2,208,256]{2,1,0:T(8,128)(2,1)S(1)}, bf16[2,208,256]{2,1,0:T(8,128)(2,1)S(1)}, u32[]{:S(2)}, u32[]{:S(2)}) collective-permute-start(bf16[2,208,256]{2,1,0:T(8,128)(2,1)S(1)} %pad_maximum_fusion), channel_id=1, source_target_pairs={{0,8},{4,12},{8,0},{12,4},{16,24},{20,28},{24,16},{28,20},{1,9},{5... | collective-permute-start | bytes 638984 | tf_op jit(solution)/shard_map/ppermute | solution.py:529
  11.3 5.3 %unit.1 = (bf16[8,256,1024]{2,1,0:T(8,128)(2,1)}, f32[8,1,1024]{2,1,0:T(1,128)S(1)}) custom-call(s32[4]{0:T(128)S(1)} %pad_add_fusion.place, bf16[256,32768]{1,0:T(8,128)(2,1)} %v_hbm.5), custom_call_target="tpu_custom_call" | custom-call | flops 8388608 | bytes 8388608 | tf_op jit(solution)/shard_map/unit/pallas_call | solution.py:144
  16.8 2.7 %collective-permute-start.3 = (bf16[4,32,256]{2,1,0:T(8,128)(2,1)S(1)}, bf16[4,32,256]{2,1,0:T(8,128)(2,1)S(1)}, u32[]{:S(2)}, u32[]{:S(2)}) collective-permute-start(bf16[4,32,256]{2,1,0:T(8,128)(2,1)S(1)} %pad_maximum_fusion.3), channel_id=1, source_target_pairs={{0,16},{4,20},{8,24},{12,28},{16,0},{20,4},{24,8},{28,12},{1,17},{... | collective-permute-start | bytes 196616 | tf_op jit(solution)/shard_map/ppermute | solution.py:529
  19.4 3.1 %collective-permute-done.3 = bf16[4,32,256]{2,1,0:T(8,128)(2,1)S(1)} collective-permute-done((bf16[4,32,256]{2,1,0:T(8,128)(2,1)S(1)}, bf16[4,32,256]{2,1,0:T(8,128)(2,1)S(1)}, u32[]{:S(2)}, u32[]{:S(2)}) %collective-permute-start.3) | collective-permute-done | bytes 65568 | tf_op jit(solution)/shard_map/ppermute | solution.py:529
  22.6 5.5 %energy.1 = (bf16[8,256,1024]{2,1,0:T(8,128)(2,1)}, f32[1,256]{1,0:T(1,128)S(1)}) custom-call(bf16[256,256]{1,0:T(8,128)(2,1)S(1)} %bitcast.11, bf16[8,256,1024]{2,1,0:T(8,128)(2,1)} %get-tuple-element.47.unit_hbm.refs_0_), custom_call_target="tpu_custom_call" | custom-call | flops 1073741824 | bytes 8388608 | tf_op jit(solution)/shard_map/energy/pallas_call | solution.py:189
  28.2 1.6 %collective-permute-start.5 = (f32[1,256]{1,0:T(1,128)S(1)}, f32[1,256]{1,0:T(1,128)S(1)}, u32[]{:S(2)}, u32[]{:S(2)}) collective-permute-start(f32[1,256]{1,0:T(1,128)S(1)} %get-tuple-element.49), channel_id=1, source_target_pairs={{0,2},{1,3},{2,0},{3,1},{4,6},{5,7},{6,4},{7,5},{8,10},{9,11},{10,... | collective-permute-start | bytes 3080 | tf_op jit(solution)/shard_map/ppermute | solution.py:532
  29.8 0.3 collective-permute-start.6
  30.1 0.1 convert_element_type.52.pairs_ref
  30.2 2.0 %collective-permute-start.2 = (bf16[4,176,256]{2,1,0:T(8,128)(2,1)S(1)}, bf16[4,176,256]{2,1,0:T(8,128)(2,1)S(1)}, u32[]{:S(2)}, u32[]{:S(2)}) collective-permute-start(bf16[4,176,256]{2,1,0:T(8,128)(2,1)S(1)} %fusion.rest_ref), channel_id=1, source_target_pairs={{0,16},{4,20},{8,24},{12,28},{16,0},{20,4},{24,8},{28,12},{1,17},{... | collective-permute-start | bytes 1081352 | tf_op jit(solution)/shard_map/ppermute | solution.py:529
  32.2 0.6 collective-permute-done.6
  32.8 1.5 %collective-permute-start.7 = (f32[1,256]{1,0:T(1,128)S(1)}, f32[1,256]{1,0:T(1,128)S(1)}, u32[]{:S(2)}, u32[]{:S(2)}) collective-permute-start(f32[1,256]{1,0:T(1,128)S(1)} %add_add_fusion.5), channel_id=1, source_target_pairs={{0,4},{4,0},{8,12},{12,8},{16,20},{20,16},{24,28},{28,24},{1,5},{5... | collective-permute-start | bytes 3080 | tf_op jit(solution)/shard_map/ppermute | solution.py:529
  34.3 2.0 %collective-permute-start.9 = (f32[1,256]{1,0:T(1,128)S(1)}, f32[1,256]{1,0:T(1,128)S(1)}, u32[]{:S(2)}, u32[]{:S(2)}) collective-permute-start(f32[1,256]{1,0:T(1,128)S(1)} %add_add_fusion.5), channel_id=1, source_target_pairs={{0,12},{4,8},{8,4},{12,0},{16,28},{20,24},{24,20},{28,16},{1,13},{... | collective-permute-start | bytes 3080 | tf_op jit(solution)/shard_map/ppermute | solution.py:529
  36.3 9.1 %student_near.1 = (bf16[8,640,1024]{2,1,0:T(8,128)(2,1)}, f32[1,640]{1,0:T(1,128)S(1)}, bf16[256,640]{1,0:T(8,128)(2,1)S(1)}, f32[256,256]{1,0:T(8,128)S(1)}, f32[256,640]{1,0:T(8,128)S(1)}) custom-call(bf16[4,176,256]{2,1,0:T(8,128)(2,1)S(1)} %fusion.rest_ref, s32[1,640]{1,0:T(1,128)S(1)} %convert_element_type.52.pairs_ref, ...), custom_call_target="tpu_custom_call" | custom-call | flops 5368709120 | bytes 10485760 | tf_op jit(solution)/shard_map/student_near/pallas_call | solution.py:347
  45.4 3.4 %collective-permute-done.2.rest_ref = bf16[4,176,256]{2,1,0:T(8,128)(2,1)S(1)} collective-permute-done((bf16[4,176,256]{2,1,0:T(8,128)(2,1)S(1)}, bf16[4,176,256]{2,1,0:T(8,128)(2,1)S(1)}, u32[]{:S(2)}, u32[]{:S(2)}) %collective-permute-start.2) | collective-permute-done | bytes 360480 | tf_op jit(solution)/shard_map/ppermute | solution.py:529
  48.8 3.8 %iterate.1 = f32[1,256]{1,0:T(1,128)S(1)} custom-call(f32[1,256]{1,0:T(1,128)S(1)} %add_add_fusion.4.sum_in, bf16[8,256,1024]{2,1,0:T(8,128)(2,1)} %get-tuple-element.51.energy_hbm), custom_call_target="tpu_custom_call" | custom-call | flops 8388608 | bytes 8388608 | tf_op jit(solution)/shard_map/iterate/pallas_call | solution.py:273
  52.6 0.1 collective-permute-start.10
  52.7 1.6 %collective-permute-start.11 = (f32[1,256]{1,0:T(1,128)S(1)}, f32[1,256]{1,0:T(1,128)S(1)}, u32[]{:S(2)}, u32[]{:S(2)}) collective-permute-start(f32[1,256]{1,0:T(1,128)S(1)} %iterate.1), channel_id=1, source_target_pairs={{0,2},{1,3},{2,0},{3,1},{4,6},{5,7},{6,4},{7,5},{8,10},{9,11},{10,... | collective-permute-start | bytes 3080 | tf_op jit(solution)/shard_map/ppermute | solution.py:532
  54.3 0.3 collective-permute-start.12
  54.6 0.1 convert_element_type.55.pairs_ref
  54.7 1.6 %collective-permute-done.11 = f32[1,256]{1,0:T(1,128)S(1)} collective-permute-done((f32[1,256]{1,0:T(1,128)S(1)}, f32[1,256]{1,0:T(1,128)S(1)}, u32[]{:S(2)}, u32[]{:S(2)}) %collective-permute-start.11) | collective-permute-done | bytes 1056 | tf_op jit(solution)/shard_map/ppermute | solution.py:532
  56.3 1.0 collective-permute-done.12
  57.3 1.5 %collective-permute-start.13 = (f32[1,256]{1,0:T(1,128)S(1)}, f32[1,256]{1,0:T(1,128)S(1)}, u32[]{:S(2)}, u32[]{:S(2)}) collective-permute-start(f32[1,256]{1,0:T(1,128)S(1)} %add_add_fusion.3), channel_id=1, source_target_pairs={{0,4},{4,0},{8,12},{12,8},{16,20},{20,16},{24,28},{28,24},{1,5},{5... | collective-permute-start | bytes 3080 | tf_op jit(solution)/shard_map/ppermute | solution.py:529
  58.8 2.0 %collective-permute-start.15 = (f32[1,256]{1,0:T(1,128)S(1)}, f32[1,256]{1,0:T(1,128)S(1)}, u32[]{:S(2)}, u32[]{:S(2)}) collective-permute-start(f32[1,256]{1,0:T(1,128)S(1)} %add_add_fusion.3), channel_id=1, source_target_pairs={{0,12},{4,8},{8,4},{12,0},{16,28},{20,24},{24,20},{28,16},{1,13},{... | collective-permute-start | bytes 3080 | tf_op jit(solution)/shard_map/ppermute | solution.py:529
  60.7 6.7 %student_far.1 = (bf16[8,640,1024]{2,1,0:T(8,128)(2,1)}, f32[1,640]{1,0:T(1,128)S(1)}, bf16[256,640]{1,0:T(8,128)(2,1)S(1)}, f32[256,256]{1,0:T(8,128)S(1)}) custom-call(bf16[4,176,256]{2,1,0:T(8,128)(2,1)S(1)} %collective-permute-done.2.rest_ref, s32[1,640]{1,0:T(1,128)S(1)} %convert_element_type.55.pairs_ref, ...), custom_call_target="tpu_custom_call" | custom-call | flops 5368709120 | bytes 10485760 | tf_op jit(solution)/shard_map/student_far/pallas_call | solution.py:347
  67.5 7.1 %iterate_last.1 = (f32[1,1536]{1,0:T(1,128)S(1)}, f32[256,256]{1,0:T(8,128)S(1)}, bf16[8,256,1024]{2,1,0:T(8,128)(2,1)}) custom-call(f32[1,256]{1,0:T(1,128)S(1)} %add_add_fusion.2.sum_in, bf16[8,256,1024]{2,1,0:T(8,128)(2,1)} %get-tuple-element.51.energy_hbm, bf16[8,256,1024]{2,1,0:T(8,128)(2,1)} %get-tuple-element.47.unit_hbm.refs_0_, ...), custom_call_target="tpu_custom_call" | custom-call | flops 8388608 | bytes 8388608 | tf_op jit(solution)/shard_map/iterate_last/pallas_call | solution.py:273
  74.6 0.7 collective-permute-start.17
  75.3 1.1 collective-permute-start.18
  76.5 1.8 %collective-permute-done.17 = f32[1,1536]{1,0:T(1,128)S(1)} collective-permute-done((f32[1,1536]{1,0:T(1,128)S(1)}, f32[1,1536]{1,0:T(1,128)S(1)}, u32[]{:S(2)}, u32[]{:S(2)}) %collective-permute-start.17) | collective-permute-done | bytes 6176 | tf_op jit(solution)/shard_map/ppermute | solution.py:532
  78.4 1.6 %collective-permute-start.19 = (f32[1,1536]{1,0:T(1,128)S(1)}, f32[1,1536]{1,0:T(1,128)S(1)}, u32[]{:S(2)}, u32[]{:S(2)}) collective-permute-start(f32[1,1536]{1,0:T(1,128)S(1)} %add_add_fusion.1), channel_id=1, source_target_pairs={{0,4},{4,0},{8,12},{12,8},{16,20},{20,16},{24,28},{28,24},{1,5},{5... | collective-permute-start | bytes 18440 | tf_op jit(solution)/shard_map/ppermute | solution.py:529
  80.0 2.0 %collective-permute-start.21 = (f32[1,1536]{1,0:T(1,128)S(1)}, f32[1,1536]{1,0:T(1,128)S(1)}, u32[]{:S(2)}, u32[]{:S(2)}) collective-permute-start(f32[1,1536]{1,0:T(1,128)S(1)} %add_add_fusion.1), channel_id=1, source_target_pairs={{0,12},{4,8},{8,4},{12,0},{16,28},{20,24},{24,20},{28,16},{1,13},{... | collective-permute-start | bytes 18440 | tf_op jit(solution)/shard_map/ppermute | solution.py:529
  82.0 0.1 collective-permute-done.19
  82.1 1.5 %collective-permute-done.20 = f32[1,1536]{1,0:T(1,128)S(1)} collective-permute-done((f32[1,1536]{1,0:T(1,128)S(1)}, f32[1,1536]{1,0:T(1,128)S(1)}, u32[]{:S(2)}, u32[]{:S(2)}) %collective-permute-start.20) | collective-permute-done | bytes 6176 | tf_op jit(solution)/shard_map/ppermute | solution.py:529
  83.6 0.9 collective-permute-done.21
  84.5 8.6 %head.2 = (f32[32,32768]{1,0:T(8,128)}, bf16[32,4096]{1,0:T(8,128)(2,1)S(1)}, bf16[32,4096]{1,0:T(8,128)(2,1)S(1)}, bf16[32,4096]{1,0:T(8,128)(2,1)S(1)}, f32[12...) custom-call(s32[4]{0:T(128)S(1)} %pad_add_fusion.place, f32[1,1536]{1,0:T(1,128)S(1)} %add_add_fusion.both_ref, ...), custom_call_target="tpu_custom_call" | custom-call | flops 6442450944 | bytes 14680064 | tf_op jit(solution)/shard_map/head/pallas_call | solution.py:472
  93.1 1.4 %collective-permute-start.28 = (f32[136,640]{1,0:T(8,128)S(1)}, f32[136,640]{1,0:T(8,128)S(1)}, u32[]{:S(2)}, u32[]{:S(2)}) collective-permute-start(f32[136,640]{1,0:T(8,128)S(1)} %get-tuple-element.81), channel_id=1, source_target_pairs={{0,2},{1,3},{2,0},{3,1},{4,6},{5,7},{6,4},{7,5},{8,10},{9,11},{10,... | collective-permute-start | bytes 1044488 | tf_op jit(solution)/shard_map/ppermute | solution.py:532
  94.6 2.0 %collective-permute-start.24 = (bf16[32,4096]{1,0:T(8,128)(2,1)S(1)}, bf16[32,4096]{1,0:T(8,128)(2,1)S(1)}, u32[]{:S(2)}, u32[]{:S(2)}) collective-permute-start(bf16[32,4096]{1,0:T(8,128)(2,1)S(1)} %get-tuple-element.75), channel_id=1, source_target_pairs={{0,12},{4,8},{8,4},{12,0},{16,28},{20,24},{24,20},{28,16},{1,13},{... | collective-permute-start | bytes 786440 | tf_op jit(solution)/shard_map/ppermute | solution.py:529
  96.6 0.1 collective-permute-start.23
  96.7 1.4 %collective-permute-start.22 = (bf16[32,4096]{1,0:T(8,128)(2,1)S(1)}, bf16[32,4096]{1,0:T(8,128)(2,1)S(1)}, u32[]{:S(2)}, u32[]{:S(2)}) collective-permute-start(bf16[32,4096]{1,0:T(8,128)(2,1)S(1)} %get-tuple-element.69), channel_id=1, source_target_pairs={{0,4},{4,0},{8,12},{12,8},{16,20},{20,16},{24,28},{28,24},{1,5},{5... | collective-permute-start | bytes 786440 | tf_op jit(solution)/shard_map/ppermute | solution.py:529
  98.1 8.3 %head.3 = (f32[32,32768]{1,0:T(8,128)}, bf16[32,4096]{1,0:T(8,128)(2,1)S(1)}, bf16[32,4096]{1,0:T(8,128)(2,1)S(1)}, bf16[32,4096]{1,0:T(8,128)(2,1)S(1)}) custom-call(s32[4]{0:T(128)S(1)} %pad_add_fusion.place, f32[1,1536]{1,0:T(1,128)S(1)} %add_add_fusion.both_ref, ...), custom_call_target="tpu_custom_call", output_to_operand_aliasing={{0}: (12, {})} | custom-call | flops 6442450944 | bytes 14680064 | tf_op jit(solution)/shard_map/head/pallas_call | solution.py:472
  106.5 0.1 constant_dynamic-slice_fusion.1.denom_ref
  106.5 0.4 collective-permute-done.23
  107.0 0.8 collective-permute-done.22
  107.8 0.6 collective-permute-start.25
  108.4 1.7 %collective-permute-start.26 = (bf16[32,4096]{1,0:T(8,128)(2,1)S(1)}, bf16[32,4096]{1,0:T(8,128)(2,1)S(1)}, u32[]{:S(2)}, u32[]{:S(2)}) collective-permute-start(bf16[32,4096]{1,0:T(8,128)(2,1)S(1)} %get-tuple-element.78), channel_id=1, source_target_pairs={{0,8},{4,12},{8,0},{12,4},{16,24},{20,28},{24,16},{28,20},{1,9},{5... | collective-permute-start | bytes 786440 | tf_op jit(solution)/shard_map/ppermute | solution.py:529
  110.1 1.1 collective-permute-start.27
  111.3 0.8 convert_dynamic-update-slice_fusion.5
  112.1 0.8 convert_dynamic-update-slice_fusion.4
  112.9 0.8 convert_dynamic-update-slice_fusion.3
  113.9 2.2 %collective-permute-done.25 = bf16[32,4096]{1,0:T(8,128)(2,1)S(1)} collective-permute-done((bf16[32,4096]{1,0:T(8,128)(2,1)S(1)}, bf16[32,4096]{1,0:T(8,128)(2,1)S(1)}, u32[]{:S(2)}, u32[]{:S(2)}) %collective-permute-start.25) | collective-permute-done | bytes 262176 | tf_op jit(solution)/shard_map/ppermute | solution.py:529
  116.1 0.8 convert_dynamic-update-slice_fusion.2
  116.9 0.7 collective-permute-done.26
  117.6 0.8 convert_dynamic-update-slice_fusion.1
  118.5 0.2 fusion.1
  118.7 1.5 %collective-permute-start.30 = (f32[72,160]{1,0:T(8,128)S(1)}, f32[72,160]{1,0:T(8,128)S(1)}, u32[]{:S(2)}, u32[]{:S(2)}) collective-permute-start(f32[72,160]{1,0:T(8,128)S(1)} %get-tuple-element.91), channel_id=1, source_target_pairs={{0,4},{4,0},{8,12},{12,8},{16,20},{20,16},{24,28},{28,24},{1,5},{5... | collective-permute-start | bytes 138248 | tf_op jit(solution)/shard_map/ppermute | solution.py:529
  120.2 1.7 %collective-permute-start.31 = (f32[72,160]{1,0:T(8,128)S(1)}, f32[72,160]{1,0:T(8,128)S(1)}, u32[]{:S(2)}, u32[]{:S(2)}) collective-permute-start(f32[72,160]{1,0:T(8,128)S(1)} %get-tuple-element.92), channel_id=1, source_target_pairs={{0,8},{4,12},{8,0},{12,4},{16,24},{20,28},{24,16},{28,20},{1,9},{5... | collective-permute-start | bytes 138248 | tf_op jit(solution)/shard_map/ppermute | solution.py:529
  121.9 0.3 collective-permute-start.32
  122.3 1.9 %collective-permute-done.27 = bf16[32,4096]{1,0:T(8,128)(2,1)S(1)} collective-permute-done((bf16[32,4096]{1,0:T(8,128)(2,1)S(1)}, bf16[32,4096]{1,0:T(8,128)(2,1)S(1)}, u32[]{:S(2)}, u32[]{:S(2)}) %collective-permute-start.27) | collective-permute-done | bytes 262176 | tf_op jit(solution)/shard_map/ppermute | solution.py:529
  124.2 0.8 convert_dynamic-update-slice_fusion
  125.0 2.1 %collective-permute-done.32.refs_3_ = f32[72,160]{1,0:T(8,128)S(1)} collective-permute-done((f32[72,160]{1,0:T(8,128)S(1)}, f32[72,160]{1,0:T(8,128)S(1)}, u32[]{:S(2)}, u32[]{:S(2)}) %collective-permute-start.32) | collective-permute-done | bytes 46112 | tf_op jit(solution)/shard_map/ppermute | solution.py:529
  127.2 1.4 %finish.1 = (f32[64,160]{1,0:T(8,128)}, f32[1,160]{1,0:T(1,128)}) custom-call(s32[4]{0:T(128)S(1)} %pad_add_fusion.place, f32[1,1536]{1,0:T(1,128)S(1)} %add_add_fusion.both_ref, f32[1,160]{1,0:T(1,128)S(1)} %constant_dynamic-slice_fusion.1.denom_ref, s32[1,160]{1,0:T(1,128)S(1)} %bitcast.13, bf16[160,256]{1,0:T(8,128)(2,1)S(1)} %copy-done, ...), custom_call_target="tpu_custom_call" | custom-call | tf_op jit(solution)/shard_map/finish/pallas_call | solution.py:504
  (52 shorter events, 0.8 us)
Async XLA Ops:
  2.3 6.1 %collective-permute-start = (bf16[1,208,256]{2,1,0:T(8,128)(2,1)}, bf16[1,208,256]{2,1,0:T(8,128)(2,1)S(1)}, u32[]{:S(2)}, u32[]{:S(2)}) collective-permute-start(bf16[1,208,256]{2,1,0:T(8,128)(2,1)} %bitcast.14), channel_id=1, source_target_pairs={{0,4},{4,0},{8,12},{12,8},{16,20},{20,16},{24,28},{28,24},{1,5},{5... | collective-permute-start | bytes 319496 | tf_op jit(solution)/shard_map/ppermute | solution.py:529
  9.4 7.3 %collective-permute-start.1 = (bf16[2,208,256]{2,1,0:T(8,128)(2,1)S(1)}, bf16[2,208,256]{2,1,0:T(8,128)(2,1)S(1)}, u32[]{:S(2)}, u32[]{:S(2)}) collective-permute-start(bf16[2,208,256]{2,1,0:T(8,128)(2,1)S(1)} %pad_maximum_fusion), channel_id=1, source_target_pairs={{0,8},{4,12},{8,0},{12,4},{16,24},{20,28},{24,16},{28,20},{1,9},{5... | collective-permute-start | bytes 638984 | tf_op jit(solution)/shard_map/ppermute | solution.py:529
  16.8 5.8 %collective-permute-start.3 = (bf16[4,32,256]{2,1,0:T(8,128)(2,1)S(1)}, bf16[4,32,256]{2,1,0:T(8,128)(2,1)S(1)}, u32[]{:S(2)}, u32[]{:S(2)}) collective-permute-start(bf16[4,32,256]{2,1,0:T(8,128)(2,1)S(1)} %pad_maximum_fusion.3), channel_id=1, source_target_pairs={{0,16},{4,20},{8,24},{12,28},{16,0},{20,4},{24,8},{28,12},{1,17},{... | collective-permute-start | bytes 196616 | tf_op jit(solution)/shard_map/ppermute | solution.py:529
  28.1 4.1 %collective-permute-start.4 = (f32[1,256]{1,0:T(1,128)S(1)}, f32[1,256]{1,0:T(1,128)S(1)}, u32[]{:S(2)}, u32[]{:S(2)}) collective-permute-start(f32[1,256]{1,0:T(1,128)S(1)} %get-tuple-element.49), channel_id=1, source_target_pairs={{0,1},{1,0},{2,3},{3,2},{4,5},{5,4},{6,7},{7,6},{8,9},{9,8},{10,11... | collective-permute-start | bytes 3080 | tf_op jit(solution)/shard_map/ppermute | solution.py:532
  28.2 4.0 %collective-permute-start.5 = (f32[1,256]{1,0:T(1,128)S(1)}, f32[1,256]{1,0:T(1,128)S(1)}, u32[]{:S(2)}, u32[]{:S(2)}) collective-permute-start(f32[1,256]{1,0:T(1,128)S(1)} %get-tuple-element.49), channel_id=1, source_target_pairs={{0,2},{1,3},{2,0},{3,1},{4,6},{5,7},{6,4},{7,5},{8,10},{9,11},{10,... | collective-permute-start | bytes 3080 | tf_op jit(solution)/shard_map/ppermute | solution.py:532
  29.8 3.0 %collective-permute-start.6 = (f32[1,256]{1,0:T(1,128)S(1)}, f32[1,256]{1,0:T(1,128)S(1)}, u32[]{:S(2)}, u32[]{:S(2)}) collective-permute-start(f32[1,256]{1,0:T(1,128)S(1)} %get-tuple-element.49), channel_id=1, source_target_pairs={{0,3},{1,2},{2,1},{3,0},{4,7},{5,6},{6,5},{7,4},{8,11},{9,10},{10,... | collective-permute-start | bytes 3080 | tf_op jit(solution)/shard_map/ppermute | solution.py:532
  30.2 18.7 %collective-permute-start.2 = (bf16[4,176,256]{2,1,0:T(8,128)(2,1)S(1)}, bf16[4,176,256]{2,1,0:T(8,128)(2,1)S(1)}, u32[]{:S(2)}, u32[]{:S(2)}) collective-permute-start(bf16[4,176,256]{2,1,0:T(8,128)(2,1)S(1)} %fusion.rest_ref), channel_id=1, source_target_pairs={{0,16},{4,20},{8,24},{12,28},{16,0},{20,4},{24,8},{28,12},{1,17},{... | collective-permute-start | bytes 1081352 | tf_op jit(solution)/shard_map/ppermute | solution.py:529
  32.8 12.6 %collective-permute-start.7 = (f32[1,256]{1,0:T(1,128)S(1)}, f32[1,256]{1,0:T(1,128)S(1)}, u32[]{:S(2)}, u32[]{:S(2)}) collective-permute-start(f32[1,256]{1,0:T(1,128)S(1)} %add_add_fusion.5), channel_id=1, source_target_pairs={{0,4},{4,0},{8,12},{12,8},{16,20},{20,16},{24,28},{28,24},{1,5},{5... | collective-permute-start | bytes 3080 | tf_op jit(solution)/shard_map/ppermute | solution.py:529
  34.3 11.1 %collective-permute-start.8 = (f32[1,256]{1,0:T(1,128)S(1)}, f32[1,256]{1,0:T(1,128)S(1)}, u32[]{:S(2)}, u32[]{:S(2)}) collective-permute-start(f32[1,256]{1,0:T(1,128)S(1)} %add_add_fusion.5), channel_id=1, source_target_pairs={{0,8},{4,12},{8,0},{12,4},{16,24},{20,28},{24,16},{28,20},{1,9},{5... | collective-permute-start | bytes 3080 | tf_op jit(solution)/shard_map/ppermute | solution.py:529
  34.3 11.1 %collective-permute-start.9 = (f32[1,256]{1,0:T(1,128)S(1)}, f32[1,256]{1,0:T(1,128)S(1)}, u32[]{:S(2)}, u32[]{:S(2)}) collective-permute-start(f32[1,256]{1,0:T(1,128)S(1)} %add_add_fusion.5), channel_id=1, source_target_pairs={{0,12},{4,8},{8,4},{12,0},{16,28},{20,24},{24,20},{28,16},{1,13},{... | collective-permute-start | bytes 3080 | tf_op jit(solution)/shard_map/ppermute | solution.py:529
  52.6 2.1 %collective-permute-start.10 = (f32[1,256]{1,0:T(1,128)S(1)}, f32[1,256]{1,0:T(1,128)S(1)}, u32[]{:S(2)}, u32[]{:S(2)}) collective-permute-start(f32[1,256]{1,0:T(1,128)S(1)} %iterate.1), channel_id=1, source_target_pairs={{0,1},{1,0},{2,3},{3,2},{4,5},{5,4},{6,7},{7,6},{8,9},{9,8},{10,11... | collective-permute-start | bytes 3080 | tf_op jit(solution)/shard_map/ppermute | solution.py:532
  52.7 3.6 %collective-permute-start.11 = (f32[1,256]{1,0:T(1,128)S(1)}, f32[1,256]{1,0:T(1,128)S(1)}, u32[]{:S(2)}, u32[]{:S(2)}) collective-permute-start(f32[1,256]{1,0:T(1,128)S(1)} %iterate.1), channel_id=1, source_target_pairs={{0,2},{1,3},{2,0},{3,1},{4,6},{5,7},{6,4},{7,5},{8,10},{9,11},{10,... | collective-permute-start | bytes 3080 | tf_op jit(solution)/shard_map/ppermute | solution.py:532
  54.3 3.0 %collective-permute-start.12 = (f32[1,256]{1,0:T(1,128)S(1)}, f32[1,256]{1,0:T(1,128)S(1)}, u32[]{:S(2)}, u32[]{:S(2)}) collective-permute-start(f32[1,256]{1,0:T(1,128)S(1)} %iterate.1), channel_id=1, source_target_pairs={{0,3},{1,2},{2,1},{3,0},{4,7},{5,6},{6,5},{7,4},{8,11},{9,10},{10,... | collective-permute-start | bytes 3080 | tf_op jit(solution)/shard_map/ppermute | solution.py:532
  57.3 10.2 %collective-permute-start.13 = (f32[1,256]{1,0:T(1,128)S(1)}, f32[1,256]{1,0:T(1,128)S(1)}, u32[]{:S(2)}, u32[]{:S(2)}) collective-permute-start(f32[1,256]{1,0:T(1,128)S(1)} %add_add_fusion.3), channel_id=1, source_target_pairs={{0,4},{4,0},{8,12},{12,8},{16,20},{20,16},{24,28},{28,24},{1,5},{5... | collective-permute-start | bytes 3080 | tf_op jit(solution)/shard_map/ppermute | solution.py:529
  58.8 8.7 %collective-permute-start.14 = (f32[1,256]{1,0:T(1,128)S(1)}, f32[1,256]{1,0:T(1,128)S(1)}, u32[]{:S(2)}, u32[]{:S(2)}) collective-permute-start(f32[1,256]{1,0:T(1,128)S(1)} %add_add_fusion.3), channel_id=1, source_target_pairs={{0,8},{4,12},{8,0},{12,4},{16,24},{20,28},{24,16},{28,20},{1,9},{5... | collective-permute-start | bytes 3080 | tf_op jit(solution)/shard_map/ppermute | solution.py:529
  58.8 8.7 %collective-permute-start.15 = (f32[1,256]{1,0:T(1,128)S(1)}, f32[1,256]{1,0:T(1,128)S(1)}, u32[]{:S(2)}, u32[]{:S(2)}) collective-permute-start(f32[1,256]{1,0:T(1,128)S(1)} %add_add_fusion.3), channel_id=1, source_target_pairs={{0,12},{4,8},{8,4},{12,0},{16,28},{20,24},{24,20},{28,16},{1,13},{... | collective-permute-start | bytes 3080 | tf_op jit(solution)/shard_map/ppermute | solution.py:529
  74.6 1.9 %collective-permute-start.16 = (f32[1,1536]{1,0:T(1,128)S(1)}, f32[1,1536]{1,0:T(1,128)S(1)}, u32[]{:S(2)}, u32[]{:S(2)}) collective-permute-start(f32[1,1536]{1,0:T(1,128)S(1)} %get-tuple-element.55), channel_id=1, source_target_pairs={{0,1},{1,0},{2,3},{3,2},{4,5},{5,4},{6,7},{7,6},{8,9},{9,8},{10,11... | collective-permute-start | bytes 18440 | tf_op jit(solution)/shard_map/ppermute | solution.py:532
  74.6 3.7 %collective-permute-start.17 = (f32[1,1536]{1,0:T(1,128)S(1)}, f32[1,1536]{1,0:T(1,128)S(1)}, u32[]{:S(2)}, u32[]{:S(2)}) collective-permute-start(f32[1,1536]{1,0:T(1,128)S(1)} %get-tuple-element.55), channel_id=1, source_target_pairs={{0,2},{1,3},{2,0},{3,1},{4,6},{5,7},{6,4},{7,5},{8,10},{9,11},{10,... | collective-permute-start | bytes 18440 | tf_op jit(solution)/shard_map/ppermute | solution.py:532
  75.3 3.1 %collective-permute-start.18 = (f32[1,1536]{1,0:T(1,128)S(1)}, f32[1,1536]{1,0:T(1,128)S(1)}, u32[]{:S(2)}, u32[]{:S(2)}) collective-permute-start(f32[1,1536]{1,0:T(1,128)S(1)} %get-tuple-element.55), channel_id=1, source_target_pairs={{0,3},{1,2},{2,1},{3,0},{4,7},{5,6},{6,5},{7,4},{8,11},{9,10},{10,... | collective-permute-start | bytes 18440 | tf_op jit(solution)/shard_map/ppermute | solution.py:532
  78.4 3.7 %collective-permute-start.19 = (f32[1,1536]{1,0:T(1,128)S(1)}, f32[1,1536]{1,0:T(1,128)S(1)}, u32[]{:S(2)}, u32[]{:S(2)}) collective-permute-start(f32[1,1536]{1,0:T(1,128)S(1)} %add_add_fusion.1), channel_id=1, source_target_pairs={{0,4},{4,0},{8,12},{12,8},{16,20},{20,16},{24,28},{28,24},{1,5},{5... | collective-permute-start | bytes 18440 | tf_op jit(solution)/shard_map/ppermute | solution.py:529
  80.0 3.6 %collective-permute-start.20 = (f32[1,1536]{1,0:T(1,128)S(1)}, f32[1,1536]{1,0:T(1,128)S(1)}, u32[]{:S(2)}, u32[]{:S(2)}) collective-permute-start(f32[1,1536]{1,0:T(1,128)S(1)} %add_add_fusion.1), channel_id=1, source_target_pairs={{0,8},{4,12},{8,0},{12,4},{16,24},{20,28},{24,16},{28,20},{1,9},{5... | collective-permute-start | bytes 18440 | tf_op jit(solution)/shard_map/ppermute | solution.py:529
  80.0 4.5 %collective-permute-start.21 = (f32[1,1536]{1,0:T(1,128)S(1)}, f32[1,1536]{1,0:T(1,128)S(1)}, u32[]{:S(2)}, u32[]{:S(2)}) collective-permute-start(f32[1,1536]{1,0:T(1,128)S(1)} %add_add_fusion.1), channel_id=1, source_target_pairs={{0,12},{4,8},{8,4},{12,0},{16,28},{20,24},{24,20},{28,16},{1,13},{... | collective-permute-start | bytes 18440 | tf_op jit(solution)/shard_map/ppermute | solution.py:529
  93.1 20.6 %collective-permute-start.28 = (f32[136,640]{1,0:T(8,128)S(1)}, f32[136,640]{1,0:T(8,128)S(1)}, u32[]{:S(2)}, u32[]{:S(2)}) collective-permute-start(f32[136,640]{1,0:T(8,128)S(1)} %get-tuple-element.81), channel_id=1, source_target_pairs={{0,2},{1,3},{2,0},{3,1},{4,6},{5,7},{6,4},{7,5},{8,10},{9,11},{10,... | collective-permute-start | bytes 1044488 | tf_op jit(solution)/shard_map/ppermute | solution.py:532
  94.6 11.9 %collective-permute-start.24 = (bf16[32,4096]{1,0:T(8,128)(2,1)S(1)}, bf16[32,4096]{1,0:T(8,128)(2,1)S(1)}, u32[]{:S(2)}, u32[]{:S(2)}) collective-permute-start(bf16[32,4096]{1,0:T(8,128)(2,1)S(1)} %get-tuple-element.75), channel_id=1, source_target_pairs={{0,12},{4,8},{8,4},{12,0},{16,28},{20,24},{24,20},{28,16},{1,13},{... | collective-permute-start | bytes 786440 | tf_op jit(solution)/shard_map/ppermute | solution.py:529
  96.6 10.4 %collective-permute-start.23 = (bf16[32,4096]{1,0:T(8,128)(2,1)S(1)}, bf16[32,4096]{1,0:T(8,128)(2,1)S(1)}, u32[]{:S(2)}, u32[]{:S(2)}) collective-permute-start(bf16[32,4096]{1,0:T(8,128)(2,1)S(1)} %get-tuple-element.72), channel_id=1, source_target_pairs={{0,8},{4,12},{8,0},{12,4},{16,24},{20,28},{24,16},{28,20},{1,9},{5... | collective-permute-start | bytes 786440 | tf_op jit(solution)/shard_map/ppermute | solution.py:529
  96.7 11.1 %collective-permute-start.22 = (bf16[32,4096]{1,0:T(8,128)(2,1)S(1)}, bf16[32,4096]{1,0:T(8,128)(2,1)S(1)}, u32[]{:S(2)}, u32[]{:S(2)}) collective-permute-start(bf16[32,4096]{1,0:T(8,128)(2,1)S(1)} %get-tuple-element.69), channel_id=1, source_target_pairs={{0,4},{4,0},{8,12},{12,8},{16,20},{20,16},{24,28},{28,24},{1,5},{5... | collective-permute-start | bytes 786440 | tf_op jit(solution)/shard_map/ppermute | solution.py:529
  106.4 20.7 %copy-start = (bf16[160,256]{1,0:T(8,128)(2,1)S(1)}, bf16[160,256]{1,0:T(8,128)(2,1)}, u32[]{:S(2)}) copy-start(bf16[160,256]{1,0:T(8,128)(2,1)} %stud_ref.3) | copy-start | bytes 245764
  106.4 20.7 %copy-start.1 = (s32[160]{0:T(256)S(1)}, s32[160]{0:T(256)}, u32[]{:S(2)}) copy-start(s32[160]{0:T(256)} %param.7) | copy-start | bytes 1924
  107.8 8.3 %collective-permute-start.25 = (bf16[32,4096]{1,0:T(8,128)(2,1)S(1)}, bf16[32,4096]{1,0:T(8,128)(2,1)S(1)}, u32[]{:S(2)}, u32[]{:S(2)}) collective-permute-start(bf16[32,4096]{1,0:T(8,128)(2,1)S(1)} %get-tuple-element.77), channel_id=1, source_target_pairs={{0,4},{4,0},{8,12},{12,8},{16,20},{20,16},{24,28},{28,24},{1,5},{5... | collective-permute-start | bytes 786440 | tf_op jit(solution)/shard_map/ppermute | solution.py:529
  108.4 9.2 %collective-permute-start.26 = (bf16[32,4096]{1,0:T(8,128)(2,1)S(1)}, bf16[32,4096]{1,0:T(8,128)(2,1)S(1)}, u32[]{:S(2)}, u32[]{:S(2)}) collective-permute-start(bf16[32,4096]{1,0:T(8,128)(2,1)S(1)} %get-tuple-element.78), channel_id=1, source_target_pairs={{0,8},{4,12},{8,0},{12,4},{16,24},{20,28},{24,16},{28,20},{1,9},{5... | collective-permute-start | bytes 786440 | tf_op jit(solution)/shard_map/ppermute | solution.py:529
  110.1 14.1 %collective-permute-start.27 = (bf16[32,4096]{1,0:T(8,128)(2,1)S(1)}, bf16[32,4096]{1,0:T(8,128)(2,1)S(1)}, u32[]{:S(2)}, u32[]{:S(2)}) collective-permute-start(bf16[32,4096]{1,0:T(8,128)(2,1)S(1)} %get-tuple-element.79), channel_id=1, source_target_pairs={{0,12},{4,8},{8,4},{12,0},{16,28},{20,24},{24,20},{28,16},{1,13},{... | collective-permute-start | bytes 786440 | tf_op jit(solution)/shard_map/ppermute | solution.py:529
  113.9 4.6 %collective-permute-start.29 = (f32[72,640]{1,0:T(8,128)S(1)}, f32[72,640]{1,0:T(8,128)S(1)}, u32[]{:S(2)}, u32[]{:S(2)}) collective-permute-start(f32[72,640]{1,0:T(8,128)S(1)} %pad_maximum_fusion.1), channel_id=1, source_target_pairs={{0,1},{1,0},{2,3},{3,2},{4,5},{5,4},{6,7},{7,6},{8,9},{9,8},{10,11... | collective-permute-start | bytes 552968 | tf_op jit(solution)/shard_map/ppermute | solution.py:532
  118.7 6.3 %collective-permute-start.30 = (f32[72,160]{1,0:T(8,128)S(1)}, f32[72,160]{1,0:T(8,128)S(1)}, u32[]{:S(2)}, u32[]{:S(2)}) collective-permute-start(f32[72,160]{1,0:T(8,128)S(1)} %get-tuple-element.91), channel_id=1, source_target_pairs={{0,4},{4,0},{8,12},{12,8},{16,20},{20,16},{24,28},{28,24},{1,5},{5... | collective-permute-start | bytes 138248 | tf_op jit(solution)/shard_map/ppermute | solution.py:529
  120.2 4.8 %collective-permute-start.31 = (f32[72,160]{1,0:T(8,128)S(1)}, f32[72,160]{1,0:T(8,128)S(1)}, u32[]{:S(2)}, u32[]{:S(2)}) collective-permute-start(f32[72,160]{1,0:T(8,128)S(1)} %get-tuple-element.92), channel_id=1, source_target_pairs={{0,8},{4,12},{8,0},{12,4},{16,24},{20,28},{24,16},{28,20},{1,9},{5... | collective-permute-start | bytes 138248 | tf_op jit(solution)/shard_map/ppermute | solution.py:529
  121.9 5.3 %collective-permute-start.32 = (f32[72,160]{1,0:T(8,128)S(1)}, f32[72,160]{1,0:T(8,128)S(1)}, u32[]{:S(2)}, u32[]{:S(2)}) collective-permute-start(f32[72,160]{1,0:T(8,128)S(1)} %get-tuple-element.89), channel_id=1, source_target_pairs={{0,12},{4,8},{8,4},{12,0},{16,28},{20,24},{24,20},{28,16},{1,13},{... | collective-permute-start | bytes 138248 | tf_op jit(solution)/shard_map/ppermute | solution.py:529

commit v4 on v3

--- a/solution.py
+++ b/solution.py
@@ -546,35 +546,38 @@
 
     own_pairs = pairing.reshape(1, s_dev)
     unit, inv = unit_call(place, v, kl)
-    packed = prepare_call(teacher_features, student_features, own_pairs)[None]
-    packed = join(packed, 1)
-    other, unit, inv = lax.optimization_barrier((swap_rows(packed, 2), unit, inv))
-    packed = join(packed, 2, other)
+    packed = prepare_call(teacher_features, student_features, own_pairs)
+    blocks = [packed] + [swap_rows(packed, n) for n in range(1, GROUP)]
+    blocks[-1], unit, inv = lax.optimization_barrier((blocks[-1], unit, inv))
+    for n in (1, 2):
+        low = (at // n) % 2 == 0
+        blocks = [jnp.where(low, blocks[j], blocks[j ^ n]) for j in range(GROUP)]
+    packed = jnp.stack(blocks)
     teach_all, near = packed[:, :t_dev], packed[:, t_dev:]
-    n = GROUP
-    while n < n_rows:
-        teach_all = join(teach_all, n)
-        n *= 2
-    teach_all = teach_all.reshape(t, d)
 
     def pairs_of(rest):
         digits = rest[:, s_dev : s_dev + 2, :s_dev].astype(F32)
         return (digits[:, 0] * 64.0 + digits[:, 1]).astype(jnp.int32).reshape(1, -1)
 
-    energy, sums = energy_call(teach_all, unit, total_k)
-    far = swap_rows(near, GROUP)
+    near_pairs = pairs_of(near)
+    expo_near, denom_near, near_t, weight, pull = student_call(near, near_pairs, unit, t, True)
+    n = GROUP
+    while n < n_rows:
+        other = swap_rows(teach_all, n)
+        teach_all = join(teach_all, n, other)
+        n *= 2
+    far = swap_rows(lax.optimization_barrier((near, other))[0], GROUP)
     n = 2 * GROUP
     while n < n_rows:
         far = jnp.concatenate([far, swap_rows(jnp.concatenate([near, far], axis=0), n)], axis=0)
         n *= 2
-    near_pairs = pairs_of(near)
-    expo_near, denom_near, near_t, weight, pull = student_call(near, near_pairs, unit, t, True)
-    sums = total(sums)
-    far, denom_near, sums = lax.optimization_barrier((far, denom_near, sums))
+    energy, sums = energy_call(teach_all.reshape(t, d), unit, total_k)
+    sums = lax.optimization_barrier((total(sums), denom_near))[0]
     far_pairs = pairs_of(far)
     expo_far, denom_far, far_t, more_weight = student_call(far, far_pairs, unit, t, False)
     pairs = jnp.concatenate([near_pairs, far_pairs], axis=1)
     (sums,) = iterate_call(sums, energy, total_k)
+    sums = lax.optimization_barrier((sums, far))[0]
     both, mean, scaled = iterate_call(total(sums), energy, total_k, (unit, denom_near, denom_far))
     both = total(both)
     students = (expo_near, expo_far, near_t, far_t, weight, more_weight)
@@ -597,12 +600,6 @@
                 share, pieces[-1][n - 1] = lax.optimization_barrier((share, pieces[-1][n - 1]))
             arrived.append(swap_rows(share, n))
         pieces.append(arrived)
-    proto_grad = out[0]
-    for part, arrived in enumerate(pieces):
-        for n, got in enumerate(arrived, 1):
-            start = (at ^ n) * kl + part * (kl // PARTS)
-            proto_grad = lax.dynamic_update_slice(proto_grad, got.astype(F32), (0, start))
-
     n = n_proto // 2
     while n >= 1:
         if n < n_proto // 2:
@@ -621,6 +618,12 @@
         return lax.dynamic_slice_in_dim(terms, (at ^ n) * s_dev, s_dev, 1)
 
     parts = [block(0)] + [swap_rows(block(n), n) for n in range(1, GROUP)]
+    pieces[-1] = lax.optimization_barrier((pieces[-1], parts))[0]
+    proto_grad = out[0]
+    for part, arrived in enumerate(pieces):
+        for n, got in enumerate(arrived, 1):
+            start = (at ^ n) * kl + part * (kl // PARTS)
+            proto_grad = lax.dynamic_update_slice(proto_grad, got.astype(F32), (0, start))
     own = lax.dynamic_slice_in_dim(both, t + at * s_dev, s_dev, 1)
     student_grad, loss = finish_call(t, place, both, own, own_pairs, student_features, parts, d // n_proto)
     return (proto_grad, student_grad.T, loss.reshape(s_dev))

time: 129 us -> 121 us (0.938)
  waiting for transfers between devices: 25.5 us -> 19.6 us
  starting transfers between devices: 37.9 us -> 36.3 us
    ppermute x22 -> x23, waiting for transfers between devices: 20.5 us -> 14.5 us  [swap_rows(): return lax.ppermute(x, 'rows', [(j, j ^ n) for j in range(n_rows)])]
    ppermute x22 -> x23, starting transfers between devices: 30.6 us -> 29 us  [swap_rows(): return lax.ppermute(x, 'rows', [(j, j ^ n) for j in range(n_rows)])]
  transfers between devices with their start and end apart: 33 -> 34, of which waited for: 17 -> 14; matrix products, arithmetic and copies ran while one was open for 4% -> 3% of each run, Pallas kernels for 23% -> 28%
where the time goes in v4:
time: 121 us; the launch traced here: 120 us
  Pallas kernels  57.3 us (47%)
  starting transfers between devices  36.3 us (30%)
  waiting for transfers between devices  19.6 us (16%)
  other arithmetic  5.59 us (5%)
    ppermute x23, starting transfers between devices, swap_rows(): return lax.ppermute(x, 'rows', [(j, j ^ n) for j in range(n_rows)])  29 us
    pallas_call x2, Pallas kernels, head_call(): pl.pallas_call(functools.partial(head_kernel, factor, first), out_shape=o...  16.9 us
    pallas_call x2, Pallas kernels, student_call(): pl.pallas_call(functools.partial(student_kernel, 2 * (rest.shape[1] - 16)...  15.8 us
    ppermute x23, waiting for transfers between devices, swap_rows(): return lax.ppermute(x, 'rows', [(j, j ^ n) for j in range(n_rows)])  14.5 us
    pallas_call x2, Pallas kernels, iterate_call(): pl.pallas_call(functools.partial(iterate_kernel, float(total_k), last), o...  10.8 us
    ppermute x11, starting transfers between devices, swap_proto(): return lax.ppermute(x, 'proto', [(j, j ^ n) for j in range(n_proto)])  7.3 us
    pallas_call x1, Pallas kernels, energy_call(): pl.pallas_call(functools.partial(energy_kernel, float(total_k)), out_shap...  5.47 us
    pallas_call x1, Pallas kernels, unit_call(): pl.pallas_call(unit_kernel, out_shape=(jax.ShapeDtypeStruct(shape, BF16),...  5.31 us
  transfers between devices with their start and end apart: 34, of which 14 were waited for; matrix products, arithmetic and copies ran while one was open for 3% of the time, Pallas kernels for 28%

profile of v4, /device:TPU:0, one launch (start us, length us, event | category | flops | bytes accessed | tf_op | source)
XLA Modules:
  0.0 120.1 jit_solution(9199041918657180070)
XLA Ops:
  0.6 1.7 %prepare.1 = bf16[208,256]{1,0:T(8,128)(2,1)} custom-call(bf16[32,256]{1,0:T(8,128)(2,1)} %teach_ref.1, bf16[160,256]{1,0:T(8,128)(2,1)} %stud_ref.3, s32[1,160]{1,0:T(1,128)} %bitcast.17), custom_call_target="tpu_custom_call" | custom-call | tf_op jit(solution)/shard_map/prepare/pallas_call | solution.py:105
  2.3 4.0 %collective-permute-start.2 = (bf16[208,256]{1,0:T(8,128)(2,1)}, bf16[208,256]{1,0:T(8,128)(2,1)S(1)}, u32[]{:S(2)}, u32[]{:S(2)}) collective-permute-start(bf16[208,256]{1,0:T(8,128)(2,1)} %prepare.1), channel_id=1, source_target_pairs={{0,12},{4,8},{8,4},{12,0},{16,28},{20,24},{24,20},{28,16},{1,13},{... | collective-permute-start | bytes 319496 | tf_op jit(solution)/shard_map/ppermute | solution.py:529
  6.2 0.5 collective-permute-start
  6.8 0.1 pad_add_fusion.place
  6.9 5.3 %unit.1 = (bf16[8,256,1024]{2,1,0:T(8,128)(2,1)}, f32[8,1,1024]{2,1,0:T(1,128)S(1)}) custom-call(s32[4]{0:T(128)S(1)} %pad_add_fusion.place, bf16[256,32768]{1,0:T(8,128)(2,1)} %v_hbm.5), custom_call_target="tpu_custom_call" | custom-call | flops 8388608 | bytes 8388608 | tf_op jit(solution)/shard_map/unit/pallas_call | solution.py:144
  12.4 3.1 %collective-permute-start.3 = (bf16[4,32,256]{2,1,0:T(8,128)(2,1)S(1)}, bf16[4,32,256]{2,1,0:T(8,128)(2,1)S(1)}, u32[]{:S(2)}, u32[]{:S(2)}) collective-permute-start(bf16[4,32,256]{2,1,0:T(8,128)(2,1)S(1)} %pad_maximum_fusion.3), channel_id=1, source_target_pairs={{0,16},{4,20},{8,24},{12,28},{16,0},{20,4},{24,8},{28,12},{1,17},{... | collective-permute-start | bytes 196616 | tf_op jit(solution)/shard_map/ppermute | solution.py:529
  15.5 2.5 %collective-permute-done.3 = bf16[4,32,256]{2,1,0:T(8,128)(2,1)S(1)} collective-permute-done((bf16[4,32,256]{2,1,0:T(8,128)(2,1)S(1)}, bf16[4,32,256]{2,1,0:T(8,128)(2,1)S(1)}, u32[]{:S(2)}, u32[]{:S(2)}) %collective-permute-start.3) | collective-permute-done | bytes 65568 | tf_op jit(solution)/shard_map/ppermute | solution.py:529
  18.0 5.5 %energy.1 = (bf16[8,256,1024]{2,1,0:T(8,128)(2,1)}, f32[1,256]{1,0:T(1,128)S(1)}) custom-call(bf16[256,256]{1,0:T(8,128)(2,1)S(1)} %bitcast.16, bf16[8,256,1024]{2,1,0:T(8,128)(2,1)} %get-tuple-element.50.unit_hbm.refs_0_), custom_call_target="tpu_custom_call" | custom-call | flops 1073741824 | bytes 8388608 | tf_op jit(solution)/shard_map/energy/pallas_call | solution.py:189
  23.5 0.1 collective-permute-start.4
  23.5 1.7 %collective-permute-start.5 = (f32[1,256]{1,0:T(1,128)S(1)}, f32[1,256]{1,0:T(1,128)S(1)}, u32[]{:S(2)}, u32[]{:S(2)}) collective-permute-start(f32[1,256]{1,0:T(1,128)S(1)} %get-tuple-element.51), channel_id=1, source_target_pairs={{0,2},{1,3},{2,0},{3,1},{4,6},{5,7},{6,4},{7,5},{8,10},{9,11},{10,... | collective-permute-start | bytes 3080 | tf_op jit(solution)/shard_map/ppermute | solution.py:532
  25.2 0.2 collective-permute-start.6
  25.5 0.1 convert_element_type.52.pairs_ref
  25.6 2.8 %collective-permute-start.10 = (bf16[4,176,256]{2,1,0:T(8,128)(2,1)S(1)}, bf16[4,176,256]{2,1,0:T(8,128)(2,1)S(1)}, u32[]{:S(2)}, u32[]{:S(2)}) collective-permute-start(bf16[4,176,256]{2,1,0:T(8,128)(2,1)S(1)} %slice.49.rest_ref), channel_id=1, source_target_pairs={{0,16},{4,20},{8,24},{12,28},{16,0},{20,4},{24,8},{28,12},{1,17},{... | collective-permute-start | bytes 1081352 | tf_op jit(solution)/shard_map/ppermute | solution.py:529
  28.3 1.6 %collective-permute-start.7 = (f32[1,256]{1,0:T(1,128)S(1)}, f32[1,256]{1,0:T(1,128)S(1)}, u32[]{:S(2)}, u32[]{:S(2)}) collective-permute-start(f32[1,256]{1,0:T(1,128)S(1)} %add_add_fusion.5), channel_id=1, source_target_pairs={{0,4},{4,0},{8,12},{12,8},{16,20},{20,16},{24,28},{28,24},{1,5},{5... | collective-permute-start | bytes 3080 | tf_op jit(solution)/shard_map/ppermute | solution.py:529
  29.9 2.1 %collective-permute-start.8 = (f32[1,256]{1,0:T(1,128)S(1)}, f32[1,256]{1,0:T(1,128)S(1)}, u32[]{:S(2)}, u32[]{:S(2)}) collective-permute-start(f32[1,256]{1,0:T(1,128)S(1)} %add_add_fusion.5), channel_id=1, source_target_pairs={{0,8},{4,12},{8,0},{12,4},{16,24},{20,28},{24,16},{28,20},{1,9},{5... | collective-permute-start | bytes 3080 | tf_op jit(solution)/shard_map/ppermute | solution.py:529
  32.0 9.1 %student_near.1 = (bf16[8,640,1024]{2,1,0:T(8,128)(2,1)}, f32[1,640]{1,0:T(1,128)S(1)}, bf16[256,640]{1,0:T(8,128)(2,1)S(1)}, f32[256,256]{1,0:T(8,128)S(1)}, f32[256,640]{1,0:T(8,128)S(1)}) custom-call(bf16[4,176,256]{2,1,0:T(8,128)(2,1)S(1)} %slice.49.rest_ref, s32[1,640]{1,0:T(1,128)S(1)} %convert_element_type.52.pairs_ref, ...), custom_call_target="tpu_custom_call" | custom-call | flops 5368709120 | bytes 10485760 | tf_op jit(solution)/shard_map/student_near/pallas_call | solution.py:347
  41.2 3.8 %iterate.1 = f32[1,256]{1,0:T(1,128)S(1)} custom-call(f32[1,256]{1,0:T(1,128)S(1)} %add_add_fusion.4.sum_in, bf16[8,256,1024]{2,1,0:T(8,128)(2,1)} %get-tuple-element.54.energy_hbm), custom_call_target="tpu_custom_call" | custom-call | flops 8388608 | bytes 8388608 | tf_op jit(solution)/shard_map/iterate/pallas_call | solution.py:273
  45.0 1.6 %collective-permute-start.12 = (f32[1,256]{1,0:T(1,128)S(1)}, f32[1,256]{1,0:T(1,128)S(1)}, u32[]{:S(2)}, u32[]{:S(2)}) collective-permute-start(f32[1,256]{1,0:T(1,128)S(1)} %iterate.1), channel_id=1, source_target_pairs={{0,2},{1,3},{2,0},{3,1},{4,6},{5,7},{6,4},{7,5},{8,10},{9,11},{10,... | collective-permute-start | bytes 3080 | tf_op jit(solution)/shard_map/ppermute | solution.py:532
  46.6 0.3 collective-permute-start.13
  46.9 0.1 convert_element_type.55.pairs_ref
  47.0 1.6 %collective-permute-done.12 = f32[1,256]{1,0:T(1,128)S(1)} collective-permute-done((f32[1,256]{1,0:T(1,128)S(1)}, f32[1,256]{1,0:T(1,128)S(1)}, u32[]{:S(2)}, u32[]{:S(2)}) %collective-permute-start.12) | collective-permute-done | bytes 1056 | tf_op jit(solution)/shard_map/ppermute | solution.py:532
  48.7 0.9 collective-permute-done.13
  49.6 1.5 %collective-permute-start.14 = (f32[1,256]{1,0:T(1,128)S(1)}, f32[1,256]{1,0:T(1,128)S(1)}, u32[]{:S(2)}, u32[]{:S(2)}) collective-permute-start(f32[1,256]{1,0:T(1,128)S(1)} %add_add_fusion.3), channel_id=1, source_target_pairs={{0,4},{4,0},{8,12},{12,8},{16,20},{20,16},{24,28},{28,24},{1,5},{5... | collective-permute-start | bytes 3080 | tf_op jit(solution)/shard_map/ppermute | solution.py:529
  51.1 2.0 %collective-permute-start.15 = (f32[1,256]{1,0:T(1,128)S(1)}, f32[1,256]{1,0:T(1,128)S(1)}, u32[]{:S(2)}, u32[]{:S(2)}) collective-permute-start(f32[1,256]{1,0:T(1,128)S(1)} %add_add_fusion.3), channel_id=1, source_target_pairs={{0,8},{4,12},{8,0},{12,4},{16,24},{20,28},{24,16},{28,20},{1,9},{5... | collective-permute-start | bytes 3080 | tf_op jit(solution)/shard_map/ppermute | solution.py:529
  53.1 6.7 %student_far.1 = (bf16[8,640,1024]{2,1,0:T(8,128)(2,1)}, f32[1,640]{1,0:T(1,128)S(1)}, bf16[256,640]{1,0:T(8,128)(2,1)S(1)}, f32[256,256]{1,0:T(8,128)S(1)}) custom-call(bf16[4,176,256]{2,1,0:T(8,128)(2,1)S(1)} %collective-permute-done.10.rest_ref, s32[1,640]{1,0:T(1,128)S(1)} %convert_element_type.55.pairs_ref, ...), custom_call_target="tpu_custom_call" | custom-call | flops 5368709120 | bytes 10485760 | tf_op jit(solution)/shard_map/student_far/pallas_call | solution.py:347
  59.8 7.1 %iterate_last.1 = (f32[1,1536]{1,0:T(1,128)S(1)}, f32[256,256]{1,0:T(8,128)S(1)}, bf16[8,256,1024]{2,1,0:T(8,128)(2,1)}) custom-call(f32[1,256]{1,0:T(1,128)S(1)} %add_add_fusion.2.sum_in, bf16[8,256,1024]{2,1,0:T(8,128)(2,1)} %get-tuple-element.54.energy_hbm, bf16[8,256,1024]{2,1,0:T(8,128)(2,1)} %get-tuple-element.50.unit_hbm.refs_0_, ...), custom_call_target="tpu_custom_call" | custom-call | flops 8388608 | bytes 8388608 | tf_op jit(solution)/shard_map/iterate_last/pallas_call | solution.py:273
  66.9 0.1 collective-permute-start.17
  67.0 0.7 collective-permute-start.18
  67.7 1.1 collective-permute-start.19
  68.8 1.8 %collective-permute-done.18 = f32[1,1536]{1,0:T(1,128)S(1)} collective-permute-done((f32[1,1536]{1,0:T(1,128)S(1)}, f32[1,1536]{1,0:T(1,128)S(1)}, u32[]{:S(2)}, u32[]{:S(2)}) %collective-permute-start.18) | collective-permute-done | bytes 6176 | tf_op jit(solution)/shard_map/ppermute | solution.py:532
  70.7 0.1 collective-permute-done.19
  70.8 1.5 %collective-permute-start.20 = (f32[1,1536]{1,0:T(1,128)S(1)}, f32[1,1536]{1,0:T(1,128)S(1)}, u32[]{:S(2)}, u32[]{:S(2)}) collective-permute-start(f32[1,1536]{1,0:T(1,128)S(1)} %add_add_fusion.1), channel_id=1, source_target_pairs={{0,4},{4,0},{8,12},{12,8},{16,20},{20,16},{24,28},{28,24},{1,5},{5... | collective-permute-start | bytes 18440 | tf_op jit(solution)/shard_map/ppermute | solution.py:529
  72.3 2.0 %collective-permute-start.21 = (f32[1,1536]{1,0:T(1,128)S(1)}, f32[1,1536]{1,0:T(1,128)S(1)}, u32[]{:S(2)}, u32[]{:S(2)}) collective-permute-start(f32[1,1536]{1,0:T(1,128)S(1)} %add_add_fusion.1), channel_id=1, source_target_pairs={{0,8},{4,12},{8,0},{12,4},{16,24},{20,28},{24,16},{28,20},{1,9},{5... | collective-permute-start | bytes 18440 | tf_op jit(solution)/shard_map/ppermute | solution.py:529
  74.3 0.1 collective-permute-done.20
  74.5 1.5 %collective-permute-done.21 = f32[1,1536]{1,0:T(1,128)S(1)} collective-permute-done((f32[1,1536]{1,0:T(1,128)S(1)}, f32[1,1536]{1,0:T(1,128)S(1)}, u32[]{:S(2)}, u32[]{:S(2)}) %collective-permute-start.21) | collective-permute-done | bytes 6176 | tf_op jit(solution)/shard_map/ppermute | solution.py:529
  75.9 2.9 %collective-permute-done.22 = f32[1,1536]{1,0:T(1,128)S(1)} collective-permute-done((f32[1,1536]{1,0:T(1,128)S(1)}, f32[1,1536]{1,0:T(1,128)S(1)}, u32[]{:S(2)}, u32[]{:S(2)}) %collective-permute-start.22) | collective-permute-done | bytes 6176 | tf_op jit(solution)/shard_map/ppermute | solution.py:529
  78.9 8.6 %head.2 = (f32[32,32768]{1,0:T(8,128)}, bf16[32,4096]{1,0:T(8,128)(2,1)S(1)}, bf16[32,4096]{1,0:T(8,128)(2,1)S(1)}, bf16[32,4096]{1,0:T(8,128)(2,1)S(1)}, f32[12...) custom-call(s32[4]{0:T(128)S(1)} %pad_add_fusion.place, f32[1,1536]{1,0:T(1,128)S(1)} %add_add_fusion.both_ref, ...), custom_call_target="tpu_custom_call" | custom-call | flops 6442450944 | bytes 14680064 | tf_op jit(solution)/shard_map/head/pallas_call | solution.py:472
  87.5 1.4 %collective-permute-start.29 = (f32[136,640]{1,0:T(8,128)S(1)}, f32[136,640]{1,0:T(8,128)S(1)}, u32[]{:S(2)}, u32[]{:S(2)}) collective-permute-start(f32[136,640]{1,0:T(8,128)S(1)} %get-tuple-element.84), channel_id=1, source_target_pairs={{0,2},{1,3},{2,0},{3,1},{4,6},{5,7},{6,4},{7,5},{8,10},{9,11},{10,... | collective-permute-start | bytes 1044488 | tf_op jit(solution)/shard_map/ppermute | solution.py:532
  88.9 0.1 collective-permute-start.25
  89.0 1.9 %collective-permute-start.24 = (bf16[32,4096]{1,0:T(8,128)(2,1)S(1)}, bf16[32,4096]{1,0:T(8,128)(2,1)S(1)}, u32[]{:S(2)}, u32[]{:S(2)}) collective-permute-start(bf16[32,4096]{1,0:T(8,128)(2,1)S(1)} %get-tuple-element.75), channel_id=1, source_target_pairs={{0,8},{4,12},{8,0},{12,4},{16,24},{20,28},{24,16},{28,20},{1,9},{5... | collective-permute-start | bytes 786440 | tf_op jit(solution)/shard_map/ppermute | solution.py:529
  90.9 1.5 %collective-permute-start.23 = (bf16[32,4096]{1,0:T(8,128)(2,1)S(1)}, bf16[32,4096]{1,0:T(8,128)(2,1)S(1)}, u32[]{:S(2)}, u32[]{:S(2)}) collective-permute-start(bf16[32,4096]{1,0:T(8,128)(2,1)S(1)} %get-tuple-element.72), channel_id=1, source_target_pairs={{0,4},{4,0},{8,12},{12,8},{16,20},{20,16},{24,28},{28,24},{1,5},{5... | collective-permute-start | bytes 786440 | tf_op jit(solution)/shard_map/ppermute | solution.py:529
  92.4 8.3 %head.3 = (f32[32,32768]{1,0:T(8,128)}, bf16[32,4096]{1,0:T(8,128)(2,1)S(1)}, bf16[32,4096]{1,0:T(8,128)(2,1)S(1)}, bf16[32,4096]{1,0:T(8,128)(2,1)S(1)}) custom-call(s32[4]{0:T(128)S(1)} %pad_add_fusion.place, f32[1,1536]{1,0:T(1,128)S(1)} %add_add_fusion.both_ref, ...), custom_call_target="tpu_custom_call", output_to_operand_aliasing={{0}: (12, {})} | custom-call | flops 6442450944 | bytes 14680064 | tf_op jit(solution)/shard_map/head/pallas_call | solution.py:472
  100.8 0.1 constant_dynamic-slice_fusion.denom_ref
  100.9 0.1 collective-permute-start.28
  101.0 1.9 %collective-permute-start.27 = (bf16[32,4096]{1,0:T(8,128)(2,1)S(1)}, bf16[32,4096]{1,0:T(8,128)(2,1)S(1)}, u32[]{:S(2)}, u32[]{:S(2)}) collective-permute-start(bf16[32,4096]{1,0:T(8,128)(2,1)S(1)} %get-tuple-element.81), channel_id=1, source_target_pairs={{0,8},{4,12},{8,0},{12,4},{16,24},{20,28},{24,16},{28,20},{1,9},{5... | collective-permute-start | bytes 786440 | tf_op jit(solution)/shard_map/ppermute | solution.py:529
  102.9 1.5 %collective-permute-start.26 = (bf16[32,4096]{1,0:T(8,128)(2,1)S(1)}, bf16[32,4096]{1,0:T(8,128)(2,1)S(1)}, u32[]{:S(2)}, u32[]{:S(2)}) collective-permute-start(bf16[32,4096]{1,0:T(8,128)(2,1)S(1)} %get-tuple-element.80), channel_id=1, source_target_pairs={{0,4},{4,0},{8,12},{12,8},{16,20},{20,16},{24,28},{28,24},{1,5},{5... | collective-permute-start | bytes 786440 | tf_op jit(solution)/shard_map/ppermute | solution.py:529
  104.4 0.8 convert_dynamic-update-slice_fusion.5
  105.3 0.1 collective-permute-start.30
  105.4 0.8 convert_dynamic-update-slice_fusion.4
  106.2 0.6 collective-permute-done.30
  106.8 0.2 fusion
  107.0 0.6 collective-permute-start.31
  107.6 0.1 collective-permute-start.32
  107.8 2.6 %collective-permute-done.28 = bf16[32,4096]{1,0:T(8,128)(2,1)S(1)} collective-permute-done((bf16[32,4096]{1,0:T(8,128)(2,1)S(1)}, bf16[32,4096]{1,0:T(8,128)(2,1)S(1)}, u32[]{:S(2)}, u32[]{:S(2)}) %collective-permute-start.28) | collective-permute-done | bytes 262176 | tf_op jit(solution)/shard_map/ppermute | solution.py:529
  110.4 0.3 collective-permute-start.33
  110.7 0.8 convert_dynamic-update-slice_fusion.3
  111.5 2.2 %collective-permute-done.27 = bf16[32,4096]{1,0:T(8,128)(2,1)S(1)} collective-permute-done((bf16[32,4096]{1,0:T(8,128)(2,1)S(1)}, bf16[32,4096]{1,0:T(8,128)(2,1)S(1)}, u32[]{:S(2)}, u32[]{:S(2)}) %collective-permute-start.27) | collective-permute-done | bytes 262176 | tf_op jit(solution)/shard_map/ppermute | solution.py:529
  113.7 1.0 collective-permute-done.26
  114.7 0.8 collective-permute-done.31.refs_1_
  115.5 0.8 collective-permute-done.33.refs_3_
  116.3 0.8 convert_dynamic-update-slice_fusion.2
  117.1 0.8 convert_dynamic-update-slice_fusion.1
  117.9 0.8 convert_dynamic-update-slice_fusion
  118.8 1.4 %finish.1 = (f32[64,160]{1,0:T(8,128)}, f32[1,160]{1,0:T(1,128)}) custom-call(s32[4]{0:T(128)S(1)} %pad_add_fusion.place, f32[1,1536]{1,0:T(1,128)S(1)} %add_add_fusion.both_ref, f32[1,160]{1,0:T(1,128)S(1)} %constant_dynamic-slice_fusion.denom_ref, s32[1,160]{1,0:T(1,128)S(1)} %bitcast.18, bf16[160,256]{1,0:T(8,128)(2,1)S(1)} %copy-done, ...), custom_call_target="tpu_custom_call" | custom-call | tf_op jit(solution)/shard_map/finish/pallas_call | solution.py:504
  (55 shorter events, 0.6 us)
Async XLA Ops:
  2.3 9.9 %collective-permute-start.2 = (bf16[208,256]{1,0:T(8,128)(2,1)}, bf16[208,256]{1,0:T(8,128)(2,1)S(1)}, u32[]{:S(2)}, u32[]{:S(2)}) collective-permute-start(bf16[208,256]{1,0:T(8,128)(2,1)} %prepare.1), channel_id=1, source_target_pairs={{0,12},{4,8},{8,4},{12,0},{16,28},{20,24},{24,20},{28,16},{1,13},{... | collective-permute-start | bytes 319496 | tf_op jit(solution)/shard_map/ppermute | solution.py:529
  6.2 6.0 %collective-permute-start = (bf16[208,256]{1,0:T(8,128)(2,1)}, bf16[208,256]{1,0:T(8,128)(2,1)S(1)}, u32[]{:S(2)}, u32[]{:S(2)}) collective-permute-start(bf16[208,256]{1,0:T(8,128)(2,1)} %prepare.1), channel_id=1, source_target_pairs={{0,4},{4,0},{8,12},{12,8},{16,20},{20,16},{24,28},{28,24},{1,5},{5... | collective-permute-start | bytes 319496 | tf_op jit(solution)/shard_map/ppermute | solution.py:529
  6.8 5.5 %collective-permute-start.1 = (bf16[208,256]{1,0:T(8,128)(2,1)}, bf16[208,256]{1,0:T(8,128)(2,1)S(1)}, u32[]{:S(2)}, u32[]{:S(2)}) collective-permute-start(bf16[208,256]{1,0:T(8,128)(2,1)} %prepare.1), channel_id=1, source_target_pairs={{0,8},{4,12},{8,0},{12,4},{16,24},{20,28},{24,16},{28,20},{1,9},{5... | collective-permute-start | bytes 319496 | tf_op jit(solution)/shard_map/ppermute | solution.py:529
  6.9 5.4 %copy-start.2 = (bf16[208,256]{1,0:T(8,128)(2,1)S(1)}, bf16[208,256]{1,0:T(8,128)(2,1)}, u32[]{:S(2)}) copy-start(bf16[208,256]{1,0:T(8,128)(2,1)} %prepare.1) | copy-start | bytes 319492
  12.4 5.6 %collective-permute-start.3 = (bf16[4,32,256]{2,1,0:T(8,128)(2,1)S(1)}, bf16[4,32,256]{2,1,0:T(8,128)(2,1)S(1)}, u32[]{:S(2)}, u32[]{:S(2)}) collective-permute-start(bf16[4,32,256]{2,1,0:T(8,128)(2,1)S(1)} %pad_maximum_fusion.3), channel_id=1, source_target_pairs={{0,16},{4,20},{8,24},{12,28},{16,0},{20,4},{24,8},{28,12},{1,17},{... | collective-permute-start | bytes 196616 | tf_op jit(solution)/shard_map/ppermute | solution.py:529
  23.5 4.9 %collective-permute-start.4 = (f32[1,256]{1,0:T(1,128)S(1)}, f32[1,256]{1,0:T(1,128)S(1)}, u32[]{:S(2)}, u32[]{:S(2)}) collective-permute-start(f32[1,256]{1,0:T(1,128)S(1)} %get-tuple-element.51), channel_id=1, source_target_pairs={{0,1},{1,0},{2,3},{3,2},{4,5},{5,4},{6,7},{7,6},{8,9},{9,8},{10,11... | collective-permute-start | bytes 3080 | tf_op jit(solution)/shard_map/ppermute | solution.py:532
  23.5 4.8 %collective-permute-start.5 = (f32[1,256]{1,0:T(1,128)S(1)}, f32[1,256]{1,0:T(1,128)S(1)}, u32[]{:S(2)}, u32[]{:S(2)}) collective-permute-start(f32[1,256]{1,0:T(1,128)S(1)} %get-tuple-element.51), channel_id=1, source_target_pairs={{0,2},{1,3},{2,0},{3,1},{4,6},{5,7},{6,4},{7,5},{8,10},{9,11},{10,... | collective-permute-start | bytes 3080 | tf_op jit(solution)/shard_map/ppermute | solution.py:532
  25.2 3.1 %collective-permute-start.6 = (f32[1,256]{1,0:T(1,128)S(1)}, f32[1,256]{1,0:T(1,128)S(1)}, u32[]{:S(2)}, u32[]{:S(2)}) collective-permute-start(f32[1,256]{1,0:T(1,128)S(1)} %get-tuple-element.51), channel_id=1, source_target_pairs={{0,3},{1,2},{2,1},{3,0},{4,7},{5,6},{6,5},{7,4},{8,11},{9,10},{10,... | collective-permute-start | bytes 3080 | tf_op jit(solution)/shard_map/ppermute | solution.py:532
  25.6 19.4 %collective-permute-start.10 = (bf16[4,176,256]{2,1,0:T(8,128)(2,1)S(1)}, bf16[4,176,256]{2,1,0:T(8,128)(2,1)S(1)}, u32[]{:S(2)}, u32[]{:S(2)}) collective-permute-start(bf16[4,176,256]{2,1,0:T(8,128)(2,1)S(1)} %slice.49.rest_ref), channel_id=1, source_target_pairs={{0,16},{4,20},{8,24},{12,28},{16,0},{20,4},{24,8},{28,12},{1,17},{... | collective-permute-start | bytes 1081352 | tf_op jit(solution)/shard_map/ppermute | solution.py:529
  28.3 12.8 %collective-permute-start.7 = (f32[1,256]{1,0:T(1,128)S(1)}, f32[1,256]{1,0:T(1,128)S(1)}, u32[]{:S(2)}, u32[]{:S(2)}) collective-permute-start(f32[1,256]{1,0:T(1,128)S(1)} %add_add_fusion.5), channel_id=1, source_target_pairs={{0,4},{4,0},{8,12},{12,8},{16,20},{20,16},{24,28},{28,24},{1,5},{5... | collective-permute-start | bytes 3080 | tf_op jit(solution)/shard_map/ppermute | solution.py:529
  29.9 11.2 %collective-permute-start.8 = (f32[1,256]{1,0:T(1,128)S(1)}, f32[1,256]{1,0:T(1,128)S(1)}, u32[]{:S(2)}, u32[]{:S(2)}) collective-permute-start(f32[1,256]{1,0:T(1,128)S(1)} %add_add_fusion.5), channel_id=1, source_target_pairs={{0,8},{4,12},{8,0},{12,4},{16,24},{20,28},{24,16},{28,20},{1,9},{5... | collective-permute-start | bytes 3080 | tf_op jit(solution)/shard_map/ppermute | solution.py:529
  32.0 9.1 %collective-permute-start.9 = (f32[1,256]{1,0:T(1,128)S(1)}, f32[1,256]{1,0:T(1,128)S(1)}, u32[]{:S(2)}, u32[]{:S(2)}) collective-permute-start(f32[1,256]{1,0:T(1,128)S(1)} %add_add_fusion.5), channel_id=1, source_target_pairs={{0,12},{4,8},{8,4},{12,0},{16,28},{20,24},{24,20},{28,16},{1,13},{... | collective-permute-start | bytes 3080 | tf_op jit(solution)/shard_map/ppermute | solution.py:529
  45.0 2.1 %collective-permute-start.11 = (f32[1,256]{1,0:T(1,128)S(1)}, f32[1,256]{1,0:T(1,128)S(1)}, u32[]{:S(2)}, u32[]{:S(2)}) collective-permute-start(f32[1,256]{1,0:T(1,128)S(1)} %iterate.1), channel_id=1, source_target_pairs={{0,1},{1,0},{2,3},{3,2},{4,5},{5,4},{6,7},{7,6},{8,9},{9,8},{10,11... | collective-permute-start | bytes 3080 | tf_op jit(solution)/shard_map/ppermute | solution.py:532
  45.0 3.6 %collective-permute-start.12 = (f32[1,256]{1,0:T(1,128)S(1)}, f32[1,256]{1,0:T(1,128)S(1)}, u32[]{:S(2)}, u32[]{:S(2)}) collective-permute-start(f32[1,256]{1,0:T(1,128)S(1)} %iterate.1), channel_id=1, source_target_pairs={{0,2},{1,3},{2,0},{3,1},{4,6},{5,7},{6,4},{7,5},{8,10},{9,11},{10,... | collective-permute-start | bytes 3080 | tf_op jit(solution)/shard_map/ppermute | solution.py:532
  46.6 3.0 %collective-permute-start.13 = (f32[1,256]{1,0:T(1,128)S(1)}, f32[1,256]{1,0:T(1,128)S(1)}, u32[]{:S(2)}, u32[]{:S(2)}) collective-permute-start(f32[1,256]{1,0:T(1,128)S(1)} %iterate.1), channel_id=1, source_target_pairs={{0,3},{1,2},{2,1},{3,0},{4,7},{5,6},{6,5},{7,4},{8,11},{9,10},{10,... | collective-permute-start | bytes 3080 | tf_op jit(solution)/shard_map/ppermute | solution.py:532
  49.6 10.2 %collective-permute-start.14 = (f32[1,256]{1,0:T(1,128)S(1)}, f32[1,256]{1,0:T(1,128)S(1)}, u32[]{:S(2)}, u32[]{:S(2)}) collective-permute-start(f32[1,256]{1,0:T(1,128)S(1)} %add_add_fusion.3), channel_id=1, source_target_pairs={{0,4},{4,0},{8,12},{12,8},{16,20},{20,16},{24,28},{28,24},{1,5},{5... | collective-permute-start | bytes 3080 | tf_op jit(solution)/shard_map/ppermute | solution.py:529
  51.1 8.7 %collective-permute-start.15 = (f32[1,256]{1,0:T(1,128)S(1)}, f32[1,256]{1,0:T(1,128)S(1)}, u32[]{:S(2)}, u32[]{:S(2)}) collective-permute-start(f32[1,256]{1,0:T(1,128)S(1)} %add_add_fusion.3), channel_id=1, source_target_pairs={{0,8},{4,12},{8,0},{12,4},{16,24},{20,28},{24,16},{28,20},{1,9},{5... | collective-permute-start | bytes 3080 | tf_op jit(solution)/shard_map/ppermute | solution.py:529
  53.1 6.7 %collective-permute-start.16 = (f32[1,256]{1,0:T(1,128)S(1)}, f32[1,256]{1,0:T(1,128)S(1)}, u32[]{:S(2)}, u32[]{:S(2)}) collective-permute-start(f32[1,256]{1,0:T(1,128)S(1)} %add_add_fusion.3), channel_id=1, source_target_pairs={{0,12},{4,8},{8,4},{12,0},{16,28},{20,24},{24,20},{28,16},{1,13},{... | collective-permute-start | bytes 3080 | tf_op jit(solution)/shard_map/ppermute | solution.py:529
  66.9 1.9 %collective-permute-start.17 = (f32[1,1536]{1,0:T(1,128)S(1)}, f32[1,1536]{1,0:T(1,128)S(1)}, u32[]{:S(2)}, u32[]{:S(2)}) collective-permute-start(f32[1,1536]{1,0:T(1,128)S(1)} %get-tuple-element.58), channel_id=1, source_target_pairs={{0,1},{1,0},{2,3},{3,2},{4,5},{5,4},{6,7},{7,6},{8,9},{9,8},{10,11... | collective-permute-start | bytes 18440 | tf_op jit(solution)/shard_map/ppermute | solution.py:532
  67.0 3.7 %collective-permute-start.18 = (f32[1,1536]{1,0:T(1,128)S(1)}, f32[1,1536]{1,0:T(1,128)S(1)}, u32[]{:S(2)}, u32[]{:S(2)}) collective-permute-start(f32[1,1536]{1,0:T(1,128)S(1)} %get-tuple-element.58), channel_id=1, source_target_pairs={{0,2},{1,3},{2,0},{3,1},{4,6},{5,7},{6,4},{7,5},{8,10},{9,11},{10,... | collective-permute-start | bytes 18440 | tf_op jit(solution)/shard_map/ppermute | solution.py:532
  67.7 3.1 %collective-permute-start.19 = (f32[1,1536]{1,0:T(1,128)S(1)}, f32[1,1536]{1,0:T(1,128)S(1)}, u32[]{:S(2)}, u32[]{:S(2)}) collective-permute-start(f32[1,1536]{1,0:T(1,128)S(1)} %get-tuple-element.58), channel_id=1, source_target_pairs={{0,3},{1,2},{2,1},{3,0},{4,7},{5,6},{6,5},{7,4},{8,11},{9,10},{10,... | collective-permute-start | bytes 18440 | tf_op jit(solution)/shard_map/ppermute | solution.py:532
  70.8 3.7 %collective-permute-start.20 = (f32[1,1536]{1,0:T(1,128)S(1)}, f32[1,1536]{1,0:T(1,128)S(1)}, u32[]{:S(2)}, u32[]{:S(2)}) collective-permute-start(f32[1,1536]{1,0:T(1,128)S(1)} %add_add_fusion.1), channel_id=1, source_target_pairs={{0,4},{4,0},{8,12},{12,8},{16,20},{20,16},{24,28},{28,24},{1,5},{5... | collective-permute-start | bytes 18440 | tf_op jit(solution)/shard_map/ppermute | solution.py:529
  72.3 3.6 %collective-permute-start.21 = (f32[1,1536]{1,0:T(1,128)S(1)}, f32[1,1536]{1,0:T(1,128)S(1)}, u32[]{:S(2)}, u32[]{:S(2)}) collective-permute-start(f32[1,1536]{1,0:T(1,128)S(1)} %add_add_fusion.1), channel_id=1, source_target_pairs={{0,8},{4,12},{8,0},{12,4},{16,24},{20,28},{24,16},{28,20},{1,9},{5... | collective-permute-start | bytes 18440 | tf_op jit(solution)/shard_map/ppermute | solution.py:529
  74.3 4.5 %collective-permute-start.22 = (f32[1,1536]{1,0:T(1,128)S(1)}, f32[1,1536]{1,0:T(1,128)S(1)}, u32[]{:S(2)}, u32[]{:S(2)}) collective-permute-start(f32[1,1536]{1,0:T(1,128)S(1)} %add_add_fusion.1), channel_id=1, source_target_pairs={{0,12},{4,8},{8,4},{12,0},{16,28},{20,24},{24,20},{28,16},{1,13},{... | collective-permute-start | bytes 18440 | tf_op jit(solution)/shard_map/ppermute | solution.py:529
  87.5 17.7 %collective-permute-start.29 = (f32[136,640]{1,0:T(8,128)S(1)}, f32[136,640]{1,0:T(8,128)S(1)}, u32[]{:S(2)}, u32[]{:S(2)}) collective-permute-start(f32[136,640]{1,0:T(8,128)S(1)} %get-tuple-element.84), channel_id=1, source_target_pairs={{0,2},{1,3},{2,0},{3,1},{4,6},{5,7},{6,4},{7,5},{8,10},{9,11},{10,... | collective-permute-start | bytes 1044488 | tf_op jit(solution)/shard_map/ppermute | solution.py:532
  88.9 11.9 %collective-permute-start.25 = (bf16[32,4096]{1,0:T(8,128)(2,1)S(1)}, bf16[32,4096]{1,0:T(8,128)(2,1)S(1)}, u32[]{:S(2)}, u32[]{:S(2)}) collective-permute-start(bf16[32,4096]{1,0:T(8,128)(2,1)S(1)} %get-tuple-element.78), channel_id=1, source_target_pairs={{0,12},{4,8},{8,4},{12,0},{16,28},{20,24},{24,20},{28,16},{1,13},{... | collective-permute-start | bytes 786440 | tf_op jit(solution)/shard_map/ppermute | solution.py:529
  89.0 12.0 %collective-permute-start.24 = (bf16[32,4096]{1,0:T(8,128)(2,1)S(1)}, bf16[32,4096]{1,0:T(8,128)(2,1)S(1)}, u32[]{:S(2)}, u32[]{:S(2)}) collective-permute-start(bf16[32,4096]{1,0:T(8,128)(2,1)S(1)} %get-tuple-element.75), channel_id=1, source_target_pairs={{0,8},{4,12},{8,0},{12,4},{16,24},{20,28},{24,16},{28,20},{1,9},{5... | collective-permute-start | bytes 786440 | tf_op jit(solution)/shard_map/ppermute | solution.py:529
  90.9 12.0 %collective-permute-start.23 = (bf16[32,4096]{1,0:T(8,128)(2,1)S(1)}, bf16[32,4096]{1,0:T(8,128)(2,1)S(1)}, u32[]{:S(2)}, u32[]{:S(2)}) collective-permute-start(bf16[32,4096]{1,0:T(8,128)(2,1)S(1)} %get-tuple-element.72), channel_id=1, source_target_pairs={{0,4},{4,0},{8,12},{12,8},{16,20},{20,16},{24,28},{28,24},{1,5},{5... | collective-permute-start | bytes 786440 | tf_op jit(solution)/shard_map/ppermute | solution.py:529
  100.8 18.0 %copy-start = (bf16[160,256]{1,0:T(8,128)(2,1)S(1)}, bf16[160,256]{1,0:T(8,128)(2,1)}, u32[]{:S(2)}) copy-start(bf16[160,256]{1,0:T(8,128)(2,1)} %stud_ref.3) | copy-start | bytes 245764
  100.8 18.0 %copy-start.1 = (s32[160]{0:T(256)S(1)}, s32[160]{0:T(256)}, u32[]{:S(2)}) copy-start(s32[160]{0:T(256)} %param.7) | copy-start | bytes 1924
  100.9 9.5 %collective-permute-start.28 = (bf16[32,4096]{1,0:T(8,128)(2,1)S(1)}, bf16[32,4096]{1,0:T(8,128)(2,1)S(1)}, u32[]{:S(2)}, u32[]{:S(2)}) collective-permute-start(bf16[32,4096]{1,0:T(8,128)(2,1)S(1)} %get-tuple-element.82), channel_id=1, source_target_pairs={{0,12},{4,8},{8,4},{12,0},{16,28},{20,24},{24,20},{28,16},{1,13},{... | collective-permute-start | bytes 786440 | tf_op jit(solution)/shard_map/ppermute | solution.py:529
  101.0 12.8 %collective-permute-start.27 = (bf16[32,4096]{1,0:T(8,128)(2,1)S(1)}, bf16[32,4096]{1,0:T(8,128)(2,1)S(1)}, u32[]{:S(2)}, u32[]{:S(2)}) collective-permute-start(bf16[32,4096]{1,0:T(8,128)(2,1)S(1)} %get-tuple-element.81), channel_id=1, source_target_pairs={{0,8},{4,12},{8,0},{12,4},{16,24},{20,28},{24,16},{28,20},{1,9},{5... | collective-permute-start | bytes 786440 | tf_op jit(solution)/shard_map/ppermute | solution.py:529
  102.9 11.8 %collective-permute-start.26 = (bf16[32,4096]{1,0:T(8,128)(2,1)S(1)}, bf16[32,4096]{1,0:T(8,128)(2,1)S(1)}, u32[]{:S(2)}, u32[]{:S(2)}) collective-permute-start(bf16[32,4096]{1,0:T(8,128)(2,1)S(1)} %get-tuple-element.80), channel_id=1, source_target_pairs={{0,4},{4,0},{8,12},{12,8},{16,20},{20,16},{24,28},{28,24},{1,5},{5... | collective-permute-start | bytes 786440 | tf_op jit(solution)/shard_map/ppermute | solution.py:529
  105.3 1.5 %collective-permute-start.30 = (f32[72,640]{1,0:T(8,128)S(1)}, f32[72,640]{1,0:T(8,128)S(1)}, u32[]{:S(2)}, u32[]{:S(2)}) collective-permute-start(f32[72,640]{1,0:T(8,128)S(1)} %pad_maximum_fusion.1), channel_id=1, source_target_pairs={{0,1},{1,0},{2,3},{3,2},{4,5},{5,4},{6,7},{7,6},{8,9},{9,8},{10,11... | collective-permute-start | bytes 552968 | tf_op jit(solution)/shard_map/ppermute | solution.py:532
  107.0 8.4 %collective-permute-start.31 = (f32[72,160]{1,0:T(8,128)S(1)}, f32[72,160]{1,0:T(8,128)S(1)}, u32[]{:S(2)}, u32[]{:S(2)}) collective-permute-start(f32[72,160]{1,0:T(8,128)S(1)} %get-tuple-element.97), channel_id=1, source_target_pairs={{0,4},{4,0},{8,12},{12,8},{16,20},{20,16},{24,28},{28,24},{1,5},{5... | collective-permute-start | bytes 138248 | tf_op jit(solution)/shard_map/ppermute | solution.py:529
  107.6 7.8 %collective-permute-start.32 = (f32[72,160]{1,0:T(8,128)S(1)}, f32[72,160]{1,0:T(8,128)S(1)}, u32[]{:S(2)}, u32[]{:S(2)}) collective-permute-start(f32[72,160]{1,0:T(8,128)S(1)} %get-tuple-element.98), channel_id=1, source_target_pairs={{0,8},{4,12},{8,0},{12,4},{16,24},{20,28},{24,16},{28,20},{1,9},{5... | collective-permute-start | bytes 138248 | tf_op jit(solution)/shard_map/ppermute | solution.py:529
  110.4 5.9 %collective-permute-start.33 = (f32[72,160]{1,0:T(8,128)S(1)}, f32[72,160]{1,0:T(8,128)S(1)}, u32[]{:S(2)}, u32[]{:S(2)}) collective-permute-start(f32[72,160]{1,0:T(8,128)S(1)} %get-tuple-element.95), channel_id=1, source_target_pairs={{0,12},{4,8},{8,4},{12,0},{16,28},{20,24},{24,20},{28,16},{1,13},{... | collective-permute-start | bytes 138248 | tf_op jit(solution)/shard_map/ppermute | solution.py:529

commit v5 on v4

--- a/solution.py
+++ b/solution.py
@@ -12,9 +12,10 @@
 eps = 1e-06
 LOG2E = 1.4426950408889634
 GROUP = 4
-CHUNKS = 8
-LIMIT = 50
-PARTS = 2
+CHUNKS = 4
+SPLIT = 2
+LIMIT = 44
+SIZES = (5, 3)
 F32 = jnp.float32
 BF16 = jnp.bfloat16
 NT = (((1,), (1,)), ((), ()))
@@ -38,7 +39,7 @@
 
 SMEM = pl.BlockSpec(memory_space=pltpu.SMEM)
 DMA = pltpu.SemaphoreType.DMA
-AHEAD = 3
+AHEAD = 4
 
 
 def begin(chunks, fetch):
@@ -205,18 +206,14 @@
 
 def iterate_kernel(total_k, last, sum_in, energy_hbm, *refs):
     if last:
-        unit_hbm, near_ref, far_ref, sum_ref, mean_ref, scaled_hbm = refs[:6]
-        acc, row, energy, sems_in, scaled, unit, sems_out = refs[6:]
-        mean_ref[...] = jnp.zeros_like(mean_ref)
+        near_ref, far_ref, sum_ref, scaled_hbm = refs[:4]
+        acc, row, energy, sems_in, scaled, sems_out = refs[4:]
     else:
         sum_ref, acc, row, energy, sems_in = refs
     chunks, t, width = energy.shape
 
     def fetch(i):
-        copy = pltpu.make_async_copy(energy_hbm.at[i], energy.at[i], sems_in.at[i, 0])
-        if not last:
-            return (copy,)
-        return (copy, pltpu.make_async_copy(unit_hbm.at[i], unit.at[i], sems_in.at[i, 1]))
+        return (pltpu.make_async_copy(energy_hbm.at[i], energy.at[i], sems_in.at[i]),)
 
     def store(i):
         return pltpu.make_async_copy(scaled.at[i], scaled_hbm.at[i], sems_out.at[i])
@@ -240,7 +237,6 @@
         acc[...] += part
         if last:
             store(i).start()
-            mean_ref[...] += lax.dot_general(unit[i], scaled[i], NT, preferred_element_type=F32)
 
     stream(chunks, fetch, work)
     sum_ref[:, :t] = to_row(acc[...])
@@ -258,18 +254,16 @@
     out_shape = [jax.ShapeDtypeStruct((1, t), F32)]
     in_specs, out_specs = vmem(1) + anywhere(1), vmem(1)
     scratch = [
-        pltpu.VMEM((t, 128), F32), pltpu.VMEM((t, 128), F32), pltpu.VMEM(energy.shape, BF16), DMA((chunks, 2))
+        pltpu.VMEM((t, 128), F32), pltpu.VMEM((t, 128), F32), pltpu.VMEM(energy.shape, BF16), DMA((chunks,))
     ]
     if last:
-        unit, near, far = more
-        d = unit.shape[1]
+        near, far = more
         out_shape = [
             jax.ShapeDtypeStruct((1, t + near.shape[1] + far.shape[1]), F32),
-            jax.ShapeDtypeStruct((d, t), F32),
             jax.ShapeDtypeStruct(energy.shape, BF16),
         ]
-        in_specs, out_specs = in_specs + anywhere(1) + vmem(2), vmem(2) + anywhere(1)
-        scratch += [pltpu.VMEM(energy.shape, BF16), pltpu.VMEM(unit.shape, BF16), DMA((chunks,))]
+        in_specs, out_specs = in_specs + vmem(2), vmem(1) + anywhere(1)
+        scratch += [pltpu.VMEM(energy.shape, BF16), DMA((chunks,))]
     return pl.pallas_call(
         functools.partial(iterate_kernel, float(total_k), last),
         out_shape=out_shape,
@@ -358,19 +352,57 @@
     )(rest, pairs, unit)
 
 
+def mean_kernel(pairs_ref, unit_hbm, scaled_hbm, mean_ref, unit, scaled, total, sems):
+    chunks, t, width = scaled.shape
+
+    def fetch(i):
+        return (
+            pltpu.make_async_copy(unit_hbm.at[i], unit.at[i], sems.at[i, 0]),
+            pltpu.make_async_copy(scaled_hbm.at[i], scaled.at[i], sems.at[i, 1]),
+        )
+
+    begin(chunks, fetch)
+    total[...] = jnp.zeros_like(total)
+
+    def work(i):
+        total[...] += lax.dot_general(unit[i], scaled[i], NT, preferred_element_type=F32)
+
+    stream(chunks, fetch, work)
+    pairs = pairs_ref[...]
+    which = lax.broadcasted_iota(jnp.int32, (t, pairs.shape[1]), 0)
+    mean_ref[...] = jnp.dot(
+        total[...], (which == pairs).astype(F32), preferred_element_type=F32, precision=lax.Precision.HIGHEST
+    )
+
+
+def mean_call(pairs, unit, scaled):
+    chunks, d, width = unit.shape
+    t = scaled.shape[1]
+    return pl.pallas_call(
+        mean_kernel,
+        out_shape=jax.ShapeDtypeStruct((d, pairs.shape[1]), F32),
+        in_specs=vmem(1) + anywhere(2),
+        out_specs=vmem(1)[0],
+        scratch_shapes=[
+            pltpu.VMEM(unit.shape, BF16), pltpu.VMEM(scaled.shape, BF16), pltpu.VMEM((d, t), F32), DMA((chunks, 2))
+        ],
+        cost_estimate=pl.CostEstimate(
+            flops=6 * t * d * chunks * width, bytes_accessed=4 * d * chunks * width, transcendentals=0
+        ),
+        compiler_params=params(LIMIT),
+        name="mean",
+    )(pairs, unit, scaled)
+
+
 def back_terms(factor, place, both_ref, pairs_ref, stud_t_ref, pull_ref, mean_ref, keep_ref, send_ref, tail_ref, back):
     d, n = pull_ref.shape
-    t = mean_ref.shape[1]
+    t = both_ref.shape[1] - pairs_ref.shape[1]
     sums = both_ref[:, :t]
     denom = both_ref[:, t : t + n]
     row = 1.0 / (sums * float(t))
     pairs = pairs_ref[:, :n]
     mass = pick(to_column(row * sums * float(t)), pairs)
-    which = lax.broadcasted_iota(jnp.int32, (t, n), 0)
-    onehot = (which == pairs).astype(F32)
-    target = jnp.dot(
-        mean_ref[...] * (row * t), onehot, preferred_element_type=F32, precision=lax.Precision.HIGHEST
-    )
+    target = mean_ref[...] * pick(to_column(row * float(t)), pairs)
     stud_t = stud_t_ref[...].astype(F32)
     terms = (pull_ref[...] * (mass / denom) - target) * factor
     back[...] = terms
@@ -395,18 +427,22 @@
         own_hbm, sends, refs = refs[1], refs[2 : GROUP + 1], refs[GROUP + 1 :]
     lhs, lhs_teach, grad, expo, scaled, v, own, sems_in, sems_out = refs
     chunks, t, width = scaled.shape
-    all_chunks = inv_ref.shape[0]
+    all_chunks = SPLIT * inv_ref.shape[0]
     n_near, n_far = near_ref.shape[1], far_ref.shape[1]
     rows = own.shape[1]
 
+    def cut(ref, i):
+        at = (first + i) // SPLIT
+        return ref.at[at, :, pl.ds(pl.multiple_of((first + i - at * SPLIT) * width, width), width)]
+
     def start_of(i):
         return pl.multiple_of((place[0] * all_chunks + first + i) * width, width)
 
     def fetches(i):
         return (
-            pltpu.make_async_copy(near_hbm.at[first + i], expo.at[i, pl.ds(0, n_near), :], sems_in.at[i, 0]),
-            pltpu.make_async_copy(far_hbm.at[first + i], expo.at[i, pl.ds(n_near, n_far), :], sems_in.at[i, 3]),
-            pltpu.make_async_copy(scaled_hbm.at[first + i], scaled.at[i], sems_in.at[i, 1]),
+            pltpu.make_async_copy(cut(near_hbm, i), expo.at[i, pl.ds(0, n_near), :], sems_in.at[i, 0]),
+            pltpu.make_async_copy(cut(far_hbm, i), expo.at[i, pl.ds(n_near, n_far), :], sems_in.at[i, 3]),
+            pltpu.make_async_copy(cut(scaled_hbm, i), scaled.at[i], sems_in.at[i, 1]),
             pltpu.make_async_copy(v_hbm.at[:, pl.ds(start_of(i), width)], v.at[i], sems_in.at[i, 2]),
         )
 
@@ -432,7 +468,7 @@
     def work(i):
         head = jnp.dot(lhs[...], expo[i], preferred_element_type=F32)
         head = head + jnp.dot(lhs_teach[...], scaled[i], preferred_element_type=F32)
-        inv = inv_ref[first + i]
+        inv = cut(inv_ref, i)[...]
         unit = v[i].astype(F32) * inv
         proj = jnp.sum(unit * head, axis=0, keepdims=True)
         grad[...] = (head - unit * proj) * inv
@@ -450,7 +486,7 @@
 def head_call(first, chunks, place, both, pairs, students, inv, scaled, v, factor, rows, more):
     near, far, near_t, far_t, weight, more_weight = students
     d, s = near_t.shape[0], pairs.shape[1]
-    _, t, width = scaled.shape
+    t, width = scaled.shape[1], scaled.shape[2] // SPLIT
     kl = chunks * width
     out_shape = [jax.ShapeDtypeStruct((rows, v.shape[1]), F32)] + [jax.ShapeDtypeStruct((rows, kl), BF16)] * (GROUP - 1)
     out_specs = anywhere(1) + vmem(GROUP - 1)
@@ -484,6 +520,47 @@
     )(place, both, pairs, near_t, far_t, weight, more_weight, inv, near, far, scaled, v, *more)
 
 
+def place_kernel(first, place, *refs):
+    arrived, refs = refs[: GROUP - 1], refs[GROUP:]
+    out_hbm, got, wide, sems_in, sems_out = refs
+    width = wide.shape[2]
+    count = out_hbm.shape[1] // GROUP
+
+    def fetch(n):
+        return pltpu.make_async_copy(arrived[n], got.at[n], sems_in.at[n])
+
+    def store(n):
+        start = pl.multiple_of((place[0] ^ (n + 1)) * count + first, 128)
+        return pltpu.make_async_copy(wide.at[n], out_hbm.at[:, pl.ds(start, width)], sems_out.at[n])
+
+    for n in range(GROUP - 1):
+        fetch(n).start()
+    for n in range(GROUP - 1):
+        fetch(n).wait()
+        wide[n] = got[n].astype(F32)
+        store(n).start()
+    for n in range(GROUP - 1):
+        store(n).wait()
+
+
+def place_call(first, place, arrived, out):
+    rows, width = arrived[0].shape
+    return pl.pallas_call(
+        functools.partial(place_kernel, first),
+        out_shape=jax.ShapeDtypeStruct(out.shape, F32),
+        in_specs=[SMEM] + anywhere(GROUP),
+        out_specs=anywhere(1)[0],
+        scratch_shapes=[
+            pltpu.VMEM((GROUP - 1, rows, width), BF16), pltpu.VMEM((GROUP - 1, rows, width), F32),
+            DMA((GROUP - 1,)), DMA((GROUP - 1,)),
+        ],
+        input_output_aliases={GROUP: 0},
+        cost_estimate=pl.CostEstimate(flops=0, bytes_accessed=18 * rows * width, transcendentals=0),
+        compiler_params=params(LIMIT),
+        name="place",
+    )(place, *arrived, out)
+
+
 def finish_kernel(t, place, both_ref, denom_ref, pairs_ref, stud_ref, *refs):
     terms, (grad_ref, loss_ref, unit) = refs[:GROUP], refs[GROUP:]
     total = (terms[0][...] + terms[1][...]) + (terms[2][...] + terms[3][...])
@@ -531,13 +608,21 @@
     def swap_proto(x, n):
         return lax.ppermute(x, "proto", [(j, j ^ n) for j in range(n_proto)])
 
+    def over(swap, size, x):
+        n = 1
+        while n < size:
+            x = (x + swap(x, n)) + (swap(x, 2 * n) + swap(x, 3 * n))
+            n *= 4
+        return x
+
+    def over_proto(x):
+        return over(swap_proto, n_proto, x)
+
+    def over_group(x):
+        return over(swap_rows, GROUP, x)
+
     def total(x):
-        for swap, size in ((swap_proto, n_proto), (swap_rows, GROUP)):
-            n = 1
-            while n < size:
-                x = (x + swap(x, n)) + (swap(x, 2 * n) + swap(x, 3 * n))
-                n *= 4
-        return x
+        return over_group(over_proto(x))
 
     def join(x, n, other=None):
         other = swap_rows(x, n) if other is None else other
@@ -560,7 +645,6 @@
         return (digits[:, 0] * 64.0 + digits[:, 1]).astype(jnp.int32).reshape(1, -1)
 
     near_pairs = pairs_of(near)
-    expo_near, denom_near, near_t, weight, pull = student_call(near, near_pairs, unit, t, True)
     n = GROUP
     while n < n_rows:
         other = swap_rows(teach_all, n)
@@ -572,21 +656,26 @@
         far = jnp.concatenate([far, swap_rows(jnp.concatenate([near, far], axis=0), n)], axis=0)
         n *= 2
     energy, sums = energy_call(teach_all.reshape(t, d), unit, total_k)
-    sums = lax.optimization_barrier((total(sums), denom_near))[0]
+    sums = over_proto(sums)
+    near = lax.optimization_barrier((near, sums))[0]
+    expo_near, denom_near, near_t, weight, pull = student_call(near, near_pairs, unit, t, True)
+    sums = lax.optimization_barrier((over_group(sums), denom_near))[0]
     far_pairs = pairs_of(far)
     expo_far, denom_far, far_t, more_weight = student_call(far, far_pairs, unit, t, False)
     pairs = jnp.concatenate([near_pairs, far_pairs], axis=1)
     (sums,) = iterate_call(sums, energy, total_k)
     sums = lax.optimization_barrier((sums, far))[0]
-    both, mean, scaled = iterate_call(total(sums), energy, total_k, (unit, denom_near, denom_far))
+    both, scaled = iterate_call(total(sums), energy, total_k, (denom_near, denom_far))
+    mean = mean_call(near_pairs, unit, scaled)
     both = total(both)
     students = (expo_near, expo_far, near_t, far_t, weight, more_weight)
 
     rows = d // n_rows
-    chunks = CHUNKS // PARTS
+    width = kl // (CHUNKS * SPLIT)
+    offsets = [sum(SIZES[:n]) for n in range(len(SIZES))]
     more = (pull, mean)
     pieces = []
-    for first in range(0, CHUNKS, chunks):
+    for first, chunks in zip(offsets, SIZES):
         out = head_call(
             first, chunks, place, both, pairs, students, inv, scaled, v, factor, rows, more
         )
@@ -596,10 +685,13 @@
         arrived = []
         for n in range(1, GROUP):
             share = out[n]
-            if pieces:
-                share, pieces[-1][n - 1] = lax.optimization_barrier((share, pieces[-1][n - 1]))
+            if pieces and n == GROUP - 1:
+                share = lax.optimization_barrier((share, pieces[-1]))[0]
             arrived.append(swap_rows(share, n))
         pieces.append(arrived)
+    proto_grad = out[0]
+    for part, arrived in enumerate(pieces[:-1]):
+        proto_grad = place_call(offsets[part] * width, place, arrived, proto_grad)
     n = n_proto // 2
     while n >= 1:
         if n < n_proto // 2:
@@ -608,7 +700,7 @@
             send = lax.dynamic_slice_in_dim(body_rows, (1 - bit) * height, height, 0)
             body_rows = lax.dynamic_slice_in_dim(body_rows, bit * height, height, 0)
             send = jnp.concatenate([send, tail], axis=0)
-        got = swap_proto(send, n)
+        got = lax.optimization_barrier((swap_proto(send, n), out[1] if n == n_proto // 2 else proto_grad))[0]
         height = body_rows.shape[0]
         body_rows, tail = body_rows + got[:height], tail + got[height:]
         n //= 2
@@ -618,12 +710,7 @@
         return lax.dynamic_slice_in_dim(terms, (at ^ n) * s_dev, s_dev, 1)
 
     parts = [block(0)] + [swap_rows(block(n), n) for n in range(1, GROUP)]
-    pieces[-1] = lax.optimization_barrier((pieces[-1], parts))[0]
-    proto_grad = out[0]
-    for part, arrived in enumerate(pieces):
-        for n, got in enumerate(arrived, 1):
-            start = (at ^ n) * kl + part * (kl // PARTS)
-            proto_grad = lax.dynamic_update_slice(proto_grad, got.astype(F32), (0, start))
+    proto_grad = place_call(offsets[-1] * width, place, pieces[-1], proto_grad)
     own = lax.dynamic_slice_in_dim(both, t + at * s_dev, s_dev, 1)
     student_grad, loss = finish_call(t, place, both, own, own_pairs, student_features, parts, d // n_proto)
     return (proto_grad, student_grad.T, loss.reshape(s_dev))

time: 121 us -> 116 us (0.959)
  waiting for transfers between devices: 19.6 us -> 12.8 us
  local copies, waits for them, and re-layouts: 0.33 us -> 6.71 us
  other arithmetic: 5.59 us -> 1.3 us
  starting transfers between devices: 36.3 us -> 39.4 us
  Pallas kernels: 57.3 us -> 54.6 us
    pallas_call x0 -> x3, Pallas kernels: none -> 7.97 us  [the longest x2 4.59 us: place_call(): pl.pallas_call(functools.partial(place_kernel, first), out_shape=jax.Shap...]
    ppermute x23, waiting for transfers between devices: 14.5 us -> 8 us  [swap_rows(): return lax.ppermute(x, 'rows', [(j, j ^ n) for j in range(n_rows)])]
    unnamed x7 -> x17, local copies, waits for them, and re-layouts: 0.02 us -> 6.4 us
    dynamic_update_slice x6 -> x0, other arithmetic: 4.97 us -> none  [body(): lax.dynamic_update_slice(proto_grad, got.astype(F32), (0, start))]
    pallas_call x2, Pallas kernels: 10.8 us -> 6.53 us  [iterate_call(): pl.pallas_call(functools.partial(iterate_kernel, float(total_k), last), o...]
    ppermute x23, starting transfers between devices: 29 us -> 32.3 us  [swap_rows(): return lax.ppermute(x, 'rows', [(j, j ^ n) for j in range(n_rows)])]
    pallas_call x2, Pallas kernels: 15.8 us -> 13.6 us  [student_call(): pl.pallas_call(functools.partial(student_kernel, 2 * (rest.shape[1] - 16)...]
    pallas_call x1, Pallas kernels: 5.47 us -> 3.59 us  [energy_call(): pl.pallas_call(functools.partial(energy_kernel, float(total_k)), out_shap...]
  transfers between devices with their start and end apart: 34 -> 34, of which waited for: 14 -> 10; matrix products, arithmetic and copies ran while one was open for 3% -> 1% of each run, Pallas kernels for 28% -> 30%
where the time goes in v5:
time: 116 us
  Pallas kernels  54.6 us (47%)
  starting transfers between devices  39.4 us (34%)
  waiting for transfers between devices  12.8 us (11%)
  local copies, waits for them, and re-layouts  6.71 us (6%)
  other arithmetic  1.3 us (1%)
    ppermute x23, starting transfers between devices, swap_rows(): return lax.ppermute(x, 'rows', [(j, j ^ n) for j in range(n_rows)])  32.3 us
    pallas_call x2, Pallas kernels, head_call(): pl.pallas_call(functools.partial(head_kernel, factor, first), out_shape=o...  16.2 us
    pallas_call x2, Pallas kernels, student_call(): pl.pallas_call(functools.partial(student_kernel, 2 * (rest.shape[1] - 16)...  13.6 us
    ppermute x23, waiting for transfers between devices, swap_rows(): return lax.ppermute(x, 'rows', [(j, j ^ n) for j in range(n_rows)])  8 us
    ppermute x11, starting transfers between devices, swap_proto(): return lax.ppermute(x, 'proto', [(j, j ^ n) for j in range(n_proto)])  7.15 us
    pallas_call x2, Pallas kernels, iterate_call(): pl.pallas_call(functools.partial(iterate_kernel, float(total_k), last), o...  6.53 us
    unnamed x17, local copies, waits for them, and re-layouts  6.4 us
    ppermute x11, waiting for transfers between devices, swap_proto(): return lax.ppermute(x, 'proto', [(j, j ^ n) for j in range(n_proto)])  4.78 us
  transfers between devices with their start and end apart: 34, of which 10 were waited for; matrix products, arithmetic and copies ran while one was open for 1% of the time, Pallas kernels for 30%

profile of v5, /device:TPU:0, one launch (start us, length us, event | category | flops | bytes accessed | tf_op | source)
XLA Modules:
  0.0 115.8 jit_solution(14396519301697852939)
XLA Ops:
  0.6 1.7 %prepare.1 = bf16[208,256]{1,0:T(8,128)(2,1)} custom-call(bf16[32,256]{1,0:T(8,128)(2,1)} %teach_ref.1, bf16[160,256]{1,0:T(8,128)(2,1)} %stud_ref.3, s32[1,160]{1,0:T(1,128)} %bitcast.17), custom_call_target="tpu_custom_call" | custom-call | tf_op jit(solution)/shard_map/prepare/pallas_call | solution.py:106
  2.3 4.0 %collective-permute-start.2 = (bf16[208,256]{1,0:T(8,128)(2,1)}, bf16[208,256]{1,0:T(8,128)(2,1)S(1)}, u32[]{:S(2)}, u32[]{:S(2)}) collective-permute-start(bf16[208,256]{1,0:T(8,128)(2,1)} %prepare.1), channel_id=1, source_target_pairs={{0,12},{4,8},{8,4},{12,0},{16,28},{20,24},{24,20},{28,16},{1,13},{... | collective-permute-start | bytes 319496 | tf_op jit(solution)/shard_map/ppermute | solution.py:606
  6.2 0.5 collective-permute-start
  6.8 0.0 collective-permute-start.1
  6.8 0.1 pad_add_fusion.place
  6.9 3.6 %unit.1 = (bf16[4,256,2048]{2,1,0:T(8,128)(2,1)S(1)}, f32[4,1,2048]{2,1,0:T(1,128)S(1)}) custom-call(s32[4]{0:T(128)S(1)} %pad_add_fusion.place, bf16[256,32768]{1,0:T(8,128)(2,1)} %v_hbm.5), custom_call_target="tpu_custom_call" | custom-call | flops 8388608 | bytes 8388608 | tf_op jit(solution)/shard_map/unit/pallas_call | solution.py:145
  10.5 2.0 %copy-done.2 = bf16[4,256,2048]{2,1,0:T(8,128)(2,1)} copy-done((bf16[4,256,2048]{2,1,0:T(8,128)(2,1)}, bf16[4,256,2048]{2,1,0:T(8,128)(2,1)S(1)}, u32[]{:S(2)}) %copy-start.2) | copy-done | bytes 4194328
  12.6 3.1 %collective-permute-start.3 = (bf16[4,32,256]{2,1,0:T(8,128)(2,1)S(1)}, bf16[4,32,256]{2,1,0:T(8,128)(2,1)S(1)}, u32[]{:S(2)}, u32[]{:S(2)}) collective-permute-start(bf16[4,32,256]{2,1,0:T(8,128)(2,1)S(1)} %pad_maximum_fusion.3), channel_id=1, source_target_pairs={{0,16},{4,20},{8,24},{12,28},{16,0},{20,4},{24,8},{28,12},{1,17},{... | collective-permute-start | bytes 196616 | tf_op jit(solution)/shard_map/ppermute | solution.py:606
  15.7 0.1 convert_element_type.34.pairs_ref
  15.8 0.1 pad_maximum_fusion
  15.9 2.1 %collective-permute-done.3 = bf16[4,32,256]{2,1,0:T(8,128)(2,1)S(1)} collective-permute-done((bf16[4,32,256]{2,1,0:T(8,128)(2,1)S(1)}, bf16[4,32,256]{2,1,0:T(8,128)(2,1)S(1)}, u32[]{:S(2)}, u32[]{:S(2)}) %collective-permute-start.3) | collective-permute-done | bytes 65568 | tf_op jit(solution)/shard_map/ppermute | solution.py:606
  18.1 2.2 %copy-done.3 = bf16[4,256,2048]{2,1,0:T(8,128)(2,1)S(1)} copy-done((bf16[4,256,2048]{2,1,0:T(8,128)(2,1)S(1)}, bf16[4,256,2048]{2,1,0:T(8,128)(2,1)}, u32[]{:S(2)}) %copy-start.3) | copy-done | bytes 4194328
  20.3 3.6 %energy.1 = (bf16[4,256,2048]{2,1,0:T(8,128)(2,1)S(1)}, f32[1,256]{1,0:T(1,128)S(1)}) custom-call(bf16[256,256]{1,0:T(8,128)(2,1)S(1)} %bitcast.16, bf16[4,256,2048]{2,1,0:T(8,128)(2,1)S(1)} %copy-done.3), custom_call_target="tpu_custom_call" | custom-call | flops 1073741824 | bytes 8388608 | tf_op jit(solution)/shard_map/energy/pallas_call | solution.py:190
  23.9 0.1 collective-permute-start.4
  23.9 1.8 %collective-permute-start.5 = (f32[1,256]{1,0:T(1,128)S(1)}, f32[1,256]{1,0:T(1,128)S(1)}, u32[]{:S(2)}, u32[]{:S(2)}) collective-permute-start(f32[1,256]{1,0:T(1,128)S(1)} %get-tuple-element.45), channel_id=1, source_target_pairs={{0,2},{1,3},{2,0},{3,1},{4,6},{5,7},{6,4},{7,5},{8,10},{9,11},{10,... | collective-permute-start | bytes 3080 | tf_op jit(solution)/shard_map/ppermute | solution.py:609
  25.8 0.1 collective-permute-start.6
  25.9 2.9 %collective-permute-start.10 = (bf16[4,176,256]{2,1,0:T(8,128)(2,1)S(1)}, bf16[4,176,256]{2,1,0:T(8,128)(2,1)S(1)}, u32[]{:S(2)}, u32[]{:S(2)}) collective-permute-start(bf16[4,176,256]{2,1,0:T(8,128)(2,1)S(1)} %slice.49.rest_ref), channel_id=1, source_target_pairs={{0,16},{4,20},{8,24},{12,28},{16,0},{20,4},{24,8},{28,12},{1,17},{... | collective-permute-start | bytes 1081352 | tf_op jit(solution)/shard_map/ppermute | solution.py:606
  28.8 1.6 %collective-permute-start.7 = (f32[1,256]{1,0:T(1,128)S(1)}, f32[1,256]{1,0:T(1,128)S(1)}, u32[]{:S(2)}, u32[]{:S(2)}) collective-permute-start(f32[1,256]{1,0:T(1,128)S(1)} %add_add_fusion.5), channel_id=1, source_target_pairs={{0,4},{4,0},{8,12},{12,8},{16,20},{20,16},{24,28},{28,24},{1,5},{5... | collective-permute-start | bytes 3080 | tf_op jit(solution)/shard_map/ppermute | solution.py:606
  30.4 2.1 %collective-permute-start.8 = (f32[1,256]{1,0:T(1,128)S(1)}, f32[1,256]{1,0:T(1,128)S(1)}, u32[]{:S(2)}, u32[]{:S(2)}) collective-permute-start(f32[1,256]{1,0:T(1,128)S(1)} %add_add_fusion.5), channel_id=1, source_target_pairs={{0,8},{4,12},{8,0},{12,4},{16,24},{20,28},{24,16},{28,20},{1,9},{5... | collective-permute-start | bytes 3080 | tf_op jit(solution)/shard_map/ppermute | solution.py:606
  32.5 8.0 %student_near.1 = (bf16[4,640,2048]{2,1,0:T(8,128)(2,1)}, f32[1,640]{1,0:T(1,128)S(1)}, bf16[256,640]{1,0:T(8,128)(2,1)S(1)}, f32[256,256]{1,0:T(8,128)S(1)}, f32[256,640]{1,0:T(8,128)S(1)}) custom-call(bf16[4,176,256]{2,1,0:T(8,128)(2,1)S(1)} %slice.49.rest_ref, s32[1,640]{1,0:T(1,128)S(1)} %convert_element_type.34.pairs_ref, ...), custom_call_target="tpu_custom_call" | custom-call | flops 5368709120 | bytes 10485760 | tf_op jit(solution)/shard_map/student_near/pallas_call | solution.py:341
  40.5 2.6 %iterate.1 = f32[1,256]{1,0:T(1,128)S(1)} custom-call(f32[1,256]{1,0:T(1,128)S(1)} %add_add_fusion.4.sum_in, bf16[4,256,2048]{2,1,0:T(8,128)(2,1)S(1)} %get-tuple-element.49.energy_hbm), custom_call_target="tpu_custom_call" | custom-call | flops 8388608 | bytes 8388608 | tf_op jit(solution)/shard_map/iterate/pallas_call | solution.py:267
  43.1 2.3 %collective-permute-done.10.rest_ref = bf16[4,176,256]{2,1,0:T(8,128)(2,1)S(1)} collective-permute-done((bf16[4,176,256]{2,1,0:T(8,128)(2,1)S(1)}, bf16[4,176,256]{2,1,0:T(8,128)(2,1)S(1)}, u32[]{:S(2)}, u32[]{:S(2)}) %collective-permute-start.10) | collective-permute-done | bytes 360480 | tf_op jit(solution)/shard_map/ppermute | solution.py:606
  45.5 1.5 %collective-permute-start.12 = (f32[1,256]{1,0:T(1,128)S(1)}, f32[1,256]{1,0:T(1,128)S(1)}, u32[]{:S(2)}, u32[]{:S(2)}) collective-permute-start(f32[1,256]{1,0:T(1,128)S(1)} %iterate.1), channel_id=1, source_target_pairs={{0,2},{1,3},{2,0},{3,1},{4,6},{5,7},{6,4},{7,5},{8,10},{9,11},{10,... | collective-permute-start | bytes 3080 | tf_op jit(solution)/shard_map/ppermute | solution.py:609
  47.0 0.3 collective-permute-start.13
  47.4 0.1 convert_element_type.37.pairs_ref
  47.4 1.6 %collective-permute-done.12 = f32[1,256]{1,0:T(1,128)S(1)} collective-permute-done((f32[1,256]{1,0:T(1,128)S(1)}, f32[1,256]{1,0:T(1,128)S(1)}, u32[]{:S(2)}, u32[]{:S(2)}) %collective-permute-start.12) | collective-permute-done | bytes 1056 | tf_op jit(solution)/shard_map/ppermute | solution.py:609
  49.0 0.9 collective-permute-done.13
  50.0 1.5 %collective-permute-start.14 = (f32[1,256]{1,0:T(1,128)S(1)}, f32[1,256]{1,0:T(1,128)S(1)}, u32[]{:S(2)}, u32[]{:S(2)}) collective-permute-start(f32[1,256]{1,0:T(1,128)S(1)} %add_add_fusion.3), channel_id=1, source_target_pairs={{0,4},{4,0},{8,12},{12,8},{16,20},{20,16},{24,28},{28,24},{1,5},{5... | collective-permute-start | bytes 3080 | tf_op jit(solution)/shard_map/ppermute | solution.py:606
  51.5 0.8 collective-permute-start.15
  52.2 1.2 %collective-permute-start.16 = (f32[1,256]{1,0:T(1,128)S(1)}, f32[1,256]{1,0:T(1,128)S(1)}, u32[]{:S(2)}, u32[]{:S(2)}) collective-permute-start(f32[1,256]{1,0:T(1,128)S(1)} %add_add_fusion.3), channel_id=1, source_target_pairs={{0,12},{4,8},{8,4},{12,0},{16,28},{20,24},{24,20},{28,16},{1,13},{... | collective-permute-start | bytes 3080 | tf_op jit(solution)/shard_map/ppermute | solution.py:606
  53.5 2.2 %copy-done.4 = bf16[4,256,2048]{2,1,0:T(8,128)(2,1)S(1)} copy-done((bf16[4,256,2048]{2,1,0:T(8,128)(2,1)S(1)}, bf16[4,256,2048]{2,1,0:T(8,128)(2,1)}, u32[]{:S(2)}) %copy-start.4) | copy-done | bytes 4194328
  55.7 5.7 %student_far.1 = (bf16[4,640,2048]{2,1,0:T(8,128)(2,1)}, f32[1,640]{1,0:T(1,128)S(1)}, bf16[256,640]{1,0:T(8,128)(2,1)S(1)}, f32[256,256]{1,0:T(8,128)S(1)}) custom-call(bf16[4,176,256]{2,1,0:T(8,128)(2,1)S(1)} %collective-permute-done.10.rest_ref, s32[1,640]{1,0:T(1,128)S(1)} %convert_element_type.37.pairs_ref, bf16[4,256,2048]{2,1,0:T(8,128)(2,1)S(1)} %copy-done.4), custom_call_target="tpu_custom_call" | custom-call | flops 5368709120 | bytes 10485760 | tf_op jit(solution)/shard_map/student_far/pallas_call | solution.py:341
  61.4 3.9 %iterate_last.1 = (f32[1,1536]{1,0:T(1,128)S(1)}, bf16[4,256,2048]{2,1,0:T(8,128)(2,1)S(1)}) custom-call(f32[1,256]{1,0:T(1,128)S(1)} %add_add_fusion.2.sum_in, bf16[4,256,2048]{2,1,0:T(8,128)(2,1)S(1)} %copy-done.1, f32[1,640]{1,0:T(1,128)S(1)} %get-tuple-element.47.refs_0_, f32[1,640]{1,0:T(1,128)S(1)} %get-tuple-element.52.refs_1_), custom_call_target="tpu_custom_call" | custom-call | flops 8388608 | bytes 8388608 | tf_op jit(solution)/shard_map/iterate_last/pallas_call | solution.py:267
  65.4 0.1 collective-permute-start.17
  65.4 0.7 collective-permute-start.18
  66.2 1.1 collective-permute-start.19
  67.3 1.8 %collective-permute-done.18 = f32[1,1536]{1,0:T(1,128)S(1)} collective-permute-done((f32[1,1536]{1,0:T(1,128)S(1)}, f32[1,1536]{1,0:T(1,128)S(1)}, u32[]{:S(2)}, u32[]{:S(2)}) %collective-permute-start.18) | collective-permute-done | bytes 6176 | tf_op jit(solution)/shard_map/ppermute | solution.py:609
  69.1 0.1 collective-permute-done.19
  69.2 1.6 %collective-permute-start.20 = (f32[1,1536]{1,0:T(1,128)S(1)}, f32[1,1536]{1,0:T(1,128)S(1)}, u32[]{:S(2)}, u32[]{:S(2)}) collective-permute-start(f32[1,1536]{1,0:T(1,128)S(1)} %add_add_fusion.1), channel_id=1, source_target_pairs={{0,4},{4,0},{8,12},{12,8},{16,20},{20,16},{24,28},{28,24},{1,5},{5... | collective-permute-start | bytes 18440 | tf_op jit(solution)/shard_map/ppermute | solution.py:606
  70.8 0.8 collective-permute-start.21
  71.6 1.2 %collective-permute-start.22 = (f32[1,1536]{1,0:T(1,128)S(1)}, f32[1,1536]{1,0:T(1,128)S(1)}, u32[]{:S(2)}, u32[]{:S(2)}) collective-permute-start(f32[1,1536]{1,0:T(1,128)S(1)} %add_add_fusion.1), channel_id=1, source_target_pairs={{0,12},{4,8},{8,4},{12,0},{16,28},{20,24},{24,20},{28,16},{1,13},{... | collective-permute-start | bytes 18440 | tf_op jit(solution)/shard_map/ppermute | solution.py:606
  72.8 3.4 %mean.1.refs_1_ = f32[256,640]{1,0:T(8,128)S(1)} custom-call(s32[1,640]{1,0:T(1,128)S(1)} %convert_element_type.34.pairs_ref, bf16[4,256,2048]{2,1,0:T(8,128)(2,1)S(1)} %copy-done.4, bf16[4,256,2048]{2,1,0:T(8,128)(2,1)S(1)} %get-tuple-element.61.scaled_hbm), custom_call_target="tpu_custom_call" | custom-call | flops 3221225472 | bytes 8388608 | tf_op jit(solution)/shard_map/mean/pallas_call | solution.py:381
  76.2 9.4 %head.2 = (f32[32,32768]{1,0:T(8,128)}, bf16[32,5120]{1,0:T(8,128)(2,1)S(1)}, bf16[32,5120]{1,0:T(8,128)(2,1)S(1)}, bf16[32,5120]{1,0:T(8,128)(2,1)S(1)}, f32[12...) custom-call(s32[4]{0:T(128)S(1)} %pad_add_fusion.place, f32[1,1536]{1,0:T(1,128)S(1)} %add_add_fusion.both_ref, ...), custom_call_target="tpu_custom_call" | custom-call | flops 8053063680 | bytes 18350080 | tf_op jit(solution)/shard_map/head/pallas_call | solution.py:508
  85.6 1.6 %collective-permute-start.25 = (bf16[32,5120]{1,0:T(8,128)(2,1)S(1)}, bf16[32,5120]{1,0:T(8,128)(2,1)S(1)}, u32[]{:S(2)}, u32[]{:S(2)}) collective-permute-start(bf16[32,5120]{1,0:T(8,128)(2,1)S(1)} %get-tuple-element.67), channel_id=1, source_target_pairs={{0,4},{4,0},{8,12},{12,8},{16,20},{20,16},{24,28},{28,24},{1,5},{5... | collective-permute-start | bytes 983048 | tf_op jit(solution)/shard_map/ppermute | solution.py:606
  87.2 0.8 collective-permute-start.26
  87.9 1.2 %collective-permute-start.27 = (bf16[32,5120]{1,0:T(8,128)(2,1)S(1)}, bf16[32,5120]{1,0:T(8,128)(2,1)S(1)}, u32[]{:S(2)}, u32[]{:S(2)}) collective-permute-start(bf16[32,5120]{1,0:T(8,128)(2,1)S(1)} %get-tuple-element.69), channel_id=1, source_target_pairs={{0,12},{4,8},{8,4},{12,0},{16,28},{20,24},{24,20},{28,16},{1,13},{... | collective-permute-start | bytes 983048 | tf_op jit(solution)/shard_map/ppermute | solution.py:606
  89.2 1.4 %collective-permute-start.29 = (f32[136,640]{1,0:T(8,128)S(1)}, f32[136,640]{1,0:T(8,128)S(1)}, u32[]{:S(2)}, u32[]{:S(2)}) collective-permute-start(f32[136,640]{1,0:T(8,128)S(1)} %get-tuple-element.73), channel_id=1, source_target_pairs={{0,2},{1,3},{2,0},{3,1},{4,6},{5,7},{6,4},{7,5},{8,10},{9,11},{10,... | collective-permute-start | bytes 1044488 | tf_op jit(solution)/shard_map/ppermute | solution.py:609
  90.5 6.8 %head.3 = (f32[32,32768]{1,0:T(8,128)}, bf16[32,3072]{1,0:T(8,128)(2,1)S(1)}, bf16[32,3072]{1,0:T(8,128)(2,1)S(1)}, bf16[32,3072]{1,0:T(8,128)(2,1)S(1)}) custom-call(s32[4]{0:T(128)S(1)} %pad_add_fusion.place, f32[1,1536]{1,0:T(1,128)S(1)} %add_add_fusion.both_ref, ...), custom_call_target="tpu_custom_call", output_to_operand_aliasing={{0}: (12, {})} | custom-call | flops 4831838208 | bytes 11010048 | tf_op jit(solution)/shard_map/head/pallas_call | solution.py:508
  97.4 0.3 collective-permute-done.29
  97.8 0.7 pad_maximum_fusion.1
  98.5 1.5 %collective-permute-start.23 = (bf16[32,3072]{1,0:T(8,128)(2,1)S(1)}, bf16[32,3072]{1,0:T(8,128)(2,1)S(1)}, u32[]{:S(2)}, u32[]{:S(2)}) collective-permute-start(bf16[32,3072]{1,0:T(8,128)(2,1)S(1)} %get-tuple-element.64), channel_id=1, source_target_pairs={{0,4},{4,0},{8,12},{12,8},{16,20},{20,16},{24,28},{28,24},{1,5},{5... | collective-permute-start | bytes 589832 | tf_op jit(solution)/shard_map/ppermute | solution.py:606
  100.0 0.8 collective-permute-start.24
  100.8 2.2 %collective-permute-done.27.refs_2_ = bf16[32,5120]{1,0:T(8,128)(2,1)S(1)} collective-permute-done((bf16[32,5120]{1,0:T(8,128)(2,1)S(1)}, bf16[32,5120]{1,0:T(8,128)(2,1)S(1)}, u32[]{:S(2)}, u32[]{:S(2)}) %collective-permute-start.27) | collective-permute-done | bytes 327712 | tf_op jit(solution)/shard_map/ppermute | solution.py:606
  102.9 1.7 %collective-permute-start.28 = (bf16[32,3072]{1,0:T(8,128)(2,1)S(1)}, bf16[32,3072]{1,0:T(8,128)(2,1)S(1)}, u32[]{:S(2)}, u32[]{:S(2)}) collective-permute-start(bf16[32,3072]{1,0:T(8,128)(2,1)S(1)} %get-tuple-element.70), channel_id=1, source_target_pairs={{0,12},{4,8},{8,4},{12,0},{16,28},{20,24},{24,20},{28,16},{1,13},{... | collective-permute-start | bytes 589832 | tf_op jit(solution)/shard_map/ppermute | solution.py:606
  104.6 2.2 %place.2.refs_3_ = f32[32,32768]{1,0:T(8,128)} custom-call(s32[4]{0:T(128)S(1)} %pad_add_fusion.place, bf16[32,5120]{1,0:T(8,128)(2,1)S(1)} %collective-permute-done.25.refs_0_, bf16[32,5120]{1,0:T(8,128)(2,1)S(1)} %collective-permute-done.26.refs_1_, bf16[32,5120]{1,0:T(8,128)(2,1)S(1)} %collective-permute-done.27.refs_2_, ...), custom_call_target="tpu_custom_call", output_to_operand_aliasing={{}: (4, {})} | custom-call | bytes 2949120 | tf_op jit(solution)/shard_map/place/pallas_call | solution.py:548
  106.9 0.2 fusion
  107.1 0.6 collective-permute-start.31
  107.7 1.3 %collective-permute-start.32 = (f32[72,160]{1,0:T(8,128)S(1)}, f32[72,160]{1,0:T(8,128)S(1)}, u32[]{:S(2)}, u32[]{:S(2)}) collective-permute-start(f32[72,160]{1,0:T(8,128)S(1)} %get-tuple-element.86), channel_id=1, source_target_pairs={{0,8},{4,12},{8,0},{12,4},{16,24},{20,28},{24,16},{28,20},{1,9},{5... | collective-permute-start | bytes 138248 | tf_op jit(solution)/shard_map/ppermute | solution.py:606
  109.0 1.7 %collective-permute-start.33 = (f32[72,160]{1,0:T(8,128)S(1)}, f32[72,160]{1,0:T(8,128)S(1)}, u32[]{:S(2)}, u32[]{:S(2)}) collective-permute-start(f32[72,160]{1,0:T(8,128)S(1)} %get-tuple-element.83), channel_id=1, source_target_pairs={{0,12},{4,8},{8,4},{12,0},{16,28},{20,24},{24,20},{28,16},{1,13},{... | collective-permute-start | bytes 138248 | tf_op jit(solution)/shard_map/ppermute | solution.py:606
  110.7 0.1 constant_dynamic-slice_fusion.1.denom_ref
  110.7 1.2 %collective-permute-done.28.refs_2_ = bf16[32,3072]{1,0:T(8,128)(2,1)S(1)} collective-permute-done((bf16[32,3072]{1,0:T(8,128)(2,1)S(1)}, bf16[32,3072]{1,0:T(8,128)(2,1)S(1)}, u32[]{:S(2)}, u32[]{:S(2)}) %collective-permute-start.28) | collective-permute-done | bytes 196640 | tf_op jit(solution)/shard_map/ppermute | solution.py:606
  112.0 2.4 %place.3 = f32[32,32768]{1,0:T(8,128)} custom-call(s32[4]{0:T(128)S(1)} %pad_add_fusion.place, bf16[32,3072]{1,0:T(8,128)(2,1)S(1)} %collective-permute-done.23.refs_0_, bf16[32,3072]{1,0:T(8,128)(2,1)S(1)} %collective-permute-done.24.refs_1_, bf16[32,3072]{1,0:T(8,128)(2,1)S(1)} %collective-permute-done.28.refs_2_, ...), custom_call_target="tpu_custom_call", output_to_operand_aliasing={{}: (4, {})} | custom-call | bytes 1769472 | tf_op jit(solution)/shard_map/place/pallas_call | solution.py:548
  114.4 0.1 collective-permute-done.33.refs_3_
  114.5 1.4 %finish.1 = (f32[64,160]{1,0:T(8,128)}, f32[1,160]{1,0:T(1,128)}) custom-call(s32[4]{0:T(128)S(1)} %pad_add_fusion.place, f32[1,1536]{1,0:T(1,128)S(1)} %add_add_fusion.both_ref, f32[1,160]{1,0:T(1,128)S(1)} %constant_dynamic-slice_fusion.1.denom_ref, s32[1,160]{1,0:T(1,128)S(1)} %bitcast.18, bf16[160,256]{1,0:T(8,128)(2,1)S(1)} %copy-done.5, ...), custom_call_target="tpu_custom_call" | custom-call | tf_op jit(solution)/shard_map/finish/pallas_call | solution.py:581
  (62 shorter events, 0.4 us)
Async XLA Ops:
  2.3 10.2 %collective-permute-start.2 = (bf16[208,256]{1,0:T(8,128)(2,1)}, bf16[208,256]{1,0:T(8,128)(2,1)S(1)}, u32[]{:S(2)}, u32[]{:S(2)}) collective-permute-start(bf16[208,256]{1,0:T(8,128)(2,1)} %prepare.1), channel_id=1, source_target_pairs={{0,12},{4,8},{8,4},{12,0},{16,28},{20,24},{24,20},{28,16},{1,13},{... | collective-permute-start | bytes 319496 | tf_op jit(solution)/shard_map/ppermute | solution.py:606
  6.2 6.3 %collective-permute-start = (bf16[208,256]{1,0:T(8,128)(2,1)}, bf16[208,256]{1,0:T(8,128)(2,1)S(1)}, u32[]{:S(2)}, u32[]{:S(2)}) collective-permute-start(bf16[208,256]{1,0:T(8,128)(2,1)} %prepare.1), channel_id=1, source_target_pairs={{0,4},{4,0},{8,12},{12,8},{16,20},{20,16},{24,28},{28,24},{1,5},{5... | collective-permute-start | bytes 319496 | tf_op jit(solution)/shard_map/ppermute | solution.py:606
  6.8 5.7 %collective-permute-start.1 = (bf16[208,256]{1,0:T(8,128)(2,1)}, bf16[208,256]{1,0:T(8,128)(2,1)S(1)}, u32[]{:S(2)}, u32[]{:S(2)}) collective-permute-start(bf16[208,256]{1,0:T(8,128)(2,1)} %prepare.1), channel_id=1, source_target_pairs={{0,8},{4,12},{8,0},{12,4},{16,24},{20,28},{24,16},{28,20},{1,9},{5... | collective-permute-start | bytes 319496 | tf_op jit(solution)/shard_map/ppermute | solution.py:606
  6.9 5.6 %copy-start.7 = (bf16[208,256]{1,0:T(8,128)(2,1)S(1)}, bf16[208,256]{1,0:T(8,128)(2,1)}, u32[]{:S(2)}) copy-start(bf16[208,256]{1,0:T(8,128)(2,1)} %prepare.1) | copy-start | bytes 319492
  10.5 2.0 %copy-start.2 = (bf16[4,256,2048]{2,1,0:T(8,128)(2,1)}, bf16[4,256,2048]{2,1,0:T(8,128)(2,1)S(1)}, u32[]{:S(2)}) copy-start(bf16[4,256,2048]{2,1,0:T(8,128)(2,1)S(1)} %get-tuple-element.44.unit_hbm) | copy-start | bytes 12582916
  12.6 5.4 %collective-permute-start.3 = (bf16[4,32,256]{2,1,0:T(8,128)(2,1)S(1)}, bf16[4,32,256]{2,1,0:T(8,128)(2,1)S(1)}, u32[]{:S(2)}, u32[]{:S(2)}) collective-permute-start(bf16[4,32,256]{2,1,0:T(8,128)(2,1)S(1)} %pad_maximum_fusion.3), channel_id=1, source_target_pairs={{0,16},{4,20},{8,24},{12,28},{16,0},{20,4},{24,8},{28,12},{1,17},{... | collective-permute-start | bytes 196616 | tf_op jit(solution)/shard_map/ppermute | solution.py:606
  18.1 2.2 %copy-start.3 = (bf16[4,256,2048]{2,1,0:T(8,128)(2,1)S(1)}, bf16[4,256,2048]{2,1,0:T(8,128)(2,1)}, u32[]{:S(2)}) copy-start(bf16[4,256,2048]{2,1,0:T(8,128)(2,1)} %copy-done.2) | copy-start | bytes 12582916
  23.9 16.7 %copy-start = (bf16[4,256,2048]{2,1,0:T(8,128)(2,1)}, bf16[4,256,2048]{2,1,0:T(8,128)(2,1)S(1)}, u32[]{:S(2)}) copy-start(bf16[4,256,2048]{2,1,0:T(8,128)(2,1)S(1)} %get-tuple-element.49.energy_hbm) | copy-start | bytes 12582916
  23.9 4.9 %collective-permute-start.4 = (f32[1,256]{1,0:T(1,128)S(1)}, f32[1,256]{1,0:T(1,128)S(1)}, u32[]{:S(2)}, u32[]{:S(2)}) collective-permute-start(f32[1,256]{1,0:T(1,128)S(1)} %get-tuple-element.45), channel_id=1, source_target_pairs={{0,1},{1,0},{2,3},{3,2},{4,5},{5,4},{6,7},{7,6},{8,9},{9,8},{10,11... | collective-permute-start | bytes 3080 | tf_op jit(solution)/shard_map/ppermute | solution.py:609
  23.9 4.9 %collective-permute-start.5 = (f32[1,256]{1,0:T(1,128)S(1)}, f32[1,256]{1,0:T(1,128)S(1)}, u32[]{:S(2)}, u32[]{:S(2)}) collective-permute-start(f32[1,256]{1,0:T(1,128)S(1)} %get-tuple-element.45), channel_id=1, source_target_pairs={{0,2},{1,3},{2,0},{3,1},{4,6},{5,7},{6,4},{7,5},{8,10},{9,11},{10,... | collective-permute-start | bytes 3080 | tf_op jit(solution)/shard_map/ppermute | solution.py:609
  25.8 3.0 %collective-permute-start.6 = (f32[1,256]{1,0:T(1,128)S(1)}, f32[1,256]{1,0:T(1,128)S(1)}, u32[]{:S(2)}, u32[]{:S(2)}) collective-permute-start(f32[1,256]{1,0:T(1,128)S(1)} %get-tuple-element.45), channel_id=1, source_target_pairs={{0,3},{1,2},{2,1},{3,0},{4,7},{5,6},{6,5},{7,4},{8,11},{9,10},{10,... | collective-permute-start | bytes 3080 | tf_op jit(solution)/shard_map/ppermute | solution.py:609
  25.9 19.6 %collective-permute-start.10 = (bf16[4,176,256]{2,1,0:T(8,128)(2,1)S(1)}, bf16[4,176,256]{2,1,0:T(8,128)(2,1)S(1)}, u32[]{:S(2)}, u32[]{:S(2)}) collective-permute-start(bf16[4,176,256]{2,1,0:T(8,128)(2,1)S(1)} %slice.49.rest_ref), channel_id=1, source_target_pairs={{0,16},{4,20},{8,24},{12,28},{16,0},{20,4},{24,8},{28,12},{1,17},{... | collective-permute-start | bytes 1081352 | tf_op jit(solution)/shard_map/ppermute | solution.py:606
  28.8 11.6 %collective-permute-start.7 = (f32[1,256]{1,0:T(1,128)S(1)}, f32[1,256]{1,0:T(1,128)S(1)}, u32[]{:S(2)}, u32[]{:S(2)}) collective-permute-start(f32[1,256]{1,0:T(1,128)S(1)} %add_add_fusion.5), channel_id=1, source_target_pairs={{0,4},{4,0},{8,12},{12,8},{16,20},{20,16},{24,28},{28,24},{1,5},{5... | collective-permute-start | bytes 3080 | tf_op jit(solution)/shard_map/ppermute | solution.py:606
  30.4 10.1 %collective-permute-start.8 = (f32[1,256]{1,0:T(1,128)S(1)}, f32[1,256]{1,0:T(1,128)S(1)}, u32[]{:S(2)}, u32[]{:S(2)}) collective-permute-start(f32[1,256]{1,0:T(1,128)S(1)} %add_add_fusion.5), channel_id=1, source_target_pairs={{0,8},{4,12},{8,0},{12,4},{16,24},{20,28},{24,16},{28,20},{1,9},{5... | collective-permute-start | bytes 3080 | tf_op jit(solution)/shard_map/ppermute | solution.py:606
  32.5 8.0 %collective-permute-start.9 = (f32[1,256]{1,0:T(1,128)S(1)}, f32[1,256]{1,0:T(1,128)S(1)}, u32[]{:S(2)}, u32[]{:S(2)}) collective-permute-start(f32[1,256]{1,0:T(1,128)S(1)} %add_add_fusion.5), channel_id=1, source_target_pairs={{0,12},{4,8},{8,4},{12,0},{16,28},{20,24},{24,20},{28,16},{1,13},{... | collective-permute-start | bytes 3080 | tf_op jit(solution)/shard_map/ppermute | solution.py:606
  45.5 2.0 %collective-permute-start.11 = (f32[1,256]{1,0:T(1,128)S(1)}, f32[1,256]{1,0:T(1,128)S(1)}, u32[]{:S(2)}, u32[]{:S(2)}) collective-permute-start(f32[1,256]{1,0:T(1,128)S(1)} %iterate.1), channel_id=1, source_target_pairs={{0,1},{1,0},{2,3},{3,2},{4,5},{5,4},{6,7},{7,6},{8,9},{9,8},{10,11... | collective-permute-start | bytes 3080 | tf_op jit(solution)/shard_map/ppermute | solution.py:609
  45.5 3.6 %collective-permute-start.12 = (f32[1,256]{1,0:T(1,128)S(1)}, f32[1,256]{1,0:T(1,128)S(1)}, u32[]{:S(2)}, u32[]{:S(2)}) collective-permute-start(f32[1,256]{1,0:T(1,128)S(1)} %iterate.1), channel_id=1, source_target_pairs={{0,2},{1,3},{2,0},{3,1},{4,6},{5,7},{6,4},{7,5},{8,10},{9,11},{10,... | collective-permute-start | bytes 3080 | tf_op jit(solution)/shard_map/ppermute | solution.py:609
  47.0 3.0 %collective-permute-start.13 = (f32[1,256]{1,0:T(1,128)S(1)}, f32[1,256]{1,0:T(1,128)S(1)}, u32[]{:S(2)}, u32[]{:S(2)}) collective-permute-start(f32[1,256]{1,0:T(1,128)S(1)} %iterate.1), channel_id=1, source_target_pairs={{0,3},{1,2},{2,1},{3,0},{4,7},{5,6},{6,5},{7,4},{8,11},{9,10},{10,... | collective-permute-start | bytes 3080 | tf_op jit(solution)/shard_map/ppermute | solution.py:609
  50.0 11.4 %copy-start.1 = (bf16[4,256,2048]{2,1,0:T(8,128)(2,1)S(1)}, bf16[4,256,2048]{2,1,0:T(8,128)(2,1)}, u32[]{:S(2)}) copy-start(bf16[4,256,2048]{2,1,0:T(8,128)(2,1)} %copy-done) | copy-start | bytes 12582916
  50.0 11.4 %collective-permute-start.14 = (f32[1,256]{1,0:T(1,128)S(1)}, f32[1,256]{1,0:T(1,128)S(1)}, u32[]{:S(2)}, u32[]{:S(2)}) collective-permute-start(f32[1,256]{1,0:T(1,128)S(1)} %add_add_fusion.3), channel_id=1, source_target_pairs={{0,4},{4,0},{8,12},{12,8},{16,20},{20,16},{24,28},{28,24},{1,5},{5... | collective-permute-start | bytes 3080 | tf_op jit(solution)/shard_map/ppermute | solution.py:606
  51.5 9.9 %collective-permute-start.15 = (f32[1,256]{1,0:T(1,128)S(1)}, f32[1,256]{1,0:T(1,128)S(1)}, u32[]{:S(2)}, u32[]{:S(2)}) collective-permute-start(f32[1,256]{1,0:T(1,128)S(1)} %add_add_fusion.3), channel_id=1, source_target_pairs={{0,8},{4,12},{8,0},{12,4},{16,24},{20,28},{24,16},{28,20},{1,9},{5... | collective-permute-start | bytes 3080 | tf_op jit(solution)/shard_map/ppermute | solution.py:606
  52.2 9.1 %collective-permute-start.16 = (f32[1,256]{1,0:T(1,128)S(1)}, f32[1,256]{1,0:T(1,128)S(1)}, u32[]{:S(2)}, u32[]{:S(2)}) collective-permute-start(f32[1,256]{1,0:T(1,128)S(1)} %add_add_fusion.3), channel_id=1, source_target_pairs={{0,12},{4,8},{8,4},{12,0},{16,28},{20,24},{24,20},{28,16},{1,13},{... | collective-permute-start | bytes 3080 | tf_op jit(solution)/shard_map/ppermute | solution.py:606
  53.5 2.2 %copy-start.4 = (bf16[4,256,2048]{2,1,0:T(8,128)(2,1)S(1)}, bf16[4,256,2048]{2,1,0:T(8,128)(2,1)}, u32[]{:S(2)}) copy-start(bf16[4,256,2048]{2,1,0:T(8,128)(2,1)} %copy-done.2) | copy-start | bytes 12582916
  65.4 2.0 %collective-permute-start.17 = (f32[1,1536]{1,0:T(1,128)S(1)}, f32[1,1536]{1,0:T(1,128)S(1)}, u32[]{:S(2)}, u32[]{:S(2)}) collective-permute-start(f32[1,1536]{1,0:T(1,128)S(1)} %get-tuple-element.53), channel_id=1, source_target_pairs={{0,1},{1,0},{2,3},{3,2},{4,5},{5,4},{6,7},{7,6},{8,9},{9,8},{10,11... | collective-permute-start | bytes 18440 | tf_op jit(solution)/shard_map/ppermute | solution.py:609
  65.4 3.7 %collective-permute-start.18 = (f32[1,1536]{1,0:T(1,128)S(1)}, f32[1,1536]{1,0:T(1,128)S(1)}, u32[]{:S(2)}, u32[]{:S(2)}) collective-permute-start(f32[1,1536]{1,0:T(1,128)S(1)} %get-tuple-element.53), channel_id=1, source_target_pairs={{0,2},{1,3},{2,0},{3,1},{4,6},{5,7},{6,4},{7,5},{8,10},{9,11},{10,... | collective-permute-start | bytes 18440 | tf_op jit(solution)/shard_map/ppermute | solution.py:609
  66.2 3.1 %collective-permute-start.19 = (f32[1,1536]{1,0:T(1,128)S(1)}, f32[1,1536]{1,0:T(1,128)S(1)}, u32[]{:S(2)}, u32[]{:S(2)}) collective-permute-start(f32[1,1536]{1,0:T(1,128)S(1)} %get-tuple-element.53), channel_id=1, source_target_pairs={{0,3},{1,2},{2,1},{3,0},{4,7},{5,6},{6,5},{7,4},{8,11},{9,10},{10,... | collective-permute-start | bytes 18440 | tf_op jit(solution)/shard_map/ppermute | solution.py:609
  69.2 6.9 %collective-permute-start.20 = (f32[1,1536]{1,0:T(1,128)S(1)}, f32[1,1536]{1,0:T(1,128)S(1)}, u32[]{:S(2)}, u32[]{:S(2)}) collective-permute-start(f32[1,1536]{1,0:T(1,128)S(1)} %add_add_fusion.1), channel_id=1, source_target_pairs={{0,4},{4,0},{8,12},{12,8},{16,20},{20,16},{24,28},{28,24},{1,5},{5... | collective-permute-start | bytes 18440 | tf_op jit(solution)/shard_map/ppermute | solution.py:606
  70.8 5.4 %collective-permute-start.21 = (f32[1,1536]{1,0:T(1,128)S(1)}, f32[1,1536]{1,0:T(1,128)S(1)}, u32[]{:S(2)}, u32[]{:S(2)}) collective-permute-start(f32[1,1536]{1,0:T(1,128)S(1)} %add_add_fusion.1), channel_id=1, source_target_pairs={{0,8},{4,12},{8,0},{12,4},{16,24},{20,28},{24,16},{28,20},{1,9},{5... | collective-permute-start | bytes 18440 | tf_op jit(solution)/shard_map/ppermute | solution.py:606
  71.6 4.6 %collective-permute-start.22 = (f32[1,1536]{1,0:T(1,128)S(1)}, f32[1,1536]{1,0:T(1,128)S(1)}, u32[]{:S(2)}, u32[]{:S(2)}) collective-permute-start(f32[1,1536]{1,0:T(1,128)S(1)} %add_add_fusion.1), channel_id=1, source_target_pairs={{0,12},{4,8},{8,4},{12,0},{16,28},{20,24},{24,20},{28,16},{1,13},{... | collective-permute-start | bytes 18440 | tf_op jit(solution)/shard_map/ppermute | solution.py:606
  85.6 14.4 %collective-permute-start.25 = (bf16[32,5120]{1,0:T(8,128)(2,1)S(1)}, bf16[32,5120]{1,0:T(8,128)(2,1)S(1)}, u32[]{:S(2)}, u32[]{:S(2)}) collective-permute-start(bf16[32,5120]{1,0:T(8,128)(2,1)S(1)} %get-tuple-element.67), channel_id=1, source_target_pairs={{0,4},{4,0},{8,12},{12,8},{16,20},{20,16},{24,28},{28,24},{1,5},{5... | collective-permute-start | bytes 983048 | tf_op jit(solution)/shard_map/ppermute | solution.py:606
  87.2 13.6 %collective-permute-start.26 = (bf16[32,5120]{1,0:T(8,128)(2,1)S(1)}, bf16[32,5120]{1,0:T(8,128)(2,1)S(1)}, u32[]{:S(2)}, u32[]{:S(2)}) collective-permute-start(bf16[32,5120]{1,0:T(8,128)(2,1)S(1)} %get-tuple-element.68), channel_id=1, source_target_pairs={{0,8},{4,12},{8,0},{12,4},{16,24},{20,28},{24,16},{28,20},{1,9},{5... | collective-permute-start | bytes 983048 | tf_op jit(solution)/shard_map/ppermute | solution.py:606
  87.9 15.0 %collective-permute-start.27 = (bf16[32,5120]{1,0:T(8,128)(2,1)S(1)}, bf16[32,5120]{1,0:T(8,128)(2,1)S(1)}, u32[]{:S(2)}, u32[]{:S(2)}) collective-permute-start(bf16[32,5120]{1,0:T(8,128)(2,1)S(1)} %get-tuple-element.69), channel_id=1, source_target_pairs={{0,12},{4,8},{8,4},{12,0},{16,28},{20,24},{24,20},{28,16},{1,13},{... | collective-permute-start | bytes 983048 | tf_op jit(solution)/shard_map/ppermute | solution.py:606
  89.2 8.5 %collective-permute-start.29 = (f32[136,640]{1,0:T(8,128)S(1)}, f32[136,640]{1,0:T(8,128)S(1)}, u32[]{:S(2)}, u32[]{:S(2)}) collective-permute-start(f32[136,640]{1,0:T(8,128)S(1)} %get-tuple-element.73), channel_id=1, source_target_pairs={{0,2},{1,3},{2,0},{3,1},{4,6},{5,7},{6,4},{7,5},{8,10},{9,11},{10,... | collective-permute-start | bytes 1044488 | tf_op jit(solution)/shard_map/ppermute | solution.py:609
  98.5 8.4 %collective-permute-start.30 = (f32[72,640]{1,0:T(8,128)}, f32[72,640]{1,0:T(8,128)S(1)}, u32[]{:S(2)}, u32[]{:S(2)}) collective-permute-start(f32[72,640]{1,0:T(8,128)} %pad_maximum_fusion.1), channel_id=1, source_target_pairs={{0,1},{1,0},{2,3},{3,2},{4,5},{5,4},{6,7},{7,6},{8,9},{9,8},{10,11... | collective-permute-start | bytes 552968 | tf_op jit(solution)/shard_map/ppermute | solution.py:609
  98.5 10.5 %collective-permute-start.23 = (bf16[32,3072]{1,0:T(8,128)(2,1)S(1)}, bf16[32,3072]{1,0:T(8,128)(2,1)S(1)}, u32[]{:S(2)}, u32[]{:S(2)}) collective-permute-start(bf16[32,3072]{1,0:T(8,128)(2,1)S(1)} %get-tuple-element.64), channel_id=1, source_target_pairs={{0,4},{4,0},{8,12},{12,8},{16,20},{20,16},{24,28},{28,24},{1,5},{5... | collective-permute-start | bytes 589832 | tf_op jit(solution)/shard_map/ppermute | solution.py:606
  100.0 10.8 %collective-permute-start.24 = (bf16[32,3072]{1,0:T(8,128)(2,1)S(1)}, bf16[32,3072]{1,0:T(8,128)(2,1)S(1)}, u32[]{:S(2)}, u32[]{:S(2)}) collective-permute-start(bf16[32,3072]{1,0:T(8,128)(2,1)S(1)} %get-tuple-element.65), channel_id=1, source_target_pairs={{0,8},{4,12},{8,0},{12,4},{16,24},{20,28},{24,16},{28,20},{1,9},{5... | collective-permute-start | bytes 589832 | tf_op jit(solution)/shard_map/ppermute | solution.py:606
  102.9 9.0 %collective-permute-start.28 = (bf16[32,3072]{1,0:T(8,128)(2,1)S(1)}, bf16[32,3072]{1,0:T(8,128)(2,1)S(1)}, u32[]{:S(2)}, u32[]{:S(2)}) collective-permute-start(bf16[32,3072]{1,0:T(8,128)(2,1)S(1)} %get-tuple-element.70), channel_id=1, source_target_pairs={{0,12},{4,8},{8,4},{12,0},{16,28},{20,24},{24,20},{28,16},{1,13},{... | collective-permute-start | bytes 589832 | tf_op jit(solution)/shard_map/ppermute | solution.py:606
  107.1 7.2 %collective-permute-start.31 = (f32[72,160]{1,0:T(8,128)S(1)}, f32[72,160]{1,0:T(8,128)S(1)}, u32[]{:S(2)}, u32[]{:S(2)}) collective-permute-start(f32[72,160]{1,0:T(8,128)S(1)} %get-tuple-element.85), channel_id=1, source_target_pairs={{0,4},{4,0},{8,12},{12,8},{16,20},{20,16},{24,28},{28,24},{1,5},{5... | collective-permute-start | bytes 138248 | tf_op jit(solution)/shard_map/ppermute | solution.py:606
  107.7 6.6 %collective-permute-start.32 = (f32[72,160]{1,0:T(8,128)S(1)}, f32[72,160]{1,0:T(8,128)S(1)}, u32[]{:S(2)}, u32[]{:S(2)}) collective-permute-start(f32[72,160]{1,0:T(8,128)S(1)} %get-tuple-element.86), channel_id=1, source_target_pairs={{0,8},{4,12},{8,0},{12,4},{16,24},{20,28},{24,16},{28,20},{1,9},{5... | collective-permute-start | bytes 138248 | tf_op jit(solution)/shard_map/ppermute | solution.py:606
  109.0 5.5 %collective-permute-start.33 = (f32[72,160]{1,0:T(8,128)S(1)}, f32[72,160]{1,0:T(8,128)S(1)}, u32[]{:S(2)}, u32[]{:S(2)}) collective-permute-start(f32[72,160]{1,0:T(8,128)S(1)} %get-tuple-element.83), channel_id=1, source_target_pairs={{0,12},{4,8},{8,4},{12,0},{16,28},{20,24},{24,20},{28,16},{1,13},{... | collective-permute-start | bytes 138248 | tf_op jit(solution)/shard_map/ppermute | solution.py:606
  110.7 3.7 %copy-start.5 = (bf16[160,256]{1,0:T(8,128)(2,1)S(1)}, bf16[160,256]{1,0:T(8,128)(2,1)}, u32[]{:S(2)}) copy-start(bf16[160,256]{1,0:T(8,128)(2,1)} %stud_ref.3) | copy-start | bytes 245764
  110.7 3.7 %copy-start.6 = (s32[160]{0:T(256)S(1)}, s32[160]{0:T(256)}, u32[]{:S(2)}) copy-start(s32[160]{0:T(256)} %param.7) | copy-start | bytes 1924

commit v6 on v5

--- a/solution.py
+++ b/solution.py
@@ -199,7 +199,7 @@
         cost_estimate=pl.CostEstimate(
             flops=2 * t * d * chunks * width, bytes_accessed=4 * t * chunks * width, transcendentals=0
         ),
-        compiler_params=params(LIMIT),
+        compiler_params=params(52),
         name="energy",
     )(teach, unit)
 
@@ -347,7 +347,7 @@
         cost_estimate=pl.CostEstimate(
             flops=4 * s * d * chunks * width, bytes_accessed=2 * s * chunks * width, transcendentals=0
         ),
-        compiler_params=params(LIMIT),
+        compiler_params=params(52),
         name="student_near" if near else "student_far",
     )(rest, pairs, unit)
 

time: 116 us -> 114 us (0.983)
  local copies, waits for them, and re-layouts: 6.71 us -> 2.68 us
  Pallas kernels: 54.6 us -> 57.5 us
    unnamed x17 -> x19, local copies, waits for them, and re-layouts: 6.4 us -> 2.39 us
    pallas_call x2, Pallas kernels: 13.6 us -> 15.2 us  [student_call(): pl.pallas_call(functools.partial(student_kernel, 2 * (rest.shape[1] - 16)...]
    pallas_call x1, Pallas kernels: 3.59 us -> 4.97 us  [energy_call(): pl.pallas_call(functools.partial(energy_kernel, float(total_k)), out_shap...]
  transfers between devices with their start and end apart: 34 -> 34, of which waited for: 10 -> 9; matrix products, arithmetic and copies ran while one was open for 1% -> 1% of each run, Pallas kernels for 30% -> 32%
where the time goes in v6:
time: 114 us
  Pallas kernels  57.5 us (50%)
  starting transfers between devices  39.6 us (35%)
  waiting for transfers between devices  12.1 us (11%)
  local copies, waits for them, and re-layouts  2.68 us (2%)
    ppermute x23, starting transfers between devices, swap_rows(): return lax.ppermute(x, 'rows', [(j, j ^ n) for j in range(n_rows)])  32.4 us
    pallas_call x2, Pallas kernels, head_call(): pl.pallas_call(functools.partial(head_kernel, factor, first), out_shape=o...  16.2 us
    pallas_call x2, Pallas kernels, student_call(): pl.pallas_call(functools.partial(student_kernel, 2 * (rest.shape[1] - 16)...  15.2 us
    ppermute x23, waiting for transfers between devices, swap_rows(): return lax.ppermute(x, 'rows', [(j, j ^ n) for j in range(n_rows)])  7.35 us
    ppermute x11, starting transfers between devices, swap_proto(): return lax.ppermute(x, 'proto', [(j, j ^ n) for j in range(n_proto)])  7.22 us
    pallas_call x2, Pallas kernels, iterate_call(): pl.pallas_call(functools.partial(iterate_kernel, float(total_k), last), o...  6.54 us
    pallas_call x1, Pallas kernels, energy_call(): pl.pallas_call(functools.partial(energy_kernel, float(total_k)), out_shap...  4.97 us
    ppermute x11, waiting for transfers between devices, swap_proto(): return lax.ppermute(x, 'proto', [(j, j ^ n) for j in range(n_proto)])  4.75 us
  transfers between devices with their start and end apart: 34, of which 9 were waited for; matrix products, arithmetic and copies ran while one was open for 1% of the time, Pallas kernels for 32%

profile of v6, /device:TPU:0, one launch (start us, length us, event | category | flops | bytes accessed | tf_op | source)
XLA Modules:
  0.0 113.7 jit_solution(4246632381344500637)
XLA Ops:
  0.6 1.7 %prepare.1 = bf16[208,256]{1,0:T(8,128)(2,1)} custom-call(bf16[32,256]{1,0:T(8,128)(2,1)} %teach_ref.1, bf16[160,256]{1,0:T(8,128)(2,1)} %stud_ref.3, s32[1,160]{1,0:T(1,128)} %bitcast.17), custom_call_target="tpu_custom_call" | custom-call | tf_op jit(solution)/shard_map/prepare/pallas_call | solution.py:106
  2.3 4.0 %collective-permute-start.2 = (bf16[208,256]{1,0:T(8,128)(2,1)}, bf16[208,256]{1,0:T(8,128)(2,1)S(1)}, u32[]{:S(2)}, u32[]{:S(2)}) collective-permute-start(bf16[208,256]{1,0:T(8,128)(2,1)} %prepare.1), channel_id=1, source_target_pairs={{0,12},{4,8},{8,4},{12,0},{16,28},{20,24},{24,20},{28,16},{1,13},{... | collective-permute-start | bytes 319496 | tf_op jit(solution)/shard_map/ppermute | solution.py:606
  6.2 0.5 collective-permute-start
  6.8 0.0 collective-permute-start.1
  6.8 0.1 pad_add_fusion.place
  6.9 3.6 %unit.1 = (bf16[4,256,2048]{2,1,0:T(8,128)(2,1)S(1)}, f32[4,1,2048]{2,1,0:T(1,128)S(1)}) custom-call(s32[4]{0:T(128)S(1)} %pad_add_fusion.place, bf16[256,32768]{1,0:T(8,128)(2,1)} %v_hbm.5), custom_call_target="tpu_custom_call" | custom-call | flops 8388608 | bytes 8388608 | tf_op jit(solution)/shard_map/unit/pallas_call | solution.py:145
  10.5 0.0 copy-start.2
  10.5 2.0 %copy-done.2 = bf16[4,256,2048]{2,1,0:T(8,128)(2,1)} copy-done((bf16[4,256,2048]{2,1,0:T(8,128)(2,1)}, bf16[4,256,2048]{2,1,0:T(8,128)(2,1)S(1)}, u32[]{:S(2)}) %copy-start.2) | copy-done | bytes 4194328
  12.6 3.1 %collective-permute-start.3 = (bf16[4,32,256]{2,1,0:T(8,128)(2,1)S(1)}, bf16[4,32,256]{2,1,0:T(8,128)(2,1)S(1)}, u32[]{:S(2)}, u32[]{:S(2)}) collective-permute-start(bf16[4,32,256]{2,1,0:T(8,128)(2,1)S(1)} %pad_maximum_fusion.3), channel_id=1, source_target_pairs={{0,16},{4,20},{8,24},{12,28},{16,0},{20,4},{24,8},{28,12},{1,17},{... | collective-permute-start | bytes 196616 | tf_op jit(solution)/shard_map/ppermute | solution.py:606
  15.7 0.1 convert_element_type.34.pairs_ref
  15.8 0.1 pad_maximum_fusion
  15.9 2.1 %collective-permute-done.3 = bf16[4,32,256]{2,1,0:T(8,128)(2,1)S(1)} collective-permute-done((bf16[4,32,256]{2,1,0:T(8,128)(2,1)S(1)}, bf16[4,32,256]{2,1,0:T(8,128)(2,1)S(1)}, u32[]{:S(2)}, u32[]{:S(2)}) %collective-permute-start.3) | collective-permute-done | bytes 65568 | tf_op jit(solution)/shard_map/ppermute | solution.py:606
  18.1 5.0 %energy.1 = (bf16[4,256,2048]{2,1,0:T(8,128)(2,1)}, f32[1,256]{1,0:T(1,128)S(1)}) custom-call(bf16[256,256]{1,0:T(8,128)(2,1)S(1)} %bitcast.16, bf16[4,256,2048]{2,1,0:T(8,128)(2,1)} %copy-done.2), custom_call_target="tpu_custom_call" | custom-call | flops 1073741824 | bytes 8388608 | tf_op jit(solution)/shard_map/energy/pallas_call | solution.py:190
  23.0 0.1 collective-permute-start.4
  23.1 1.8 %collective-permute-start.5 = (f32[1,256]{1,0:T(1,128)S(1)}, f32[1,256]{1,0:T(1,128)S(1)}, u32[]{:S(2)}, u32[]{:S(2)}) collective-permute-start(f32[1,256]{1,0:T(1,128)S(1)} %get-tuple-element.45), channel_id=1, source_target_pairs={{0,2},{1,3},{2,0},{3,1},{4,6},{5,7},{6,4},{7,5},{8,10},{9,11},{10,... | collective-permute-start | bytes 3080 | tf_op jit(solution)/shard_map/ppermute | solution.py:609
  25.0 0.1 collective-permute-start.6
  25.1 2.9 %collective-permute-start.10 = (bf16[4,176,256]{2,1,0:T(8,128)(2,1)S(1)}, bf16[4,176,256]{2,1,0:T(8,128)(2,1)S(1)}, u32[]{:S(2)}, u32[]{:S(2)}) collective-permute-start(bf16[4,176,256]{2,1,0:T(8,128)(2,1)S(1)} %slice.49.rest_ref), channel_id=1, source_target_pairs={{0,16},{4,20},{8,24},{12,28},{16,0},{20,4},{24,8},{28,12},{1,17},{... | collective-permute-start | bytes 1081352 | tf_op jit(solution)/shard_map/ppermute | solution.py:606
  28.0 1.6 %collective-permute-start.7 = (f32[1,256]{1,0:T(1,128)S(1)}, f32[1,256]{1,0:T(1,128)S(1)}, u32[]{:S(2)}, u32[]{:S(2)}) collective-permute-start(f32[1,256]{1,0:T(1,128)S(1)} %add_add_fusion.5), channel_id=1, source_target_pairs={{0,4},{4,0},{8,12},{12,8},{16,20},{20,16},{24,28},{28,24},{1,5},{5... | collective-permute-start | bytes 3080 | tf_op jit(solution)/shard_map/ppermute | solution.py:606
  29.6 2.1 %collective-permute-start.8 = (f32[1,256]{1,0:T(1,128)S(1)}, f32[1,256]{1,0:T(1,128)S(1)}, u32[]{:S(2)}, u32[]{:S(2)}) collective-permute-start(f32[1,256]{1,0:T(1,128)S(1)} %add_add_fusion.5), channel_id=1, source_target_pairs={{0,8},{4,12},{8,0},{12,4},{16,24},{20,28},{24,16},{28,20},{1,9},{5... | collective-permute-start | bytes 3080 | tf_op jit(solution)/shard_map/ppermute | solution.py:606
  31.7 8.7 %student_near.1 = (bf16[4,640,2048]{2,1,0:T(8,128)(2,1)}, f32[1,640]{1,0:T(1,128)S(1)}, bf16[256,640]{1,0:T(8,128)(2,1)S(1)}, f32[256,256]{1,0:T(8,128)S(1)}, f32[256,640]{1,0:T(8,128)S(1)}) custom-call(bf16[4,176,256]{2,1,0:T(8,128)(2,1)S(1)} %slice.49.rest_ref, s32[1,640]{1,0:T(1,128)S(1)} %convert_element_type.34.pairs_ref, bf16[4,256,2048]{2,1,0:T(8,128)(2,1)} %copy-done.2), custom_call_target="tpu_custom_call" | custom-call | flops 5368709120 | bytes 10485760 | tf_op jit(solution)/shard_map/student_near/pallas_call | solution.py:341
  40.5 2.6 %iterate.1 = f32[1,256]{1,0:T(1,128)S(1)} custom-call(f32[1,256]{1,0:T(1,128)S(1)} %add_add_fusion.4.sum_in, bf16[4,256,2048]{2,1,0:T(8,128)(2,1)S(1)} %copy-done), custom_call_target="tpu_custom_call" | custom-call | flops 8388608 | bytes 8388608 | tf_op jit(solution)/shard_map/iterate/pallas_call | solution.py:267
  43.1 1.6 %collective-permute-done.10.rest_ref = bf16[4,176,256]{2,1,0:T(8,128)(2,1)S(1)} collective-permute-done((bf16[4,176,256]{2,1,0:T(8,128)(2,1)S(1)}, bf16[4,176,256]{2,1,0:T(8,128)(2,1)S(1)}, u32[]{:S(2)}, u32[]{:S(2)}) %collective-permute-start.10) | collective-permute-done | bytes 360480 | tf_op jit(solution)/shard_map/ppermute | solution.py:606
  44.6 1.5 %collective-permute-start.12 = (f32[1,256]{1,0:T(1,128)S(1)}, f32[1,256]{1,0:T(1,128)S(1)}, u32[]{:S(2)}, u32[]{:S(2)}) collective-permute-start(f32[1,256]{1,0:T(1,128)S(1)} %iterate.1), channel_id=1, source_target_pairs={{0,2},{1,3},{2,0},{3,1},{4,6},{5,7},{6,4},{7,5},{8,10},{9,11},{10,... | collective-permute-start | bytes 3080 | tf_op jit(solution)/shard_map/ppermute | solution.py:609
  46.2 0.3 collective-permute-start.13
  46.5 0.1 convert_element_type.37.pairs_ref
  46.6 1.6 %collective-permute-done.12 = f32[1,256]{1,0:T(1,128)S(1)} collective-permute-done((f32[1,256]{1,0:T(1,128)S(1)}, f32[1,256]{1,0:T(1,128)S(1)}, u32[]{:S(2)}, u32[]{:S(2)}) %collective-permute-start.12) | collective-permute-done | bytes 1056 | tf_op jit(solution)/shard_map/ppermute | solution.py:609
  48.2 0.9 collective-permute-done.13
  49.2 1.5 %collective-permute-start.14 = (f32[1,256]{1,0:T(1,128)S(1)}, f32[1,256]{1,0:T(1,128)S(1)}, u32[]{:S(2)}, u32[]{:S(2)}) collective-permute-start(f32[1,256]{1,0:T(1,128)S(1)} %add_add_fusion.3), channel_id=1, source_target_pairs={{0,4},{4,0},{8,12},{12,8},{16,20},{20,16},{24,28},{28,24},{1,5},{5... | collective-permute-start | bytes 3080 | tf_op jit(solution)/shard_map/ppermute | solution.py:606
  50.7 0.8 collective-permute-start.15
  51.4 1.2 %collective-permute-start.16 = (f32[1,256]{1,0:T(1,128)S(1)}, f32[1,256]{1,0:T(1,128)S(1)}, u32[]{:S(2)}, u32[]{:S(2)}) collective-permute-start(f32[1,256]{1,0:T(1,128)S(1)} %add_add_fusion.3), channel_id=1, source_target_pairs={{0,12},{4,8},{8,4},{12,0},{16,28},{20,24},{24,20},{28,16},{1,13},{... | collective-permute-start | bytes 3080 | tf_op jit(solution)/shard_map/ppermute | solution.py:606
  52.7 6.5 %student_far.1 = (bf16[4,640,2048]{2,1,0:T(8,128)(2,1)}, f32[1,640]{1,0:T(1,128)S(1)}, bf16[256,640]{1,0:T(8,128)(2,1)S(1)}, f32[256,256]{1,0:T(8,128)S(1)}) custom-call(bf16[4,176,256]{2,1,0:T(8,128)(2,1)S(1)} %collective-permute-done.10.rest_ref, s32[1,640]{1,0:T(1,128)S(1)} %convert_element_type.37.pairs_ref, bf16[4,256,2048]{2,1,0:T(8,128)(2,1)} %copy-done.2), custom_call_target="tpu_custom_call" | custom-call | flops 5368709120 | bytes 10485760 | tf_op jit(solution)/shard_map/student_far/pallas_call | solution.py:341
  59.2 4.0 %iterate_last.1 = (f32[1,1536]{1,0:T(1,128)S(1)}, bf16[4,256,2048]{2,1,0:T(8,128)(2,1)S(1)}) custom-call(f32[1,256]{1,0:T(1,128)S(1)} %add_add_fusion.2.sum_in, bf16[4,256,2048]{2,1,0:T(8,128)(2,1)S(1)} %copy-done.1, f32[1,640]{1,0:T(1,128)S(1)} %get-tuple-element.47.refs_0_, f32[1,640]{1,0:T(1,128)S(1)} %get-tuple-element.52.refs_1_), custom_call_target="tpu_custom_call" | custom-call | flops 8388608 | bytes 8388608 | tf_op jit(solution)/shard_map/iterate_last/pallas_call | solution.py:267
  63.2 0.1 collective-permute-start.17
  63.3 0.7 collective-permute-start.18
  64.0 1.1 %collective-permute-start.19 = (f32[1,1536]{1,0:T(1,128)S(1)}, f32[1,1536]{1,0:T(1,128)S(1)}, u32[]{:S(2)}, u32[]{:S(2)}) collective-permute-start(f32[1,1536]{1,0:T(1,128)S(1)} %get-tuple-element.53), channel_id=1, source_target_pairs={{0,3},{1,2},{2,1},{3,0},{4,7},{5,6},{6,5},{7,4},{8,11},{9,10},{10,... | collective-permute-start | bytes 18440 | tf_op jit(solution)/shard_map/ppermute | solution.py:609
  65.1 1.8 %collective-permute-done.18 = f32[1,1536]{1,0:T(1,128)S(1)} collective-permute-done((f32[1,1536]{1,0:T(1,128)S(1)}, f32[1,1536]{1,0:T(1,128)S(1)}, u32[]{:S(2)}, u32[]{:S(2)}) %collective-permute-start.18) | collective-permute-done | bytes 6176 | tf_op jit(solution)/shard_map/ppermute | solution.py:609
  67.0 0.1 collective-permute-done.19
  67.1 1.6 %collective-permute-start.20 = (f32[1,1536]{1,0:T(1,128)S(1)}, f32[1,1536]{1,0:T(1,128)S(1)}, u32[]{:S(2)}, u32[]{:S(2)}) collective-permute-start(f32[1,1536]{1,0:T(1,128)S(1)} %add_add_fusion.1), channel_id=1, source_target_pairs={{0,4},{4,0},{8,12},{12,8},{16,20},{20,16},{24,28},{28,24},{1,5},{5... | collective-permute-start | bytes 18440 | tf_op jit(solution)/shard_map/ppermute | solution.py:606
  68.6 0.8 collective-permute-start.21
  69.4 1.2 %collective-permute-start.22 = (f32[1,1536]{1,0:T(1,128)S(1)}, f32[1,1536]{1,0:T(1,128)S(1)}, u32[]{:S(2)}, u32[]{:S(2)}) collective-permute-start(f32[1,1536]{1,0:T(1,128)S(1)} %add_add_fusion.1), channel_id=1, source_target_pairs={{0,12},{4,8},{8,4},{12,0},{16,28},{20,24},{24,20},{28,16},{1,13},{... | collective-permute-start | bytes 18440 | tf_op jit(solution)/shard_map/ppermute | solution.py:606
  70.6 3.4 %mean.1.refs_1_ = f32[256,640]{1,0:T(8,128)S(1)} custom-call(s32[1,640]{1,0:T(1,128)S(1)} %convert_element_type.34.pairs_ref, bf16[4,256,2048]{2,1,0:T(8,128)(2,1)S(1)} %copy-done.3, bf16[4,256,2048]{2,1,0:T(8,128)(2,1)S(1)} %get-tuple-element.61.scaled_hbm), custom_call_target="tpu_custom_call" | custom-call | flops 3221225472 | bytes 8388608 | tf_op jit(solution)/shard_map/mean/pallas_call | solution.py:381
  74.1 9.4 %head.2 = (f32[32,32768]{1,0:T(8,128)}, bf16[32,5120]{1,0:T(8,128)(2,1)S(1)}, bf16[32,5120]{1,0:T(8,128)(2,1)S(1)}, bf16[32,5120]{1,0:T(8,128)(2,1)S(1)}, f32[12...) custom-call(s32[4]{0:T(128)S(1)} %pad_add_fusion.place, f32[1,1536]{1,0:T(1,128)S(1)} %add_add_fusion.both_ref, ...), custom_call_target="tpu_custom_call" | custom-call | flops 8053063680 | bytes 18350080 | tf_op jit(solution)/shard_map/head/pallas_call | solution.py:508
  83.4 1.6 %collective-permute-start.25 = (bf16[32,5120]{1,0:T(8,128)(2,1)S(1)}, bf16[32,5120]{1,0:T(8,128)(2,1)S(1)}, u32[]{:S(2)}, u32[]{:S(2)}) collective-permute-start(bf16[32,5120]{1,0:T(8,128)(2,1)S(1)} %get-tuple-element.67), channel_id=1, source_target_pairs={{0,4},{4,0},{8,12},{12,8},{16,20},{20,16},{24,28},{28,24},{1,5},{5... | collective-permute-start | bytes 983048 | tf_op jit(solution)/shard_map/ppermute | solution.py:606
  85.0 0.8 collective-permute-start.26
  85.8 1.2 %collective-permute-start.27 = (bf16[32,5120]{1,0:T(8,128)(2,1)S(1)}, bf16[32,5120]{1,0:T(8,128)(2,1)S(1)}, u32[]{:S(2)}, u32[]{:S(2)}) collective-permute-start(bf16[32,5120]{1,0:T(8,128)(2,1)S(1)} %get-tuple-element.69), channel_id=1, source_target_pairs={{0,12},{4,8},{8,4},{12,0},{16,28},{20,24},{24,20},{28,16},{1,13},{... | collective-permute-start | bytes 983048 | tf_op jit(solution)/shard_map/ppermute | solution.py:606
  87.0 1.4 %collective-permute-start.29 = (f32[136,640]{1,0:T(8,128)S(1)}, f32[136,640]{1,0:T(8,128)S(1)}, u32[]{:S(2)}, u32[]{:S(2)}) collective-permute-start(f32[136,640]{1,0:T(8,128)S(1)} %get-tuple-element.73), channel_id=1, source_target_pairs={{0,2},{1,3},{2,0},{3,1},{4,6},{5,7},{6,4},{7,5},{8,10},{9,11},{10,... | collective-permute-start | bytes 1044488 | tf_op jit(solution)/shard_map/ppermute | solution.py:609
  88.4 6.8 %head.3 = (f32[32,32768]{1,0:T(8,128)}, bf16[32,3072]{1,0:T(8,128)(2,1)S(1)}, bf16[32,3072]{1,0:T(8,128)(2,1)S(1)}, bf16[32,3072]{1,0:T(8,128)(2,1)S(1)}) custom-call(s32[4]{0:T(128)S(1)} %pad_add_fusion.place, f32[1,1536]{1,0:T(1,128)S(1)} %add_add_fusion.both_ref, ...), custom_call_target="tpu_custom_call", output_to_operand_aliasing={{0}: (12, {})} | custom-call | flops 4831838208 | bytes 11010048 | tf_op jit(solution)/shard_map/head/pallas_call | solution.py:508
  95.2 0.3 collective-permute-done.29
  95.6 0.3 copy-done.6
  95.9 0.1 copy-done.7
  96.0 0.1 collective-permute-start.30
  96.1 1.6 %collective-permute-start.23 = (bf16[32,3072]{1,0:T(8,128)(2,1)}, bf16[32,3072]{1,0:T(8,128)(2,1)S(1)}, u32[]{:S(2)}, u32[]{:S(2)}) collective-permute-start(bf16[32,3072]{1,0:T(8,128)(2,1)} %copy-done.7), channel_id=1, source_target_pairs={{0,4},{4,0},{8,12},{12,8},{16,20},{20,16},{24,28},{28,24},{1,5},{5... | collective-permute-start | bytes 589832 | tf_op jit(solution)/shard_map/ppermute | solution.py:606
  97.7 0.8 collective-permute-start.24
  98.5 2.3 %collective-permute-done.27.refs_2_ = bf16[32,5120]{1,0:T(8,128)(2,1)S(1)} collective-permute-done((bf16[32,5120]{1,0:T(8,128)(2,1)S(1)}, bf16[32,5120]{1,0:T(8,128)(2,1)S(1)}, u32[]{:S(2)}, u32[]{:S(2)}) %collective-permute-start.27) | collective-permute-done | bytes 327712 | tf_op jit(solution)/shard_map/ppermute | solution.py:606
  100.8 1.7 %collective-permute-start.28 = (bf16[32,3072]{1,0:T(8,128)(2,1)S(1)}, bf16[32,3072]{1,0:T(8,128)(2,1)S(1)}, u32[]{:S(2)}, u32[]{:S(2)}) collective-permute-start(bf16[32,3072]{1,0:T(8,128)(2,1)S(1)} %get-tuple-element.70), channel_id=1, source_target_pairs={{0,12},{4,8},{8,4},{12,0},{16,28},{20,24},{24,20},{28,16},{1,13},{... | collective-permute-start | bytes 589832 | tf_op jit(solution)/shard_map/ppermute | solution.py:606
  102.5 2.2 %place.2.refs_3_ = f32[32,32768]{1,0:T(8,128)} custom-call(s32[4]{0:T(128)S(1)} %pad_add_fusion.place, bf16[32,5120]{1,0:T(8,128)(2,1)S(1)} %collective-permute-done.25.refs_0_, bf16[32,5120]{1,0:T(8,128)(2,1)S(1)} %collective-permute-done.26.refs_1_, bf16[32,5120]{1,0:T(8,128)(2,1)S(1)} %collective-permute-done.27.refs_2_, ...), custom_call_target="tpu_custom_call", output_to_operand_aliasing={{}: (4, {})} | custom-call | bytes 2949120 | tf_op jit(solution)/shard_map/place/pallas_call | solution.py:548
  104.7 0.2 fusion
  104.9 0.6 collective-permute-start.31
  105.5 1.3 %collective-permute-start.32 = (f32[72,160]{1,0:T(8,128)S(1)}, f32[72,160]{1,0:T(8,128)S(1)}, u32[]{:S(2)}, u32[]{:S(2)}) collective-permute-start(f32[72,160]{1,0:T(8,128)S(1)} %get-tuple-element.86), channel_id=1, source_target_pairs={{0,8},{4,12},{8,0},{12,4},{16,24},{20,28},{24,16},{28,20},{1,9},{5... | collective-permute-start | bytes 138248 | tf_op jit(solution)/shard_map/ppermute | solution.py:606
  106.8 1.7 %collective-permute-start.33 = (f32[72,160]{1,0:T(8,128)S(1)}, f32[72,160]{1,0:T(8,128)S(1)}, u32[]{:S(2)}, u32[]{:S(2)}) collective-permute-start(f32[72,160]{1,0:T(8,128)S(1)} %get-tuple-element.83), channel_id=1, source_target_pairs={{0,12},{4,8},{8,4},{12,0},{16,28},{20,24},{24,20},{28,16},{1,13},{... | collective-permute-start | bytes 138248 | tf_op jit(solution)/shard_map/ppermute | solution.py:606
  108.5 0.1 constant_dynamic-slice_fusion.1.denom_ref
  108.6 1.3 %collective-permute-done.28.refs_2_ = bf16[32,3072]{1,0:T(8,128)(2,1)S(1)} collective-permute-done((bf16[32,3072]{1,0:T(8,128)(2,1)S(1)}, bf16[32,3072]{1,0:T(8,128)(2,1)S(1)}, u32[]{:S(2)}, u32[]{:S(2)}) %collective-permute-start.28) | collective-permute-done | bytes 196640 | tf_op jit(solution)/shard_map/ppermute | solution.py:606
  109.9 2.4 %place.3 = f32[32,32768]{1,0:T(8,128)} custom-call(s32[4]{0:T(128)S(1)} %pad_add_fusion.place, bf16[32,3072]{1,0:T(8,128)(2,1)S(1)} %collective-permute-done.23.refs_0_, bf16[32,3072]{1,0:T(8,128)(2,1)S(1)} %collective-permute-done.24.refs_1_, bf16[32,3072]{1,0:T(8,128)(2,1)S(1)} %collective-permute-done.28.refs_2_, ...), custom_call_target="tpu_custom_call", output_to_operand_aliasing={{}: (4, {})} | custom-call | bytes 1769472 | tf_op jit(solution)/shard_map/place/pallas_call | solution.py:548
  112.3 1.4 %finish.1 = (f32[64,160]{1,0:T(8,128)}, f32[1,160]{1,0:T(1,128)}) custom-call(s32[4]{0:T(128)S(1)} %pad_add_fusion.place, f32[1,1536]{1,0:T(1,128)S(1)} %add_add_fusion.both_ref, f32[1,160]{1,0:T(1,128)S(1)} %constant_dynamic-slice_fusion.1.denom_ref, s32[1,160]{1,0:T(1,128)S(1)} %bitcast.18, bf16[160,256]{1,0:T(8,128)(2,1)S(1)} %copy-done.4, ...), custom_call_target="tpu_custom_call" | custom-call | tf_op jit(solution)/shard_map/finish/pallas_call | solution.py:581
  (64 shorter events, 0.4 us)
Async XLA Ops:
  2.3 10.2 %collective-permute-start.2 = (bf16[208,256]{1,0:T(8,128)(2,1)}, bf16[208,256]{1,0:T(8,128)(2,1)S(1)}, u32[]{:S(2)}, u32[]{:S(2)}) collective-permute-start(bf16[208,256]{1,0:T(8,128)(2,1)} %prepare.1), channel_id=1, source_target_pairs={{0,12},{4,8},{8,4},{12,0},{16,28},{20,24},{24,20},{28,16},{1,13},{... | collective-permute-start | bytes 319496 | tf_op jit(solution)/shard_map/ppermute | solution.py:606
  6.2 6.3 %collective-permute-start = (bf16[208,256]{1,0:T(8,128)(2,1)}, bf16[208,256]{1,0:T(8,128)(2,1)S(1)}, u32[]{:S(2)}, u32[]{:S(2)}) collective-permute-start(bf16[208,256]{1,0:T(8,128)(2,1)} %prepare.1), channel_id=1, source_target_pairs={{0,4},{4,0},{8,12},{12,8},{16,20},{20,16},{24,28},{28,24},{1,5},{5... | collective-permute-start | bytes 319496 | tf_op jit(solution)/shard_map/ppermute | solution.py:606
  6.8 5.7 %collective-permute-start.1 = (bf16[208,256]{1,0:T(8,128)(2,1)}, bf16[208,256]{1,0:T(8,128)(2,1)S(1)}, u32[]{:S(2)}, u32[]{:S(2)}) collective-permute-start(bf16[208,256]{1,0:T(8,128)(2,1)} %prepare.1), channel_id=1, source_target_pairs={{0,8},{4,12},{8,0},{12,4},{16,24},{20,28},{24,16},{28,20},{1,9},{5... | collective-permute-start | bytes 319496 | tf_op jit(solution)/shard_map/ppermute | solution.py:606
  6.9 5.6 %copy-start.8 = (bf16[208,256]{1,0:T(8,128)(2,1)S(1)}, bf16[208,256]{1,0:T(8,128)(2,1)}, u32[]{:S(2)}) copy-start(bf16[208,256]{1,0:T(8,128)(2,1)} %prepare.1) | copy-start | bytes 319492
  10.5 2.0 %copy-start.2 = (bf16[4,256,2048]{2,1,0:T(8,128)(2,1)}, bf16[4,256,2048]{2,1,0:T(8,128)(2,1)S(1)}, u32[]{:S(2)}) copy-start(bf16[4,256,2048]{2,1,0:T(8,128)(2,1)S(1)} %get-tuple-element.44.unit_hbm) | copy-start | bytes 12582916
  12.6 5.4 %collective-permute-start.3 = (bf16[4,32,256]{2,1,0:T(8,128)(2,1)S(1)}, bf16[4,32,256]{2,1,0:T(8,128)(2,1)S(1)}, u32[]{:S(2)}, u32[]{:S(2)}) collective-permute-start(bf16[4,32,256]{2,1,0:T(8,128)(2,1)S(1)} %pad_maximum_fusion.3), channel_id=1, source_target_pairs={{0,16},{4,20},{8,24},{12,28},{16,0},{20,4},{24,8},{28,12},{1,17},{... | collective-permute-start | bytes 196616 | tf_op jit(solution)/shard_map/ppermute | solution.py:606
  23.0 5.0 %collective-permute-start.4 = (f32[1,256]{1,0:T(1,128)S(1)}, f32[1,256]{1,0:T(1,128)S(1)}, u32[]{:S(2)}, u32[]{:S(2)}) collective-permute-start(f32[1,256]{1,0:T(1,128)S(1)} %get-tuple-element.45), channel_id=1, source_target_pairs={{0,1},{1,0},{2,3},{3,2},{4,5},{5,4},{6,7},{7,6},{8,9},{9,8},{10,11... | collective-permute-start | bytes 3080 | tf_op jit(solution)/shard_map/ppermute | solution.py:609
  23.1 4.9 %collective-permute-start.5 = (f32[1,256]{1,0:T(1,128)S(1)}, f32[1,256]{1,0:T(1,128)S(1)}, u32[]{:S(2)}, u32[]{:S(2)}) collective-permute-start(f32[1,256]{1,0:T(1,128)S(1)} %get-tuple-element.45), channel_id=1, source_target_pairs={{0,2},{1,3},{2,0},{3,1},{4,6},{5,7},{6,4},{7,5},{8,10},{9,11},{10,... | collective-permute-start | bytes 3080 | tf_op jit(solution)/shard_map/ppermute | solution.py:609
  25.0 3.0 %collective-permute-start.6 = (f32[1,256]{1,0:T(1,128)S(1)}, f32[1,256]{1,0:T(1,128)S(1)}, u32[]{:S(2)}, u32[]{:S(2)}) collective-permute-start(f32[1,256]{1,0:T(1,128)S(1)} %get-tuple-element.45), channel_id=1, source_target_pairs={{0,3},{1,2},{2,1},{3,0},{4,7},{5,6},{6,5},{7,4},{8,11},{9,10},{10,... | collective-permute-start | bytes 3080 | tf_op jit(solution)/shard_map/ppermute | solution.py:609
  25.1 19.6 %collective-permute-start.10 = (bf16[4,176,256]{2,1,0:T(8,128)(2,1)S(1)}, bf16[4,176,256]{2,1,0:T(8,128)(2,1)S(1)}, u32[]{:S(2)}, u32[]{:S(2)}) collective-permute-start(bf16[4,176,256]{2,1,0:T(8,128)(2,1)S(1)} %slice.49.rest_ref), channel_id=1, source_target_pairs={{0,16},{4,20},{8,24},{12,28},{16,0},{20,4},{24,8},{28,12},{1,17},{... | collective-permute-start | bytes 1081352 | tf_op jit(solution)/shard_map/ppermute | solution.py:606
  28.0 12.4 %copy-start = (bf16[4,256,2048]{2,1,0:T(8,128)(2,1)S(1)}, bf16[4,256,2048]{2,1,0:T(8,128)(2,1)}, u32[]{:S(2)}) copy-start(bf16[4,256,2048]{2,1,0:T(8,128)(2,1)} %get-tuple-element.49.energy_hbm) | copy-start | bytes 12582916
  28.0 12.4 %collective-permute-start.7 = (f32[1,256]{1,0:T(1,128)S(1)}, f32[1,256]{1,0:T(1,128)S(1)}, u32[]{:S(2)}, u32[]{:S(2)}) collective-permute-start(f32[1,256]{1,0:T(1,128)S(1)} %add_add_fusion.5), channel_id=1, source_target_pairs={{0,4},{4,0},{8,12},{12,8},{16,20},{20,16},{24,28},{28,24},{1,5},{5... | collective-permute-start | bytes 3080 | tf_op jit(solution)/shard_map/ppermute | solution.py:606
  29.6 10.8 %collective-permute-start.8 = (f32[1,256]{1,0:T(1,128)S(1)}, f32[1,256]{1,0:T(1,128)S(1)}, u32[]{:S(2)}, u32[]{:S(2)}) collective-permute-start(f32[1,256]{1,0:T(1,128)S(1)} %add_add_fusion.5), channel_id=1, source_target_pairs={{0,8},{4,12},{8,0},{12,4},{16,24},{20,28},{24,16},{28,20},{1,9},{5... | collective-permute-start | bytes 3080 | tf_op jit(solution)/shard_map/ppermute | solution.py:606
  31.7 8.8 %collective-permute-start.9 = (f32[1,256]{1,0:T(1,128)S(1)}, f32[1,256]{1,0:T(1,128)S(1)}, u32[]{:S(2)}, u32[]{:S(2)}) collective-permute-start(f32[1,256]{1,0:T(1,128)S(1)} %add_add_fusion.5), channel_id=1, source_target_pairs={{0,12},{4,8},{8,4},{12,0},{16,28},{20,24},{24,20},{28,16},{1,13},{... | collective-permute-start | bytes 3080 | tf_op jit(solution)/shard_map/ppermute | solution.py:606
  44.6 2.0 %collective-permute-start.11 = (f32[1,256]{1,0:T(1,128)S(1)}, f32[1,256]{1,0:T(1,128)S(1)}, u32[]{:S(2)}, u32[]{:S(2)}) collective-permute-start(f32[1,256]{1,0:T(1,128)S(1)} %iterate.1), channel_id=1, source_target_pairs={{0,1},{1,0},{2,3},{3,2},{4,5},{5,4},{6,7},{7,6},{8,9},{9,8},{10,11... | collective-permute-start | bytes 3080 | tf_op jit(solution)/shard_map/ppermute | solution.py:609
  44.6 3.6 %collective-permute-start.12 = (f32[1,256]{1,0:T(1,128)S(1)}, f32[1,256]{1,0:T(1,128)S(1)}, u32[]{:S(2)}, u32[]{:S(2)}) collective-permute-start(f32[1,256]{1,0:T(1,128)S(1)} %iterate.1), channel_id=1, source_target_pairs={{0,2},{1,3},{2,0},{3,1},{4,6},{5,7},{6,4},{7,5},{8,10},{9,11},{10,... | collective-permute-start | bytes 3080 | tf_op jit(solution)/shard_map/ppermute | solution.py:609
  46.2 3.0 %collective-permute-start.13 = (f32[1,256]{1,0:T(1,128)S(1)}, f32[1,256]{1,0:T(1,128)S(1)}, u32[]{:S(2)}, u32[]{:S(2)}) collective-permute-start(f32[1,256]{1,0:T(1,128)S(1)} %iterate.1), channel_id=1, source_target_pairs={{0,3},{1,2},{2,1},{3,0},{4,7},{5,6},{6,5},{7,4},{8,11},{9,10},{10,... | collective-permute-start | bytes 3080 | tf_op jit(solution)/shard_map/ppermute | solution.py:609
  49.2 10.1 %copy-start.1 = (bf16[4,256,2048]{2,1,0:T(8,128)(2,1)S(1)}, bf16[4,256,2048]{2,1,0:T(8,128)(2,1)}, u32[]{:S(2)}) copy-start(bf16[4,256,2048]{2,1,0:T(8,128)(2,1)} %get-tuple-element.49.energy_hbm) | copy-start | bytes 12582916
  49.2 10.0 %collective-permute-start.14 = (f32[1,256]{1,0:T(1,128)S(1)}, f32[1,256]{1,0:T(1,128)S(1)}, u32[]{:S(2)}, u32[]{:S(2)}) collective-permute-start(f32[1,256]{1,0:T(1,128)S(1)} %add_add_fusion.3), channel_id=1, source_target_pairs={{0,4},{4,0},{8,12},{12,8},{16,20},{20,16},{24,28},{28,24},{1,5},{5... | collective-permute-start | bytes 3080 | tf_op jit(solution)/shard_map/ppermute | solution.py:606
  50.7 8.5 %collective-permute-start.15 = (f32[1,256]{1,0:T(1,128)S(1)}, f32[1,256]{1,0:T(1,128)S(1)}, u32[]{:S(2)}, u32[]{:S(2)}) collective-permute-start(f32[1,256]{1,0:T(1,128)S(1)} %add_add_fusion.3), channel_id=1, source_target_pairs={{0,8},{4,12},{8,0},{12,4},{16,24},{20,28},{24,16},{28,20},{1,9},{5... | collective-permute-start | bytes 3080 | tf_op jit(solution)/shard_map/ppermute | solution.py:606
  51.4 7.8 %collective-permute-start.16 = (f32[1,256]{1,0:T(1,128)S(1)}, f32[1,256]{1,0:T(1,128)S(1)}, u32[]{:S(2)}, u32[]{:S(2)}) collective-permute-start(f32[1,256]{1,0:T(1,128)S(1)} %add_add_fusion.3), channel_id=1, source_target_pairs={{0,12},{4,8},{8,4},{12,0},{16,28},{20,24},{24,20},{28,16},{1,13},{... | collective-permute-start | bytes 3080 | tf_op jit(solution)/shard_map/ppermute | solution.py:606
  59.2 11.5 %copy-start.3 = (bf16[4,256,2048]{2,1,0:T(8,128)(2,1)S(1)}, bf16[4,256,2048]{2,1,0:T(8,128)(2,1)}, u32[]{:S(2)}) copy-start(bf16[4,256,2048]{2,1,0:T(8,128)(2,1)} %copy-done.2) | copy-start | bytes 12582916
  63.2 2.0 %collective-permute-start.17 = (f32[1,1536]{1,0:T(1,128)S(1)}, f32[1,1536]{1,0:T(1,128)S(1)}, u32[]{:S(2)}, u32[]{:S(2)}) collective-permute-start(f32[1,1536]{1,0:T(1,128)S(1)} %get-tuple-element.53), channel_id=1, source_target_pairs={{0,1},{1,0},{2,3},{3,2},{4,5},{5,4},{6,7},{7,6},{8,9},{9,8},{10,11... | collective-permute-start | bytes 18440 | tf_op jit(solution)/shard_map/ppermute | solution.py:609
  63.3 3.7 %collective-permute-start.18 = (f32[1,1536]{1,0:T(1,128)S(1)}, f32[1,1536]{1,0:T(1,128)S(1)}, u32[]{:S(2)}, u32[]{:S(2)}) collective-permute-start(f32[1,1536]{1,0:T(1,128)S(1)} %get-tuple-element.53), channel_id=1, source_target_pairs={{0,2},{1,3},{2,0},{3,1},{4,6},{5,7},{6,4},{7,5},{8,10},{9,11},{10,... | collective-permute-start | bytes 18440 | tf_op jit(solution)/shard_map/ppermute | solution.py:609
  64.0 3.1 %collective-permute-start.19 = (f32[1,1536]{1,0:T(1,128)S(1)}, f32[1,1536]{1,0:T(1,128)S(1)}, u32[]{:S(2)}, u32[]{:S(2)}) collective-permute-start(f32[1,1536]{1,0:T(1,128)S(1)} %get-tuple-element.53), channel_id=1, source_target_pairs={{0,3},{1,2},{2,1},{3,0},{4,7},{5,6},{6,5},{7,4},{8,11},{9,10},{10,... | collective-permute-start | bytes 18440 | tf_op jit(solution)/shard_map/ppermute | solution.py:609
  67.1 6.9 %collective-permute-start.20 = (f32[1,1536]{1,0:T(1,128)S(1)}, f32[1,1536]{1,0:T(1,128)S(1)}, u32[]{:S(2)}, u32[]{:S(2)}) collective-permute-start(f32[1,1536]{1,0:T(1,128)S(1)} %add_add_fusion.1), channel_id=1, source_target_pairs={{0,4},{4,0},{8,12},{12,8},{16,20},{20,16},{24,28},{28,24},{1,5},{5... | collective-permute-start | bytes 18440 | tf_op jit(solution)/shard_map/ppermute | solution.py:606
  68.6 5.4 %collective-permute-start.21 = (f32[1,1536]{1,0:T(1,128)S(1)}, f32[1,1536]{1,0:T(1,128)S(1)}, u32[]{:S(2)}, u32[]{:S(2)}) collective-permute-start(f32[1,1536]{1,0:T(1,128)S(1)} %add_add_fusion.1), channel_id=1, source_target_pairs={{0,8},{4,12},{8,0},{12,4},{16,24},{20,28},{24,16},{28,20},{1,9},{5... | collective-permute-start | bytes 18440 | tf_op jit(solution)/shard_map/ppermute | solution.py:606
  69.4 4.6 %collective-permute-start.22 = (f32[1,1536]{1,0:T(1,128)S(1)}, f32[1,1536]{1,0:T(1,128)S(1)}, u32[]{:S(2)}, u32[]{:S(2)}) collective-permute-start(f32[1,1536]{1,0:T(1,128)S(1)} %add_add_fusion.1), channel_id=1, source_target_pairs={{0,12},{4,8},{8,4},{12,0},{16,28},{20,24},{24,20},{28,16},{1,13},{... | collective-permute-start | bytes 18440 | tf_op jit(solution)/shard_map/ppermute | solution.py:606
  83.4 14.2 %collective-permute-start.25 = (bf16[32,5120]{1,0:T(8,128)(2,1)S(1)}, bf16[32,5120]{1,0:T(8,128)(2,1)S(1)}, u32[]{:S(2)}, u32[]{:S(2)}) collective-permute-start(bf16[32,5120]{1,0:T(8,128)(2,1)S(1)} %get-tuple-element.67), channel_id=1, source_target_pairs={{0,4},{4,0},{8,12},{12,8},{16,20},{20,16},{24,28},{28,24},{1,5},{5... | collective-permute-start | bytes 983048 | tf_op jit(solution)/shard_map/ppermute | solution.py:606
  85.0 13.5 %collective-permute-start.26 = (bf16[32,5120]{1,0:T(8,128)(2,1)S(1)}, bf16[32,5120]{1,0:T(8,128)(2,1)S(1)}, u32[]{:S(2)}, u32[]{:S(2)}) collective-permute-start(bf16[32,5120]{1,0:T(8,128)(2,1)S(1)} %get-tuple-element.68), channel_id=1, source_target_pairs={{0,8},{4,12},{8,0},{12,4},{16,24},{20,28},{24,16},{28,20},{1,9},{5... | collective-permute-start | bytes 983048 | tf_op jit(solution)/shard_map/ppermute | solution.py:606
  85.8 15.0 %collective-permute-start.27 = (bf16[32,5120]{1,0:T(8,128)(2,1)S(1)}, bf16[32,5120]{1,0:T(8,128)(2,1)S(1)}, u32[]{:S(2)}, u32[]{:S(2)}) collective-permute-start(bf16[32,5120]{1,0:T(8,128)(2,1)S(1)} %get-tuple-element.69), channel_id=1, source_target_pairs={{0,12},{4,8},{8,4},{12,0},{16,28},{20,24},{24,20},{28,16},{1,13},{... | collective-permute-start | bytes 983048 | tf_op jit(solution)/shard_map/ppermute | solution.py:606
  87.0 8.5 %collective-permute-start.29 = (f32[136,640]{1,0:T(8,128)S(1)}, f32[136,640]{1,0:T(8,128)S(1)}, u32[]{:S(2)}, u32[]{:S(2)}) collective-permute-start(f32[136,640]{1,0:T(8,128)S(1)} %get-tuple-element.73), channel_id=1, source_target_pairs={{0,2},{1,3},{2,0},{3,1},{4,6},{5,7},{6,4},{7,5},{8,10},{9,11},{10,... | collective-permute-start | bytes 1044488 | tf_op jit(solution)/shard_map/ppermute | solution.py:609
  95.2 0.7 copy-start.6
  95.2 0.7 copy-start.7
  96.0 8.7 %collective-permute-start.30 = (f32[72,640]{1,0:T(8,128)S(1)}, f32[72,640]{1,0:T(8,128)S(1)}, u32[]{:S(2)}, u32[]{:S(2)}) collective-permute-start(f32[72,640]{1,0:T(8,128)S(1)} %pad_maximum_fusion.1), channel_id=1, source_target_pairs={{0,1},{1,0},{2,3},{3,2},{4,5},{5,4},{6,7},{7,6},{8,9},{9,8},{10,11... | collective-permute-start | bytes 552968 | tf_op jit(solution)/shard_map/ppermute | solution.py:609
  96.1 10.7 %collective-permute-start.23 = (bf16[32,3072]{1,0:T(8,128)(2,1)}, bf16[32,3072]{1,0:T(8,128)(2,1)S(1)}, u32[]{:S(2)}, u32[]{:S(2)}) collective-permute-start(bf16[32,3072]{1,0:T(8,128)(2,1)} %copy-done.7), channel_id=1, source_target_pairs={{0,4},{4,0},{8,12},{12,8},{16,20},{20,16},{24,28},{28,24},{1,5},{5... | collective-permute-start | bytes 589832 | tf_op jit(solution)/shard_map/ppermute | solution.py:606
  97.7 10.9 %collective-permute-start.24 = (bf16[32,3072]{1,0:T(8,128)(2,1)}, bf16[32,3072]{1,0:T(8,128)(2,1)S(1)}, u32[]{:S(2)}, u32[]{:S(2)}) collective-permute-start(bf16[32,3072]{1,0:T(8,128)(2,1)} %copy-done.6), channel_id=1, source_target_pairs={{0,8},{4,12},{8,0},{12,4},{16,24},{20,28},{24,16},{28,20},{1,9},{5... | collective-permute-start | bytes 589832 | tf_op jit(solution)/shard_map/ppermute | solution.py:606
  100.8 9.1 %collective-permute-start.28 = (bf16[32,3072]{1,0:T(8,128)(2,1)S(1)}, bf16[32,3072]{1,0:T(8,128)(2,1)S(1)}, u32[]{:S(2)}, u32[]{:S(2)}) collective-permute-start(bf16[32,3072]{1,0:T(8,128)(2,1)S(1)} %get-tuple-element.70), channel_id=1, source_target_pairs={{0,12},{4,8},{8,4},{12,0},{16,28},{20,24},{24,20},{28,16},{1,13},{... | collective-permute-start | bytes 589832 | tf_op jit(solution)/shard_map/ppermute | solution.py:606
  104.9 7.3 %collective-permute-start.31 = (f32[72,160]{1,0:T(8,128)S(1)}, f32[72,160]{1,0:T(8,128)S(1)}, u32[]{:S(2)}, u32[]{:S(2)}) collective-permute-start(f32[72,160]{1,0:T(8,128)S(1)} %get-tuple-element.85), channel_id=1, source_target_pairs={{0,4},{4,0},{8,12},{12,8},{16,20},{20,16},{24,28},{28,24},{1,5},{5... | collective-permute-start | bytes 138248 | tf_op jit(solution)/shard_map/ppermute | solution.py:606
  105.5 6.8 %collective-permute-start.32 = (f32[72,160]{1,0:T(8,128)S(1)}, f32[72,160]{1,0:T(8,128)S(1)}, u32[]{:S(2)}, u32[]{:S(2)}) collective-permute-start(f32[72,160]{1,0:T(8,128)S(1)} %get-tuple-element.86), channel_id=1, source_target_pairs={{0,8},{4,12},{8,0},{12,4},{16,24},{20,28},{24,16},{28,20},{1,9},{5... | collective-permute-start | bytes 138248 | tf_op jit(solution)/shard_map/ppermute | solution.py:606
  106.8 5.5 %collective-permute-start.33 = (f32[72,160]{1,0:T(8,128)S(1)}, f32[72,160]{1,0:T(8,128)S(1)}, u32[]{:S(2)}, u32[]{:S(2)}) collective-permute-start(f32[72,160]{1,0:T(8,128)S(1)} %get-tuple-element.83), channel_id=1, source_target_pairs={{0,12},{4,8},{8,4},{12,0},{16,28},{20,24},{24,20},{28,16},{1,13},{... | collective-permute-start | bytes 138248 | tf_op jit(solution)/shard_map/ppermute | solution.py:606
  108.6 3.7 %copy-start.4 = (bf16[160,256]{1,0:T(8,128)(2,1)S(1)}, bf16[160,256]{1,0:T(8,128)(2,1)}, u32[]{:S(2)}) copy-start(bf16[160,256]{1,0:T(8,128)(2,1)} %stud_ref.3) | copy-start | bytes 245764
  108.6 3.7 %copy-start.5 = (s32[160]{0:T(256)S(1)}, s32[160]{0:T(256)}, u32[]{:S(2)}) copy-start(s32[160]{0:T(256)} %param.7) | copy-start | bytes 1924
